TPU v7x, 256 devices: a whole 4x4x8 slice. The times are simulated.
256 devices in a mesh: space: 32 (over x, y, core), level: 8 (over z).
Axes of the slice: x: 4, y: 4, z: 8, core: 2. Of those that a mesh axis runs over, the one named last changes fastest.
Arguments:
- fields: bfloat16 [8, 16384, 768], P('level', 'space'), may hold values from -16 to 16
- norm_vert: float32 [768], replicated, may hold values from 0.1 to 1.9
- query_vert: bfloat16 [768, 768], replicated, may hold values from -0.21875 to 0.21875
- keys_vert: bfloat16 [768, 768], replicated, may hold values from -0.21875 to 0.21875
- values_vert: bfloat16 [768, 768], replicated, may hold values from -0.21875 to 0.21875
- out_vert: bfloat16 [768, 768], replicated, may hold values from -0.21875 to 0.21875
- level_bias: float32 [12, 8, 8], replicated, may hold values from -3 to 250
- norm_patch: float32 [768], replicated, may hold values from 0.1 to 1.9
- query_patch: bfloat16 [768, 768], replicated, may hold values from -0.21875 to 0.21875
- keys_patch: bfloat16 [768, 768], replicated, may hold values from -0.21875 to 0.21875
- values_patch: bfloat16 [768, 768], replicated, may hold values from -0.21875 to 0.21875
- out_patch: bfloat16 [768, 768], replicated, may hold values from -0.21875 to 0.21875
- patch_bias: float32 [12, 2], replicated, may hold values from -3 to 250
- neighbours: int32 [64, 4], P('space'), may hold values from -1 to 63, as said below
- counts: int32 [64], P('space'), may hold values from 2 to 4, as said below
- cotangent: bfloat16 [8, 16384, 768], P('level', 'space'), may hold values from -0.015625 to 0.015625
Outputs:
- out_fields: bfloat16 [8, 16384, 768], P('level', 'space')
- grad_wo: float32 [768, 768], P('space')
Inputs may be any that keep to these rules, and one draw needn't show every extreme that they name: `neighbours`: row p lists distinct patches, at most one from each device of space, held on devices at cycle distance 1 to 2 from the device of patch p (device s of space holds patches s * 2 to (s + 1) * 2 - 1); entries from counts[p] on are -1. `counts`: some patch has 4 neighbours in every draw.
All inputs are finite; a program needn't handle non-finite values.
Results may differ from a plain program's by a relative error of at most 0.025.
Values may be sent and summed in bfloat16 or wider, within the bound.
No kernel may reach another device: no remote copies, remote signals or barrier semaphores. Data moves between devices by JAX's collectives and lax.ppermute only.
A program may use at most 128 MiB of HBM per device.

v0:
```python
import jax
import jax.numpy as jnp
from jax import lax
from jax.sharding import PartitionSpec as P

H = 12
HD = 64
PATCH = 256
REACH = 2


epsilon = 1e-06


def passed_along(value, axis, steps):
    count = lax.axis_size(axis)
    pairs = [(source, (source + steps) % count) for source in range(count)]
    return lax.ppermute(value, axis, pairs)


def in_blocks(value, dim, count):
    shape = value.shape
    pieces = value.reshape(*shape[:dim], count, shape[dim] // count, *shape[dim + 1 :])
    return jnp.moveaxis(pieces, dim, 0)


def summed_on_arrival(value, axis, dim):
    pieces = in_blocks(value, dim, lax.axis_size(axis))
    arrived = lax.all_to_all(pieces, axis, split_axis=0, concat_axis=0, tiled=True)
    return arrived.astype(jnp.float32).sum(axis=0)


def sent_to_all(value, axis):
    count = lax.axis_size(axis)
    return lax.all_to_all(
        jnp.broadcast_to(value[None], (count, *value.shape)), axis, 0, 0, tiled=True
    )


def taken_together(value, axis):
    everything = sent_to_all(value, axis)
    return jnp.sum(everything.astype(jnp.float32), axis=0)


def normalize(values, scaling):
    widened = values.astype(jnp.float32)
    mean_square = jnp.mean(widened * widened, axis=-1, keepdims=True)
    return (widened * lax.rsqrt(mean_square + epsilon) * scaling).astype(jnp.bfloat16)


def project(inputs, weight):
    return jnp.dot(inputs, weight, preferred_element_type=jnp.float32).astype(jnp.bfloat16)


def vertical_heads(queries, keys_in, values_in, bias_table):
    level_count, columns, features = queries.shape
    query_heads = queries.reshape(level_count, columns, H, HD)
    key_heads = keys_in.reshape(keys_in.shape[0], columns, H, HD)
    value_heads = values_in.reshape(values_in.shape[0], columns, H, HD)
    scores = (
        jnp.einsum("ichd,jchd->hijc", query_heads, key_heads, preferred_element_type=jnp.float32)
        * HD ** (-0.5)
        + bias_table[:, :, :, None]
    )
    weights = jax.nn.softmax(scores, axis=2).astype(jnp.bfloat16)
    mixture = jnp.einsum(
        "hijc,jchd->ichd", weights, value_heads, preferred_element_type=jnp.float32
    )
    return mixture.astype(jnp.bfloat16).reshape(level_count, columns, features)


def patch_heads(queries, own_keys, nearby, live_count, bias_table):
    features = queries.shape[-1]
    patch_len = own_keys.shape[0]
    keys_all = jnp.concatenate((own_keys[None], nearby), axis=0).reshape(-1, 2 * features)
    query_heads = queries.reshape(-1, H, HD)
    key_heads = keys_all[:, :features].reshape(-1, H, HD)
    value_heads = keys_all[:, features:].reshape(-1, H, HD)
    scores = jnp.einsum(
        "qhd,khd->hqk", query_heads, key_heads, preferred_element_type=jnp.float32
    ) * HD ** (-0.5)
    block_bias = jnp.concatenate(
        (bias_table[:, :1], jnp.broadcast_to(bias_table[:, 1:], (H, nearby.shape[0]))), axis=1
    )
    scores = scores + jnp.repeat(block_bias, patch_len, axis=1)[:, None, :]
    opened = jnp.repeat(jnp.arange(nearby.shape[0] + 1, dtype=jnp.int32) <= live_count, patch_len)
    scores = jnp.where(opened[None, None, :], scores, -jnp.inf)
    weights = jax.nn.softmax(scores, axis=-1).astype(jnp.bfloat16)
    mixture = jnp.einsum("hqk,khd->qhd", weights, value_heads, preferred_element_type=jnp.float32)
    return mixture.astype(jnp.bfloat16).reshape(-1, features)


def body(
    fields,
    norm_vert,
    query_vert,
    keys_vert,
    values_vert,
    out_vert,
    level_bias,
    norm_patch,
    query_patch,
    keys_patch,
    values_patch,
    out_patch,
    patch_bias,
    neighbours,
    counts,
    cotangent,
):
    level_count, columns, features = fields.shape
    groups = lax.axis_size("level")
    normed = normalize(fields, norm_vert)
    vertical_in = jnp.concatenate((query_vert, keys_vert, values_vert), axis=1)
    split_in = normed.reshape(level_count, groups, columns // groups, features)
    merged = project(
        lax.all_to_all(split_in, "level", split_axis=1, concat_axis=0, tiled=True), vertical_in
    )[:, 0]
    result = vertical_heads(
        merged[..., :features],
        merged[..., features : 2 * features],
        merged[..., 2 * features :],
        level_bias,
    )
    mixture = result[:, None]
    attn_vert = lax.all_to_all(mixture, "level", split_axis=0, concat_axis=1, tiled=True).reshape(
        level_count, columns, features
    )
    hidden = (
        fields.astype(jnp.float32)
        + jnp.dot(attn_vert, out_vert, preferred_element_type=jnp.float32)
    ).astype(jnp.bfloat16)
    pair_in = jnp.concatenate((keys_patch, values_patch), axis=1)
    normed_patch = normalize(hidden, norm_patch)
    queries_patch = project(normed_patch, query_patch)
    key_values = project(normed_patch, pair_in)
    offsets = [stride for stride in range(1, REACH + 1)] + [
        -stride for stride in range(1, REACH + 1)
    ]
    arrived = [passed_along(normed_patch, "space", offset) for offset in offsets]
    distant = project(jnp.stack(arrived), pair_in)
    per_device = columns // PATCH
    distant = distant.reshape(2 * REACH, level_count, per_device, PATCH, 2 * features)
    position = lax.axis_index("space")
    cycle_size = lax.axis_size("space")
    clipped = jnp.maximum(neighbours, 0)
    owner = clipped // per_device
    distance = (position - owner) % cycle_size
    source = jnp.where(distance <= REACH, distance - 1, REACH + cycle_size - distance - 1)
    source = jnp.clip(source, 0, 2 * REACH - 1)
    within = clipped % per_device

    def level_mix(query_level, own_level, distant_level):
        nearby = distant_level[source, within]
        return jax.vmap(patch_heads, in_axes=(0, 0, 0, 0, None))(
            query_level, own_level, nearby, counts, patch_bias
        )

    mixture_patch = jax.vmap(level_mix, in_axes=(0, 0, 1))(
        queries_patch.reshape(level_count, per_device, PATCH, features),
        key_values.reshape(level_count, per_device, PATCH, 2 * features),
        distant,
    )
    attn_patch = mixture_patch.reshape(level_count, columns, features)
    out_fields = (
        hidden.astype(jnp.float32)
        + jnp.dot(attn_patch, out_patch, preferred_element_type=jnp.float32)
    ).astype(jnp.bfloat16)
    flat_attn = attn_patch.reshape(-1, features)
    flat_cotangent = cotangent.reshape(-1, features)
    shares = summed_on_arrival(
        lax.dot_general(
            flat_attn, flat_cotangent, (((0,), (0,)), ((), ())), preferred_element_type=jnp.float32
        ).astype(jnp.bfloat16),
        "space",
        0,
    )
    grad_wo = taken_together(shares.astype(jnp.bfloat16), "level").astype(jnp.float32)
    return (out_fields, grad_wo)


def solution(mesh):
    return jax.shard_map(
        body,
        mesh=mesh,
        in_specs=(
            P("level", "space", None),
            P(),
            P(),
            P(),
            P(),
            P(),
            P(),
            P(),
            P(),
            P(),
            P(),
            P(),
            P(),
            P("space", None),
            P("space"),
            P("level", "space", None),
        ),
        out_specs=(P("level", "space", None), P("space", None)),
        check_vma=False,
    )
```

profile of v0, /device:TPU:1, one launch (start us, length us, event | category | flops | bytes accessed | tf_op | source)
XLA Modules:
  0.0 251.2 jit_solution(17723126919041951585)
XLA Ops:
  4.5 9.0 %all-to-all-start = ((bf16[1,8,64,768]{3,2,0,1:T(8,128)(2,1)}), bf16[1,8,64,768]{3,2,0,1:T(8,128)(2,1)S(1)}, u32[]{:S(2)}, u32[]{:S(2)}) async-start(bf16[1,8,64,768]{3,2,0,1:T(8,128)(2,1)} %bitcast.1), calls=%async_computation | async-start | bytes 1572864 | tf_op jit(solution)/shard_map/all_to_all | solution.py:117
  13.6 23.4 %all-to-all-done = bf16[1,8,64,768]{3,2,0,1:T(8,128)(2,1)S(1)} async-done(((bf16[1,8,64,768]{3,2,0,1:T(8,128)(2,1)}), bf16[1,8,64,768]{3,2,0,1:T(8,128)(2,1)S(1)}, u32[]{:S(2)}, u32[]{:S(2)}) %all-to-all-start) | async-done | bytes 786464 | tf_op jit(solution)/shard_map/all_to_all | solution.py:117
  37.0 3.6 %convolution_convert_fusion.1 = bf16[8,64,2304]{2,1,0:T(8,128)(2,1)S(1)} fusion(bf16[768,768]{1,0:T(8,128)(2,1)S(1)} %copy-done.15, bf16[768,768]{1,0:T(8,128)(2,1)} %param.19, bf16[768,768]{1,0:T(8,128)(2,1)} %param.18, bf16[1,8,64,768]{3,2,0,1:T(8,128)(2,1)S(1)} %all-to-all-done), kind=kOutput, calls=%fused_computation.15 | convolution fusion | flops 1823735808 | bytes 6684672 | tf_op jit(solution)/shard_map/dot_general | solution.py:52
  47.1 3.8 %reshape.154 = bf16[8,64,12,64]{3,2,1,0:T(8,128)(2,1)} reshape(bf16[8,64,768]{2,1,0:T(8,128)(2,1)} %get-tuple-element.6) | data formatting | bytes 1572864 | tf_op jit(solution)/shard_map/reshape | solution.py:58
  50.8 5.1 %fusion.32 = f32[12,64,8,8]{3,2,1,0:T(8,128)S(1)} fusion(bf16[8,64,12,64]{3,2,1,0:T(8,128)(2,1)S(1)} %reshape.155, bf16[8,64,12,64]{3,2,1,0:T(8,128)(2,1)} %reshape.154), kind=kOutput, calls=%fused_computation.51 | convolution fusion | flops 6291456 | bytes 1769472 | tf_op jit(solution)/shard_map/ichd,jchd->hijc/dot_general | solution.py:61
  56.0 11.7 %fusion.65 = (f32[12,8,64]{1,2,0:T(8,128)S(1)}, f32[12,8,8,64]{1,2,3,0:T(8,128)S(1)}) fusion(f32[12,64,8,8]{3,2,1,0:T(8,128)S(1)} %fusion.32, f32[12,8,8]{1,2,0:T(8,128)S(1)} %copy.58), kind=kOutput, calls=%fused_computation.97 | output fusion | flops 294919 | bytes 420864 | tf_op jit(solution)/shard_map/sub | solution.py:65
  71.5 4.5 %all-to-all-start.1 = ((bf16[8,1,64,768]{3,2,1,0:T(8,128)(2,1)}), bf16[8,1,64,768]{3,2,1,0:T(8,128)(2,1)}, u32[]{:S(2)}, u32[]{:S(2)}) async-start(bf16[8,1,64,768]{3,2,1,0:T(8,128)(2,1)} %bitcast.89), calls=%async_computation.1 | async-start | bytes 1572864 | tf_op jit(solution)/shard_map/all_to_all | solution.py:126
  78.5 19.1 %all-to-all-done.1 = bf16[8,1,64,768]{3,2,1,0:T(8,128)(2,1)} async-done(((bf16[8,1,64,768]{3,2,1,0:T(8,128)(2,1)}), bf16[8,1,64,768]{3,2,1,0:T(8,128)(2,1)}, u32[]{:S(2)}, u32[]{:S(2)}) %all-to-all-start.1) | async-done | bytes 786464 | tf_op jit(solution)/shard_map/all_to_all | solution.py:126
  100.9 4.9 %collective-permute-start.3 = (bf16[1,512,768]{2,1,0:T(8,128)(2,1)}, bf16[1,512,768]{2,1,0:T(8,128)(2,1)}, u32[]{:S(2)}, u32[]{:S(2)}) collective-permute-start(bf16[1,512,768]{2,1,0:T(8,128)(2,1)} %fusion.28), channel_id=1, source_target_pairs={{0,240},{8,248},{16,0},{24,8},{32,16},{40,24},{48,32},{56,40},{64,... | collective-permute-start | bytes 2359304 | tf_op jit(solution)/shard_map/ppermute | solution.py:18
  112.5 3.4 %convolution_convert_fusion.2 = bf16[512,1536]{1,0:T(8,128)(2,1)S(1)} fusion(bf16[768,1536]{1,0:T(8,128)(2,1)} %copy-done.8, bf16[1,512,768]{2,1,0:T(8,128)(2,1)} %fusion.28), kind=kOutput, calls=%fused_computation.31 | convolution fusion | flops 1208745984 | bytes 4718592 | tf_op jit(solution)/shard_map/dot_general | solution.py:52
  115.9 6.7 %collective-permute-done.3 = bf16[1,512,768]{2,1,0:T(8,128)(2,1)} collective-permute-done((bf16[1,512,768]{2,1,0:T(8,128)(2,1)}, bf16[1,512,768]{2,1,0:T(8,128)(2,1)}, u32[]{:S(2)}, u32[]{:S(2)}) %collective-permute-start.3) | collective-permute-done | bytes 786464 | tf_op jit(solution)/shard_map/ppermute | solution.py:18
  122.6 6.7 %collective-permute-done.2 = bf16[1,512,768]{2,1,0:T(8,128)(2,1)} collective-permute-done((bf16[1,512,768]{2,1,0:T(8,128)(2,1)}, bf16[1,512,768]{2,1,0:T(8,128)(2,1)}, u32[]{:S(2)}, u32[]{:S(2)}) %collective-permute-start.2) | collective-permute-done | bytes 786464 | tf_op jit(solution)/shard_map/ppermute | solution.py:18
  129.4 3.4 %collective-permute-done = bf16[1,512,768]{2,1,0:T(8,128)(2,1)} collective-permute-done((bf16[1,512,768]{2,1,0:T(8,128)(2,1)}, bf16[1,512,768]{2,1,0:T(8,128)(2,1)}, u32[]{:S(2)}, u32[]{:S(2)}) %collective-permute-start) | collective-permute-done | bytes 786464 | tf_op jit(solution)/shard_map/ppermute | solution.py:18
  132.8 8.8 %convolution_convert_fusion = bf16[4,512,1536]{2,1,0:T(8,128)(2,1)} fusion(bf16[1,1,512,768]{3,2,1,0:T(8,128)(2,1)} %bitcast.15, bf16[1,1,512,768]{3,2,1,0:T(8,128)(2,1)} %bitcast.14, bf16[1,1,512,768]{3,2,1,0:T(8,128)(2,1)} %bitcast.13, bf16[1,1,512,768]{3,2,1,0:T(8,128)(2,1)} %bitcast.12, bf16[768,1536]{1,0:T(8,128)(2,1)S(1)} %copy-done.9), kind=kOutput, calls=%fused_computation.13 | convolution fusion | flops 4839702528 | bytes 11796480 | tf_op jit(solution)/shard_map/dot_general | solution.py:52
  141.6 6.4 %gather_fusion = bf16[8,256,1536]{2,1,0:T(8,128)(2,1)} fusion(bf16[4,2,256,1536]{3,2,1,0:T(8,128)(2,1)} %bitcast.85, s32[8]{0:T(128)S(1)} %reshape.168), kind=kCustom, calls=%fused_computation | custom fusion | bytes 12582976 | tf_op jit(solution)/shard_map/vmap()/gather | solution.py:154
  148.0 6.5 %pad_maximum_fusion = bf16[1,2,5,256,1536]{4,3,2,1,0:T(8,128)(2,1)} fusion(bf16[1,2,4,256,1536]{4,3,2,1,0:T(8,128)(2,1)} %bitcast.84, bf16[1,2,1,256,1536]{4,3,2,1,0:T(8,128)(2,1)S(1)} %bitcast.90), kind=kLoop, calls=%fused_computation.12 | loop fusion | flops 3932160 | bytes 15728640 | tf_op jit(solution)/shard_map/vmap(vmap())/concatenate | solution.py:75
  154.6 5.5 %fusion.62 = (bf16[1,2,1280,768]{3,2,1,0:T(8,128)(2,1)}, bf16[1,2,1280,768]{3,2,1,0:T(8,128)(2,1)}) fusion(bf16[1,2,1280,1536]{3,2,1,0:T(8,128)(2,1)} %bitcast.83), kind=kLoop, calls=%fused_computation.94 | loop fusion | bytes 15728640 | tf_op jit(solution)/shard_map/vmap(vmap())/slice | solution.py:77
  160.0 6.2 %copy.66 = bf16[1,2,1280,768]{2,3,1,0:T(8,128)(2,1)} copy(bf16[1,2,1280,768]{3,2,1,0:T(8,128)(2,1)} %get-tuple-element.2) | data formatting | bytes 7864320 | tf_op jit(solution)/shard_map/vmap(vmap())/slice | solution.py:77
  166.2 6.3 %copy.64 = bf16[1,2,1280,768]{2,3,1,0:T(8,128)(2,1)} copy(bf16[1,2,1280,768]{3,2,1,0:T(8,128)(2,1)} %get-tuple-element.3) | data formatting | bytes 7864320 | tf_op jit(solution)/shard_map/vmap(vmap())/slice | solution.py:78
  172.6 17.4 %fusion.66 = (f32[2,12,256]{2,1,0:T(8,128)S(1)}, f32[2,12,256,1280]{3,2,1,0:T(8,128)}) fusion(f32[12,1280]{1,0:T(8,128)S(1)} %bitcast.95, pred[2,1280]{1,0:T(4,128)(4,1)S(1)} %bitcast.96, bf16[2,1280,12,64]{1,3,2,0:T(8,128)(2,1)} %bitcast.86, bf16[2,256,12,64]{1,0,3,2:T(2,128)(2,1)S(1)} %copy-done.6), kind=kOutput, calls=%fused_computation.98 | convolution fusion | flops 1045955840 | bytes 36264448 | tf_op jit(solution)/shard_map/vmap(vmap())/sub | solution.py:88
  189.9 14.3 %fusion.43 = bf16[1,2,256,12,64]{2,4,3,1,0:T(8,128)(2,1)S(1)} fusion(bf16[2,1280,12,64]{1,3,2,0:T(8,128)(2,1)} %bitcast.87, f32[2,12,256,1280]{3,2,1,0:T(8,128)} %get-tuple-element.14, f32[2,12,256]{2,1,0:T(8,128)S(1)} %get-tuple-element.13), kind=kOutput, calls=%fused_computation.60 | convolution fusion | flops 1022754816 | bytes 36200448 | tf_op jit(solution)/shard_map/vmap(vmap(hqk,khd->qhd))/dot_general | solution.py:89
  206.2 27.6 %all_to_all.28 = bf16[32,24,768]{2,1,0:T(8,128)(2,1)S(1)} all-to-all(bf16[32,24,768]{2,1,0:T(8,128)(2,1)S(1)} %bitcast.91), channel_id=1, replica_groups=mesh['space'=32,'level'=8] {'space'}, dimensions={0} | all-to-all | bytes 2359296 | tf_op jit(solution)/shard_map/all_to_all | solution.py:29
  234.7 3.4 %all-to-all-start.3 = ((bf16[8,24,768]{2,1,0:T(8,128)(2,1)}), bf16[8,24,768]{2,1,0:T(8,128)(2,1)S(1)}, u32[]{:S(2)}, u32[]{:S(2)}) async-start(bf16[8,24,768]{2,1,0:T(8,128)(2,1)} %broadcast_in_dim.59), calls=%async_computation.3 | async-start | bytes 589824 | tf_op jit(solution)/shard_map/all_to_all | solution.py:35
  241.2 9.3 %all-to-all-done.3 = bf16[8,24,768]{2,1,0:T(8,128)(2,1)S(1)} async-done(((bf16[8,24,768]{2,1,0:T(8,128)(2,1)}), bf16[8,24,768]{2,1,0:T(8,128)(2,1)S(1)}, u32[]{:S(2)}, u32[]{:S(2)}) %all-to-all-start.3) | async-done | bytes 294944 | tf_op jit(solution)/shard_map/all_to_all | solution.py:35
  (79 shorter events, 33.1 us)
Async XLA Ops:
  0.6 97.0 %copy-start = (bf16[768,768]{1,0:T(8,128)(2,1)S(1)}, bf16[768,768]{1,0:T(8,128)(2,1)}, u32[]{:S(2)}) copy-start(bf16[768,768]{1,0:T(8,128)(2,1)} %param.21) | copy-start | bytes 3538948
  0.6 12.8 %copy-start.11 = (f32[12,8,8]{0,2,1:T(8,128)S(1)}, f32[12,8,8]{0,2,1:T(8,128)}, u32[]{:S(2)}) copy-start(f32[12,8,8]{0,2,1:T(8,128)} %param.22) | copy-start | bytes 9220
  0.7 36.4 %copy-start.15 = (bf16[768,768]{1,0:T(8,128)(2,1)S(1)}, bf16[768,768]{1,0:T(8,128)(2,1)}, u32[]{:S(2)}) copy-start(bf16[768,768]{1,0:T(8,128)(2,1)} %param.20) | copy-start | bytes 3538948
  4.5 32.6 %all-to-all-start = ((bf16[1,8,64,768]{3,2,0,1:T(8,128)(2,1)}), bf16[1,8,64,768]{3,2,0,1:T(8,128)(2,1)S(1)}, u32[]{:S(2)}, u32[]{:S(2)}) async-start(bf16[1,8,64,768]{3,2,0,1:T(8,128)(2,1)} %bitcast.1), calls=%async_computation | async-start | bytes 1572864 | tf_op jit(solution)/shard_map/all_to_all | solution.py:117
  56.0 11.7 %copy-start.3 = (bf16[8,64,12,64]{3,2,1,0:T(8,128)(2,1)S(1)}, bf16[8,64,12,64]{3,2,1,0:T(8,128)(2,1)}, u32[]{:S(2)}) copy-start(bf16[8,64,12,64]{3,2,1,0:T(8,128)(2,1)} %reshape.153) | copy-start | bytes 2359300
  69.4 6.6 %copy-start.13 = (s32[2,4]{1,0:T(2,128)S(1)}, s32[2,4]{1,0:T(2,128)}, u32[]{:S(2)}) copy-start(s32[2,4]{1,0:T(2,128)} %param.29) | copy-start | bytes 100
  69.5 6.7 %copy-start.18 = (s32[2]{0:T(128)S(1)}, s32[2]{0:T(128)}, u32[]{:S(2)}) copy-start(s32[2]{0:T(128)} %param.30) | copy-start | bytes 28
  69.5 6.9 %copy-start.14 = (f32[12,2]{0,1:T(2,128)S(1)}, f32[12,2]{0,1:T(2,128)}, u32[]{:S(2)}) copy-start(f32[12,2]{0,1:T(2,128)} %param.28) | copy-start | bytes 292
  71.5 5.9 %copy-start.4 = (bf16[768,768]{1,0:T(8,128)(2,1)S(1)}, bf16[768,768]{1,0:T(8,128)(2,1)}, u32[]{:S(2)}) copy-start(bf16[768,768]{1,0:T(8,128)(2,1)} %param.25) | copy-start | bytes 3538948
  71.5 26.1 %copy-start.2 = (bf16[1,512,768]{2,1,0:T(8,128)(2,1)S(1)}, bf16[1,512,768]{2,1,0:T(8,128)(2,1)}, u32[]{:S(2)}) copy-start(bf16[1,512,768]{2,1,0:T(8,128)(2,1)} %param.16) | copy-start | bytes 2359300
  71.5 26.1 %all-to-all-start.1 = ((bf16[8,1,64,768]{3,2,1,0:T(8,128)(2,1)}), bf16[8,1,64,768]{3,2,1,0:T(8,128)(2,1)}, u32[]{:S(2)}, u32[]{:S(2)}) async-start(bf16[8,1,64,768]{3,2,1,0:T(8,128)(2,1)} %bitcast.89), calls=%async_computation.1 | async-start | bytes 1572864 | tf_op jit(solution)/shard_map/all_to_all | solution.py:126
  78.5 21.3 %copy-start.12 = (f32[768]{0:T(1024)S(1)}, f32[768]{0:T(1024)}, u32[]{:S(2)}) copy-start(f32[768]{0:T(1024)} %param.23) | copy-start | bytes 9220
  97.6 10.1 %copy-start.5 = (bf16[768,768]{1,0:T(8,128)(2,1)S(1)}, bf16[768,768]{1,0:T(8,128)(2,1)}, u32[]{:S(2)}) copy-start(bf16[768,768]{1,0:T(8,128)(2,1)} %param.26) | copy-start | bytes 3538948
  97.6 10.1 %copy-start.7 = (bf16[768,1536]{1,0:T(8,128)(2,1)S(1)}, bf16[768,1536]{1,0:T(8,128)(2,1)}, u32[]{:S(2)}) copy-start(bf16[768,1536]{1,0:T(8,128)(2,1)} %constant_dynamic-update-slice_fusion.1) | copy-start | bytes 7077892
  99.8 9.4 %copy-start.16 = (bf16[768,768]{1,0:T(8,128)(2,1)S(1)}, bf16[768,768]{1,0:T(8,128)(2,1)}, u32[]{:S(2)}) copy-start(bf16[768,768]{1,0:T(8,128)(2,1)} %param.24) | copy-start | bytes 3538948
  100.9 21.6 %collective-permute-start.3 = (bf16[1,512,768]{2,1,0:T(8,128)(2,1)}, bf16[1,512,768]{2,1,0:T(8,128)(2,1)}, u32[]{:S(2)}, u32[]{:S(2)}) collective-permute-start(bf16[1,512,768]{2,1,0:T(8,128)(2,1)} %fusion.28), channel_id=1, source_target_pairs={{0,240},{8,248},{16,0},{24,8},{32,16},{40,24},{48,32},{56,40},{64,... | collective-permute-start | bytes 2359304 | tf_op jit(solution)/shard_map/ppermute | solution.py:18
  105.9 23.4 %collective-permute-start.2 = (bf16[1,512,768]{2,1,0:T(8,128)(2,1)}, bf16[1,512,768]{2,1,0:T(8,128)(2,1)}, u32[]{:S(2)}, u32[]{:S(2)}) collective-permute-start(bf16[1,512,768]{2,1,0:T(8,128)(2,1)} %fusion.28), channel_id=1, source_target_pairs={{0,248},{8,0},{16,8},{24,16},{32,24},{40,32},{48,40},{56,48},{64,5... | collective-permute-start | bytes 2359304 | tf_op jit(solution)/shard_map/ppermute | solution.py:18
  106.7 22.7 %collective-permute-start.1 = (bf16[1,512,768]{2,1,0:T(8,128)(2,1)}, bf16[1,512,768]{2,1,0:T(8,128)(2,1)}, u32[]{:S(2)}, u32[]{:S(2)}) collective-permute-start(bf16[1,512,768]{2,1,0:T(8,128)(2,1)} %fusion.28), channel_id=1, source_target_pairs={{0,16},{8,24},{16,32},{24,40},{32,48},{40,56},{48,64},{56,72},{64,... | collective-permute-start | bytes 2359304 | tf_op jit(solution)/shard_map/ppermute | solution.py:18
  106.7 26.1 %collective-permute-start = (bf16[1,512,768]{2,1,0:T(8,128)(2,1)}, bf16[1,512,768]{2,1,0:T(8,128)(2,1)}, u32[]{:S(2)}, u32[]{:S(2)}) collective-permute-start(bf16[1,512,768]{2,1,0:T(8,128)(2,1)} %fusion.28), channel_id=1, source_target_pairs={{0,8},{8,16},{16,24},{24,32},{32,40},{40,48},{48,56},{56,64},{64,7... | collective-permute-start | bytes 2359304 | tf_op jit(solution)/shard_map/ppermute | solution.py:18
  112.5 20.3 %copy-start.9 = (bf16[768,1536]{1,0:T(8,128)(2,1)S(1)}, bf16[768,1536]{1,0:T(8,128)(2,1)}, u32[]{:S(2)}) copy-start(bf16[768,1536]{1,0:T(8,128)(2,1)} %copy-done.8) | copy-start | bytes 7077892
  166.2 6.3 %copy-start.6 = (bf16[2,256,12,64]{1,0,3,2:T(2,128)(2,1)S(1)}, bf16[2,256,12,64]{1,0,3,2:T(2,128)(2,1)}, u32[]{:S(2)}) copy-start(bf16[2,256,12,64]{1,0,3,2:T(2,128)(2,1)} %reshape.161) | copy-start | bytes 2359300
  166.2 6.3 %copy-start.10 = (f32[2,8,5,256]{3,1,2,0:T(8,128)S(1)}, f32[2,8,5,256]{3,1,2,0:T(8,128)}, u32[]{:S(2)}) copy-start(f32[2,8,5,256]{3,1,2,0:T(8,128)} %copy.73) | copy-start | bytes 245764
  234.7 15.8 %all-to-all-start.3 = ((bf16[8,24,768]{2,1,0:T(8,128)(2,1)}), bf16[8,24,768]{2,1,0:T(8,128)(2,1)S(1)}, u32[]{:S(2)}, u32[]{:S(2)}) async-start(bf16[8,24,768]{2,1,0:T(8,128)(2,1)} %broadcast_in_dim.59), calls=%async_computation.3 | async-start | bytes 589824 | tf_op jit(solution)/shard_map/all_to_all | solution.py:35
  238.1 13.1 %copy-start.1 = (bf16[768,768]{1,0:T(8,128)(2,1)S(1)}, bf16[768,768]{1,0:T(8,128)(2,1)}, u32[]{:S(2)}) copy-start(bf16[768,768]{1,0:T(8,128)(2,1)} %param.21) | copy-start | bytes 3538948
  (2 other events, 2.5 us)
where the time goes:
time: 252 us; the launch traced here: 251 us
  waiting for transfers between devices  68.7 us (27%)
  matrix products  62 us (25%)
  local copies, waits for them, and re-layouts  44.1 us (18%)
  blocking collectives  27.6 us (11%)
  other arithmetic  24.2 us (10%)
  starting transfers between devices  23.7 us (9%)
    all_to_all x1, blocking collectives, summed_on_arrival(): lax.all_to_all(pieces, axis, split_axis=0, concat_axis=0, tiled=True)  27.6 us
    all_to_all x1, waiting for transfers between devices, body(): lax.all_to_all(split_in, 'level', split_axis=1, concat_axis=0, tiled=True)  23.4 us
    all_to_all x1, waiting for transfers between devices, body(): lax.all_to_all(mixture, 'level', split_axis=0, concat_axis=1, tiled=True)  19.1 us
    dot_general x4, matrix products, project(): jnp.dot(inputs, weight, preferred_element_type=jnp.float32)  17.8 us
    sub x1, matrix products, patch_heads(): weights = jax.nn.softmax(scores, axis=-1).astype(jnp.bfloat16)  17.4 us
    ppermute x4, waiting for transfers between devices, passed_along(): return lax.ppermute(value, axis, pairs)  16.9 us
    dot_general x1, matrix products, patch_heads(): jnp.einsum('hqk,khd->qhd', weights, value_heads, preferred_element_type=j...  14.3 us
    sub x1, other arithmetic, vertical_heads(): weights = jax.nn.softmax(scores, axis=2).astype(jnp.bfloat16)  11.7 us
  transfers between devices with their start and end apart: 7, of which 7 were waited for; matrix products, arithmetic and copies ran while one was open for 5% of the time, Pallas kernels for 0%

commit v1 on v0

v1 whole, which is shorter than its diff:
```python
import functools

import jax
import jax.numpy as jnp
from jax import lax
from jax.experimental import pallas as pl
from jax.experimental.pallas import tpu as pltpu
from jax.sharding import PartitionSpec as P

H = 12
HD = 64
PATCH = 256
PAIRS = H // 2
GROUP = 16
LOG2E = 1.4426950408889634
epsilon = 1e-06
BF = jnp.bfloat16
F32 = jnp.float32
VMEM_BYTES = 24 * 1024 * 1024


def nn(a, b):
    return jnp.dot(a, b, preferred_element_type=F32)


def nt(a, b):
    return lax.dot_general(a, b, (((1,), (1,)), ((), ())), preferred_element_type=F32)


def normalize(values, gain):
    widened = values.astype(F32)
    mean_square = jnp.mean(widened * widened, axis=-1, keepdims=True)
    return (widened * lax.rsqrt(mean_square + epsilon) * gain).astype(BF)


def paired(two_heads):
    zero = jnp.zeros((HD, two_heads.shape[1]), BF)
    top = jnp.concatenate((two_heads[:HD], zero), axis=1)
    low = jnp.concatenate((zero, two_heads[HD:]), axis=1)
    return jnp.concatenate((top, low), axis=0)


def mixed(values, weights):
    ones = jnp.ones((16, values.shape[1]), BF)
    return nn(jnp.concatenate((values, ones), axis=0), weights)


def vertical_kernel(x, gain, wq, wk, wv, wo, bias, out, normed, q, k, v, mix):
    levels, columns, features = x.shape
    tokens = levels * columns
    block = levels * GROUP
    for level in range(levels):
        rows = normalize(x[level], gain[...])
        for part in range(columns // GROUP):
            place = part * block + level * GROUP
            normed[place : place + GROUP] = rows[part * GROUP : (part + 1) * GROUP]
    for start in range(0, tokens, 256):
        piece = normed[start : start + 256]
        q[:, start : start + 256] = (nt(wq[...], piece) * (HD**-0.5 * LOG2E)).astype(BF)
        v[:, start : start + 256] = nt(wv[...], piece).astype(BF)
        k[start : start + 256] = nn(piece, wk[...]).astype(BF)
    for part in range(columns // GROUP):
        span = slice(part * block, (part + 1) * block)
        for pair in range(PAIRS):
            heads = slice(pair * 128, (pair + 1) * 128)
            scores = nn(k[span, heads], paired(q[heads, span])) + bias[pair]
            top = jnp.max(scores, axis=0, keepdims=True)
            weights = jnp.exp2(scores - top).astype(BF)
            for half in range(2):
                head = slice(pair * 128 + half * HD, pair * 128 + half * HD + HD)
                total = mixed(v[head, span], weights[:, half * block : (half + 1) * block])
                mix[head, span] = (total[:HD] / total[HD : HD + 1]).astype(BF)
    for part in range(columns // GROUP):
        span = slice(part * block, (part + 1) * block)
        projected = nn(mix[:, span].T, wo[...])
        for level in range(levels):
            place = slice(part * GROUP, (part + 1) * GROUP)
            out[level, place] = (
                x[level, place].astype(F32) + projected[level * GROUP : (level + 1) * GROUP]
            ).astype(BF)


def attend(pair, own, start, column, first, q, k, v, pbias, acc, top, total, acc_in, top_in, total_in):
    heads = slice(pair * 128, (pair + 1) * 128)
    mine = slice(own * PATCH, (own + 1) * PATCH)
    row = slice(own * PAIRS + pair, own * PAIRS + pair + 1)
    scores = nn(k[pl.ds(start, PATCH), heads], paired(q[heads, mine]))
    lane = lax.broadcasted_iota(jnp.int32, (1, 2 * PATCH), 1)
    bias = jnp.where(lane < PATCH, pbias[2 * pair, column], pbias[2 * pair + 1, column]) * LOG2E
    largest = jnp.max(scores, axis=0, keepdims=True) + bias
    if not first:
        before = top_in[row]
        largest = jnp.maximum(before, largest)
        fade = jnp.exp2(before - largest)
    weights = jnp.exp2(scores - (largest - bias)).astype(BF)
    top[row] = largest
    sums = []
    for half in range(2):
        head = slice(pair * 128 + half * HD, pair * 128 + half * HD + HD)
        part = slice(half * PATCH, (half + 1) * PATCH)
        found = mixed(v[head, pl.ds(start, PATCH)], weights[:, part])
        sums.append(found[HD : HD + 1])
        if first:
            acc[head, mine] = found[:HD]
        else:
            acc[head, mine] = acc_in[head, mine] * fade[:, part] + found[:HD]
    both = jnp.concatenate(sums, axis=1)
    total[row] = both if first else total_in[row] * fade + both


def keys_values(x, gain, wk, wv, k, v, wq=None, q=None):
    for start in range(0, x.shape[0], PATCH):
        span = slice(start, start + PATCH)
        piece = normalize(x[span], gain[...])
        if wq is not None:
            q[:, span] = (nt(wq[...], piece) * (HD**-0.5 * LOG2E)).astype(BF)
        v[:, span] = nt(wv[...], piece).astype(BF)
        k[span] = nn(piece, wk[...]).astype(BF)


def own_kernel(pbias, x, gain, wq, wk, wv, q, acc, top, total, k, v):
    keys_values(x, gain, wk, wv, k, v, wq, q)
    for own in range(2):
        for pair in range(PAIRS):
            attend(pair, own, own * PATCH, 0, True, q, k, v, pbias, acc, top, total, None, None, None)


def arrived_part(source, near, live, pbias, x, gain, wk, wv, q, acc, top, total, k, v):
    keys_values(x, gain, wk, wv, k, v)
    for own in range(2):
        found = jnp.int32(-1)
        for entry in range(near.shape[1]):
            listed = near[own, entry]
            hit = jnp.logical_and(entry < live[own], lax.shift_right_arithmetic(listed, 1) == source[0])
            found = jnp.where(hit, jnp.bitwise_and(listed, 1), found)

        @pl.when(found >= 0)
        def _():
            start = pl.multiple_of(found * PATCH, PATCH)
            for pair in range(PAIRS):
                attend(pair, own, start, 1, False, q, k, v, pbias, acc, top, total, acc, top, total)


def arrived_kernel(source, near, live, pbias, x, gain, wk, wv, q, acc_in, top_in, total_in, acc, top, total, k, v):
    acc[...] = acc_in[...]
    top[...] = top_in[...]
    total[...] = total_in[...]
    arrived_part(source, near, live, pbias, x, gain, wk, wv, q, acc, top, total, k, v)


def last_kernel(
    source, near, live, pbias, x, gain, wk, wv, q, acc_in, top_in, total_in, cot, mix, grad, acc, top, total, k, v
):
    acc[...] = acc_in[...]
    top[...] = top_in[...]
    total[...] = total_in[...]
    arrived_part(source, near, live, pbias, x, gain, wk, wv, q, acc, top, total, k, v)
    for pair in range(PAIRS):
        heads = slice(pair * 128, (pair + 1) * 128)
        for own in range(2):
            mine = slice(own * PATCH, (own + 1) * PATCH)
            inverse = 1.0 / total[own * PAIRS + pair : own * PAIRS + pair + 1]
            for half in range(2):
                head = slice(pair * 128 + half * HD, pair * 128 + half * HD + HD)
                mix[head, mine] = (
                    acc[head, mine] * inverse[:, half * PATCH : (half + 1) * PATCH]
                ).astype(BF)
        grad[heads] = nn(mix[heads], cot[...]).astype(BF)


IN_VMEM = pl.BlockSpec(memory_space=pltpu.VMEM)
IN_SMEM = pl.BlockSpec(memory_space=pltpu.SMEM)


def call(kernel, scalars, arrays, outs, scratch, flops, name):
    shapes = [jax.ShapeDtypeStruct(shape, kind) for shape, kind in outs]
    moved = sum(a.size * a.dtype.itemsize for a in arrays)
    return pl.pallas_call(
        kernel,
        out_shape=shapes,
        in_specs=[IN_SMEM] * len(scalars) + [IN_VMEM] * len(arrays),
        out_specs=[IN_VMEM] * len(outs),
        scratch_shapes=[pltpu.VMEM(shape, kind) for shape, kind in scratch],
        compiler_params=pltpu.CompilerParams(vmem_limit_bytes=VMEM_BYTES),
        cost_estimate=pl.CostEstimate(flops=flops, bytes_accessed=moved, transcendentals=0),
        name=name,
    )(*scalars, *arrays)


def expanded_bias(level_bias):
    heads, levels, _ = level_bias.shape
    same = jnp.eye(GROUP, dtype=bool)[None, :, None, :]
    table = (level_bias * LOG2E).reshape(PAIRS, 2, levels, levels)
    table = table.transpose(0, 3, 1, 2)
    wide = jnp.where(same, table.reshape(PAIRS * levels, 1, 2 * levels, 1), -jnp.inf)
    return wide.reshape(PAIRS, levels * GROUP, 2 * levels * GROUP)


def body(
    fields,
    norm_vert,
    query_vert,
    keys_vert,
    values_vert,
    out_vert,
    level_bias,
    norm_patch,
    query_patch,
    keys_patch,
    values_patch,
    out_patch,
    patch_bias,
    neighbours,
    counts,
    cotangent,
):
    _, columns, features = fields.shape
    levels = lax.axis_size("level")
    devices = lax.axis_size("space")
    place = lax.axis_index("space")
    share = columns // levels
    square = features * features
    tokens_state = [((features, columns), F32), ((2 * PAIRS, 2 * PATCH), F32), ((2 * PAIRS, 2 * PATCH), F32)]
    key_scratch = [((columns, features), BF), ((features, columns), BF)]

    def moved(value, source_of):
        return lax.ppermute(value, "space", [(source_of(d) % devices, d) for d in range(devices)])

    x = lax.all_to_all(fields.reshape(levels, share, features), "level", 0, 0, tiled=True)
    hidden = call(
        vertical_kernel,
        [],
        [x, norm_vert[None], query_vert.T, keys_vert, values_vert.T, out_vert, expanded_bias(level_bias)],
        [((levels, share, features), BF)],
        [((columns, features), BF), ((features, columns), BF), *key_scratch, ((features, columns), BF)],
        8 * columns * square,
        "vertical",
    )[0]
    hidden = lax.all_to_all(hidden, "level", 0, 0, tiled=True).reshape(columns, features)

    def outer(d):
        return d + 2 if d % 2 == 0 else d - 2

    def inner(d):
        return d - 2 if d % 2 == 0 else d + 2

    def twin(d):
        return d ^ 1

    from_outer = moved(hidden, outer)
    from_twin = moved(hidden, twin)
    from_inner = moved(hidden, inner)
    passed_on = moved(from_outer, twin)
    side = 1 - 2 * (place % 2)
    outer_at = (place + 2 * side) % devices
    inner_at = (place - 2 * side) % devices
    twin_at = place + side
    passed_at = (place - side) % devices
    gain = norm_patch[None]
    wv = values_patch.T
    q, acc, top, total = call(
        own_kernel,
        [patch_bias],
        [hidden, gain, query_patch.T, keys_patch, wv],
        [((features, columns), BF), *tokens_state],
        key_scratch,
        8 * columns * square,
        "own",
    )
    state = [acc, top, total]
    for block, at in ((from_twin, twin_at), (from_outer, outer_at), (passed_on, passed_at)):
        state = call(
            arrived_kernel,
            [at[None], neighbours, counts, patch_bias],
            [block, gain, keys_patch, wv, q, *state],
            tokens_state,
            key_scratch,
            6 * columns * square,
            "arrived",
        )
    mix, grad = call(
        last_kernel,
        [inner_at[None], neighbours, counts, patch_bias],
        [from_inner, gain, keys_patch, wv, q, *state, cotangent.reshape(columns, features)],
        [((features, columns), BF), ((features, features), BF)],
        [*tokens_state, *key_scratch],
        8 * columns * square,
        "last",
    )
    pieces = lax.all_to_all(grad.reshape(devices, features // devices, features), "space", 0, 0, tiled=True)
    shares = pieces.astype(F32).sum(axis=0).astype(BF)
    spread = jnp.broadcast_to(shares[None], (levels, *shares.shape))
    grad_wo = lax.all_to_all(spread, "level", 0, 0, tiled=True).astype(F32).sum(axis=0)
    projected = lax.dot_general(mix, out_patch, (((0,), (0,)), ((), ())), preferred_element_type=F32)
    out_fields = (hidden.astype(F32) + projected).astype(BF)
    return (out_fields[None], grad_wo)


def solution(mesh):
    return jax.shard_map(
        body,
        mesh=mesh,
        in_specs=(
            P("level", "space", None),
            *([P()] * 12),
            P("space", None),
            P("space"),
            P("level", "space", None),
        ),
        out_specs=(P("level", "space", None), P("space", None)),
        check_vma=False,
    )
```

time: 252 us -> 172 us (0.68)
  matrix products: 62 us -> 2.83 us
  Pallas kernels: 0 us -> 40 us
  waiting for transfers between devices: 68.7 us -> 31 us
  local copies, waits for them, and re-layouts: 44.1 us -> 17.1 us
  blocking collectives: 27.6 us -> 48.5 us
  other arithmetic: 24.2 us -> 4 us
    dot_general x10 -> x1, matrix products: 44.6 us -> 2.83 us  [body(): lax.dot_general(mix, out_patch, (((0,), (0,)), ((), ())), preferred_eleme...]
    pallas_call x0 -> x6, Pallas kernels: none -> 40 us  [call(): pl.pallas_call(kernel, out_shape=shapes, in_specs=[IN_SMEM] * len(scalars...]
    all_to_all x3 -> x2, waiting for transfers between devices: 51.8 us -> 22.4 us  [the longest x1 12.2 us: body(): lax.all_to_all(fields.reshape(levels, share, features), 'level', 0, 0, ti...]
    all_to_all x1 -> x2, blocking collectives: 27.6 us -> 48.5 us  [the longest x1 26.6 us: body(): lax.all_to_all(hidden, 'level', 0, 0, tiled=True).reshape(columns, features)]
    slice x6 -> x0, local copies, waits for them, and re-layouts: 19.5 us -> none  [the longest x2 11.6 us: patch_heads(): key_heads = keys_all[:, :features].reshape(-1, H, HD)]
    sub x1 -> x0, matrix products: 17.4 us -> none  [patch_heads(): weights = jax.nn.softmax(scores, axis=-1).astype(jnp.bfloat16)]
    sub x1 -> x0, other arithmetic: 11.7 us -> none  [vertical_heads(): weights = jax.nn.softmax(scores, axis=2).astype(jnp.bfloat16)]
    reshape x3 -> x0, local copies, waits for them, and re-layouts: 8.73 us -> none  [the longest x1 3.77 us: vertical_heads(): key_heads = keys_in.reshape(keys_in.shape[0], columns, H, HD)]
  transfers between devices with their start and end apart: 7 -> 6, of which waited for: 7 -> 3; matrix products, arithmetic and copies ran while one was open for 5% -> 10% of each run, Pallas kernels for 0% -> 14%
where the time goes in v1:
time: 172 us; the launch traced here: 170 us
  blocking collectives  48.5 us (28%)
  Pallas kernels  40 us (23%)
  waiting for transfers between devices  31 us (18%)
  starting transfers between devices  25.2 us (15%)
  local copies, waits for them, and re-layouts  17.1 us (10%)
  other arithmetic  4 us (2%)
  matrix products  2.83 us (2%)
    pallas_call x6, Pallas kernels, call(): pl.pallas_call(kernel, out_shape=shapes, in_specs=[IN_SMEM] * len(scalars...  40 us
    all_to_all x1, blocking collectives, body(): lax.all_to_all(hidden, 'level', 0, 0, tiled=True).reshape(columns, features)  26.6 us
    all_to_all x1, blocking collectives, body(): lax.all_to_all(grad.reshape(devices, features // devices, features), 'spa...  21.9 us
    ppermute x4, starting transfers between devices, moved(): lax.ppermute(value, 'space', [(source_of(d) % devices, d) for d in range(...  12.6 us
    all_to_all x1, waiting for transfers between devices, body(): lax.all_to_all(fields.reshape(levels, share, features), 'level', 0, 0, ti...  12.2 us
    unnamed x40, local copies, waits for them, and re-layouts  10.5 us
    all_to_all x1, waiting for transfers between devices, body(): lax.all_to_all(spread, 'level', 0, 0, tiled=True).astype(F32).sum(axis=0)  10.1 us
    all_to_all x1, starting transfers between devices, body(): lax.all_to_all(fields.reshape(levels, share, features), 'level', 0, 0, ti...  9.16 us
  transfers between devices with their start and end apart: 6, of which 3 were waited for; matrix products, arithmetic and copies ran while one was open for 10% of the time, Pallas kernels for 14%

profile of v1, /device:TPU:1, one launch (start us, length us, event | category | flops | bytes accessed | tf_op | source)
XLA Modules:
  0.0 169.6 jit_solution(17299887040722220935)
XLA Ops:
  0.7 9.2 %all-to-all-start = ((bf16[8,64,768]{2,1,0:T(8,128)(2,1)}), bf16[8,64,768]{2,1,0:T(8,128)(2,1)}, u32[]{:S(2)}, u32[]{:S(2)}) async-start(bf16[8,64,768]{2,1,0:T(8,128)(2,1)} %bitcast.31), calls=%async_computation | async-start | bytes 1572864 | tf_op jit(solution)/shard_map/all_to_all | solution.py:229
  10.1 3.1 %broadcast_select_fusion = f32[48,16,16,16]{3,2,1,0:T(8,128)} fusion(f32[48,16]{1,0:T(8,128)S(1)} %reshape.39, pred[16,16]{1,0:T(8,128)(4,1)S(1)} %iota_compare_fusion), kind=kLoop, calls=%fused_computation | loop fusion | flops 196608 | bytes 789760 | tf_op jit(solution)/shard_map/jit(_where)/select_n | solution.py:195
  13.3 5.7 %select_n.28.bias = f32[6,128,256]{2,1,0:T(8,128)} reshape(f32[48,16,16,16]{3,2,1,0:T(8,128)} %broadcast_select_fusion) | data formatting | bytes 1572864 | tf_op jit(solution)/shard_map/jit(_where)/select_n | solution.py:195
  19.6 1.6 copy.40
  21.2 12.2 %all-to-all-done.x = bf16[8,64,768]{2,1,0:T(8,128)(2,1)} async-done(((bf16[8,64,768]{2,1,0:T(8,128)(2,1)}), bf16[8,64,768]{2,1,0:T(8,128)(2,1)}, u32[]{:S(2)}, u32[]{:S(2)}) %all-to-all-start) | async-done | bytes 786464 | tf_op jit(solution)/shard_map/all_to_all | solution.py:229
  34.6 1.3 copy-done.2
  35.9 1.3 copy-done.3
  37.2 8.7 %vertical.1 = bf16[8,64,768]{2,1,0:T(8,128)(2,1)S(1)} custom-call(bf16[8,64,768]{2,1,0:T(8,128)(2,1)} %all-to-all-done.x, f32[1,768]{1,0:T(1,128)S(1)} %broadcast_in_dim.50.gain, bf16[768,768]{1,0:T(8,128)(2,1)S(1)} %bitcast.28, bf16[768,768]{1,0:T(8,128)(2,1)S(1)} %copy-done.2, bf16[768,768]{1,0:T(8,128)(2,1)S(1)} %bitcast.29, ...), custom_call_target="tpu_custom_call" | custom-call | flops 2415919104 | bytes 6294528 | tf_op jit(solution)/shard_map/vertical/pallas_call | solution.py:178
  45.9 26.6 %all_to_all.20 = bf16[8,64,768]{2,1,0:T(8,128)(2,1)} all-to-all(bf16[8,64,768]{2,1,0:T(8,128)(2,1)S(1)} %vertical.1), channel_id=1, replica_groups=mesh['space'=32,'level'=8] {'level'}, dimensions={0} | all-to-all | bytes 1572864 | tf_op jit(solution)/shard_map/all_to_all | solution.py:239
  72.5 1.2 collective-permute-start.1
  73.7 4.7 %collective-permute-start.3 = (bf16[512,768]{1,0:T(8,128)(2,1)}, bf16[512,768]{1,0:T(8,128)(2,1)}, u32[]{:S(2)}, u32[]{:S(2)}) collective-permute-start(bf16[512,768]{1,0:T(8,128)(2,1)} %bitcast.5.x), channel_id=1, source_target_pairs={{8,0},{0,8},{24,16},{16,24},{40,32},{32,40},{56,48},{48,56},{72,64... | collective-permute-start | bytes 2359304 | tf_op jit(solution)/shard_map/ppermute | solution.py:227
  78.4 8.6 %collective-permute-done.1.x = bf16[512,768]{1,0:T(8,128)(2,1)} collective-permute-done((bf16[512,768]{1,0:T(8,128)(2,1)}, bf16[512,768]{1,0:T(8,128)(2,1)}, u32[]{:S(2)}, u32[]{:S(2)}) %collective-permute-start.1) | collective-permute-done | bytes 786464 | tf_op jit(solution)/shard_map/ppermute | solution.py:227
  88.2 5.5 %collective-permute-start = (bf16[512,768]{1,0:T(8,128)(2,1)}, bf16[512,768]{1,0:T(8,128)(2,1)}, u32[]{:S(2)}, u32[]{:S(2)}) collective-permute-start(bf16[512,768]{1,0:T(8,128)(2,1)} %bitcast.5.x), channel_id=1, source_target_pairs={{240,0},{24,8},{0,16},{40,24},{16,32},{56,40},{32,48},{72,56},{48,... | collective-permute-start | bytes 2359304 | tf_op jit(solution)/shard_map/ppermute | solution.py:227
  94.5 1.6 copy.45
  96.2 1.3 copy-done.4
  97.4 7.0 %own.1 = (bf16[768,512]{1,0:T(8,128)(2,1)S(1)}, f32[768,512]{1,0:T(8,128)S(1)}, f32[12,512]{1,0:T(8,128)S(1)}, f32[12,512]{1,0:T(8,128)S(1)}) custom-call(f32[12,2]{1,0:T(8,128)S(1)} %copy.50.pbias, bf16[512,768]{1,0:T(8,128)(2,1)} %bitcast.5.x, f32[1,768]{1,0:T(1,128)S(1)} %broadcast_in_dim.56.gain, bf16[768,768]{1,0:T(8,128)(2,1)S(1)} %bitcast.26, ...), custom_call_target="tpu_custom_call" | custom-call | flops 2415919104 | bytes 4328448 | tf_op jit(solution)/shard_map/own/pallas_call | solution.py:178
  104.5 4.8 %arrived.3 = (f32[768,512]{1,0:T(8,128)S(1)}, f32[12,512]{1,0:T(8,128)S(1)}, f32[12,512]{1,0:T(8,128)S(1)}) custom-call(s32[1]{0:T(128)} %bitcast.11.source, s32[2,4]{1,0:T(2,128)S(1)} %copy-done.7, s32[2]{0:T(128)S(1)} %copy-done.8, f32[12,2]{1,0:T(8,128)S(1)} %copy.50.pbias, bf16[512,768]{1,0:T(8,128)(2,1)} %collective-permute-done.3.x, ...), custom_call_target="tpu_custom_call" | custom-call | flops 1811939328 | bytes 5557248 | tf_op jit(solution)/shard_map/arrived/pallas_call | solution.py:178
  109.2 7.0 %arrived.4 = (f32[768,512]{1,0:T(8,128)S(1)}, f32[12,512]{1,0:T(8,128)S(1)}, f32[12,512]{1,0:T(8,128)S(1)}) custom-call(s32[1]{0:T(128)} %bitcast.10.source, s32[2,4]{1,0:T(2,128)S(1)} %copy-done.7, s32[2]{0:T(128)S(1)} %copy-done.8, f32[12,2]{1,0:T(8,128)S(1)} %copy.50.pbias, bf16[512,768]{1,0:T(8,128)(2,1)} %collective-permute-done.1.x, ...), custom_call_target="tpu_custom_call" | custom-call | flops 1811939328 | bytes 5557248 | tf_op jit(solution)/shard_map/arrived/pallas_call | solution.py:178
  116.2 4.9 %arrived.5 = (f32[768,512]{1,0:T(8,128)S(1)}, f32[12,512]{1,0:T(8,128)S(1)}, f32[12,512]{1,0:T(8,128)S(1)}) custom-call(s32[1]{0:T(128)} %bitcast.9.source, s32[2,4]{1,0:T(2,128)S(1)} %copy-done.7, s32[2]{0:T(128)S(1)} %copy-done.8, f32[12,2]{1,0:T(8,128)S(1)} %copy.50.pbias, bf16[512,768]{1,0:T(8,128)(2,1)} %collective-permute-done.2.x, ...), custom_call_target="tpu_custom_call" | custom-call | flops 1811939328 | bytes 5557248 | tf_op jit(solution)/shard_map/arrived/pallas_call | solution.py:178
  121.2 7.6 %last.1 = (bf16[768,512]{1,0:T(8,128)(2,1)S(1)}, bf16[768,768]{1,0:T(8,128)(2,1)S(1)}) custom-call(s32[1]{0:T(128)} %bitcast.6.source, s32[2,4]{1,0:T(2,128)S(1)} %copy-done.7, s32[2]{0:T(128)S(1)} %copy-done.8, f32[12,2]{1,0:T(8,128)S(1)} %copy.50.pbias, bf16[512,768]{1,0:T(8,128)(2,1)} %collective-permute-done.x, f32[1,768]{1,0:T(1,128)S(1)} %broadcast_in_dim.56.gain, ...), custom_call_target="tpu_custom_call" | custom-call | flops 2415919104 | bytes 6343680 | tf_op jit(solution)/shard_map/last/pallas_call | solution.py:178
  129.7 21.9 %all_to_all.21 = bf16[32,24,768]{2,1,0:T(8,128)(2,1)S(1)} all-to-all(bf16[32,24,768]{2,1,0:T(8,128)(2,1)S(1)} %bitcast.27), channel_id=1, replica_groups=mesh['space'=32,'level'=8] {'space'}, dimensions={0} | all-to-all | bytes 2359296 | tf_op jit(solution)/shard_map/all_to_all | solution.py:290
  152.5 3.4 %all-to-all-start.3 = ((bf16[8,24,768]{2,1,0:T(8,128)(2,1)}), bf16[8,24,768]{2,1,0:T(8,128)(2,1)S(1)}, u32[]{:S(2)}, u32[]{:S(2)}) async-start(bf16[8,24,768]{2,1,0:T(8,128)(2,1)} %broadcast_in_dim.61), calls=%async_computation.3 | async-start | bytes 589824 | tf_op jit(solution)/shard_map/all_to_all | solution.py:293
  156.0 2.8 %fusion = bf16[1,512,768]{2,1,0:T(8,128)(2,1)} fusion(bf16[768,512]{1,0:T(8,128)(2,1)S(1)} %copy-done.10, bf16[768,768]{1,0:T(8,128)(2,1)S(1)} %copy-done, bf16[512,768]{1,0:T(8,128)(2,1)} %bitcast.5.x), kind=kOutput, calls=%fused_computation.2 | convolution fusion | flops 605159424 | bytes 3538944 | tf_op jit(solution)/shard_map/dot_general | solution.py:294
  158.8 10.1 %all-to-all-done.3 = bf16[8,24,768]{2,1,0:T(8,128)(2,1)S(1)} async-done(((bf16[8,24,768]{2,1,0:T(8,128)(2,1)}), bf16[8,24,768]{2,1,0:T(8,128)(2,1)S(1)}, u32[]{:S(2)}, u32[]{:S(2)}) %all-to-all-start.3) | async-done | bytes 294944 | tf_op jit(solution)/shard_map/all_to_all | solution.py:293
  (48 shorter events, 6.6 us)
Async XLA Ops:
  0.6 155.3 %copy-start = (bf16[768,768]{1,0:T(8,128)(2,1)S(1)}, bf16[768,768]{1,0:T(8,128)(2,1)}, u32[]{:S(2)}) copy-start(bf16[768,768]{1,0:T(8,128)(2,1)} %param.27) | copy-start | bytes 3538948
  0.6 9.2 %copy-start.13 = (f32[12,8,8]{0,2,1:T(8,128)S(1)}, f32[12,8,8]{0,2,1:T(8,128)}, u32[]{:S(2)}) copy-start(f32[12,8,8]{0,2,1:T(8,128)} %param.22) | copy-start | bytes 9220
  0.7 32.8 %all-to-all-start = ((bf16[8,64,768]{2,1,0:T(8,128)(2,1)}), bf16[8,64,768]{2,1,0:T(8,128)(2,1)}, u32[]{:S(2)}, u32[]{:S(2)}) async-start(bf16[8,64,768]{2,1,0:T(8,128)(2,1)} %bitcast.31), calls=%async_computation | async-start | bytes 1572864 | tf_op jit(solution)/shard_map/all_to_all | solution.py:229
  13.3 5.7 %copy-start.11 = (bf16[768,768]{1,0:T(8,128)(2,1)S(1)}, bf16[768,768]{1,0:T(8,128)(2,1)}, u32[]{:S(2)}) copy-start(bf16[768,768]{1,0:T(8,128)(2,1)} %param.18) | copy-start | bytes 3538948
  19.6 1.6 copy-start.14
  33.5 1.1 copy-start.1
  34.6 1.3 copy-start.2
  35.9 1.3 copy-start.3
  45.9 47.9 %copy-start.12 = (bf16[768,768]{1,0:T(8,128)(2,1)S(1)}, bf16[768,768]{1,0:T(8,128)(2,1)}, u32[]{:S(2)}) copy-start(bf16[768,768]{1,0:T(8,128)(2,1)} %param.26) | copy-start | bytes 3538948
  72.5 14.6 %collective-permute-start.1 = (bf16[512,768]{1,0:T(8,128)(2,1)}, bf16[512,768]{1,0:T(8,128)(2,1)}, u32[]{:S(2)}, u32[]{:S(2)}) collective-permute-start(bf16[512,768]{1,0:T(8,128)(2,1)} %bitcast.5.x), channel_id=1, source_target_pairs={{16,0},{248,8},{32,16},{8,24},{48,32},{24,40},{64,48},{40,56},{80,... | collective-permute-start | bytes 2359304 | tf_op jit(solution)/shard_map/ppermute | solution.py:227
  73.7 30.7 %collective-permute-start.3 = (bf16[512,768]{1,0:T(8,128)(2,1)}, bf16[512,768]{1,0:T(8,128)(2,1)}, u32[]{:S(2)}, u32[]{:S(2)}) collective-permute-start(bf16[512,768]{1,0:T(8,128)(2,1)} %bitcast.5.x), channel_id=1, source_target_pairs={{8,0},{0,8},{24,16},{16,24},{40,32},{32,40},{56,48},{48,56},{72,64... | collective-permute-start | bytes 2359304 | tf_op jit(solution)/shard_map/ppermute | solution.py:227
  87.0 29.1 %collective-permute-start.2 = (bf16[512,768]{1,0:T(8,128)(2,1)}, bf16[512,768]{1,0:T(8,128)(2,1)}, u32[]{:S(2)}, u32[]{:S(2)}) collective-permute-start(bf16[512,768]{1,0:T(8,128)(2,1)} %collective-permute-done.1.x), channel_id=1, source_target_pairs={{8,0},{0,8},{24,16},{16,24},{40,32},{32,40},{56,48},{48,56},{72,64... | collective-permute-start | bytes 2359304 | tf_op jit(solution)/shard_map/ppermute | solution.py:227
  88.2 32.9 %collective-permute-start = (bf16[512,768]{1,0:T(8,128)(2,1)}, bf16[512,768]{1,0:T(8,128)(2,1)}, u32[]{:S(2)}, u32[]{:S(2)}) collective-permute-start(bf16[512,768]{1,0:T(8,128)(2,1)} %bitcast.5.x), channel_id=1, source_target_pairs={{240,0},{24,8},{0,16},{40,24},{16,32},{56,40},{32,48},{72,56},{48,... | collective-permute-start | bytes 2359304 | tf_op jit(solution)/shard_map/ppermute | solution.py:227
  93.8 0.7 copy-start.16
  93.8 0.8 copy-start.15
  96.1 1.3 copy-start.4
  97.4 7.0 %copy-start.7 = (s32[2,4]{1,0:T(2,128)S(1)}, s32[2,4]{1,0:T(2,128)}, u32[]{:S(2)}) copy-start(s32[2,4]{1,0:T(2,128)} %near.7) | copy-start | bytes 100
  97.4 7.0 %copy-start.8 = (s32[2]{0:T(128)S(1)}, s32[2]{0:T(128)}, u32[]{:S(2)}) copy-start(s32[2]{0:T(128)} %live.7) | copy-start | bytes 28
  116.2 4.9 %copy-start.5 = (bf16[768,768]{1,0:T(8,128)(2,1)S(1)}, bf16[768,768]{1,0:T(8,128)(2,1)}, u32[]{:S(2)}) copy-start(bf16[768,768]{1,0:T(8,128)(2,1)} %wk.11) | copy-start | bytes 3538948
  116.2 4.9 %copy-start.6 = (bf16[1,512,768]{2,1,0:T(8,128)(2,1)S(1)}, bf16[1,512,768]{2,1,0:T(8,128)(2,1)}, u32[]{:S(2)}) copy-start(bf16[1,512,768]{2,1,0:T(8,128)(2,1)} %param.31) | copy-start | bytes 2359300
  128.8 0.9 copy-start.9
  151.6 4.4 %copy-start.10 = (bf16[768,512]{1,0:T(8,128)(2,1)S(1)}, bf16[768,512]{1,0:T(8,128)(2,1)}, u32[]{:S(2)}) copy-start(bf16[768,512]{1,0:T(8,128)(2,1)} %copy-done.9) | copy-start | bytes 2359300
  152.5 16.4 %all-to-all-start.3 = ((bf16[8,24,768]{2,1,0:T(8,128)(2,1)}), bf16[8,24,768]{2,1,0:T(8,128)(2,1)S(1)}, u32[]{:S(2)}, u32[]{:S(2)}) async-start(bf16[8,24,768]{2,1,0:T(8,128)(2,1)} %broadcast_in_dim.61), calls=%async_computation.3 | async-start | bytes 589824 | tf_op jit(solution)/shard_map/all_to_all | solution.py:293

commit v2 on v1

v2 whole, which is shorter than its diff:
```python
import functools

import jax
import jax.numpy as jnp
from jax import lax
from jax.experimental import pallas as pl
from jax.experimental.pallas import tpu as pltpu
from jax.sharding import PartitionSpec as P

H = 12
HD = 64
PATCH = 256
PAIRS = H // 2
GROUP = 16
LOG2E = 1.4426950408889634
epsilon = 1e-06
BF = jnp.bfloat16
F32 = jnp.float32
VMEM_BYTES = 24 * 1024 * 1024
MOST_VMEM = 63 * 1024 * 1024


def nn(a, b):
    return jnp.dot(a, b, preferred_element_type=F32)


def nt(a, b):
    return lax.dot_general(a, b, (((1,), (1,)), ((), ())), preferred_element_type=F32)


def normalize(values, gain):
    widened = values.astype(F32)
    mean_square = jnp.mean(widened * widened, axis=-1, keepdims=True)
    return (widened * lax.rsqrt(mean_square + epsilon) * gain).astype(BF)


def paired(two_heads):
    zero = jnp.zeros((HD, two_heads.shape[1]), BF)
    top = jnp.concatenate((two_heads[:HD], zero), axis=1)
    low = jnp.concatenate((zero, two_heads[HD:]), axis=1)
    return jnp.concatenate((top, low), axis=0)


def mixed(values, weights):
    ones = jnp.ones((16, values.shape[1]), BF)
    return nn(jnp.concatenate((values, ones), axis=0), weights)


def fetched(pairs, arrivals):
    copies = [pltpu.make_async_copy(a, b, arrivals.at[i]) for i, (a, b) in enumerate(pairs)]
    for copy in copies:
        copy.start()
    return copies


def turning_kernel(*refs):
    count = (len(refs) - 4) // 2
    ins, outs = refs[:count], refs[count : 2 * count]
    landed, turned, arrivals, sent = refs[2 * count :]
    copies = fetched([(ins[i], landed.at[i]) for i in range(count)], arrivals)
    stores = []
    for i in range(count):
        copies[i].wait()
        turned[i] = landed[i].T
        stores.append(pltpu.make_async_copy(turned.at[i], outs[i], sent.at[i]))
        stores[i].start()
    for store in stores:
        store.wait()


def vertical_kernel(
    x_in, wq_in, wk_in, wv_in, wo_in, gain, rows_of_bias, out, normed, q, k, v, mix, bias, x, wq, wk, wv, wo, arrivals
):
    levels, columns, features = x.shape
    copies = fetched([(x_in, x), (wq_in, wq), (wk_in, wk), (wv_in, wv), (wo_in, wo)], arrivals)
    tokens = levels * columns
    block = levels * GROUP
    key_column = lax.broadcasted_iota(jnp.int32, (GROUP, 2 * block), 0)
    query_column = lax.broadcasted_iota(jnp.int32, (GROUP, 2 * block), 1) % GROUP
    same = key_column == query_column
    for pair in range(PAIRS):
        for level in range(levels):
            row = rows_of_bias[pair * levels + level : pair * levels + level + 1]
            bias[pair, level * GROUP : (level + 1) * GROUP] = jnp.where(same, row, -jnp.inf)
    copies[0].wait()
    for level in range(levels):
        rows = normalize(x[level], gain[...])
        for part in range(columns // GROUP):
            place = part * block + level * GROUP
            normed[place : place + GROUP] = rows[part * GROUP : (part + 1) * GROUP]
    spans = [slice(start, start + 256) for start in range(0, tokens, 256)]
    copies[1].wait()
    for span in spans:
        q[:, span] = (nt(wq[...], normed[span]) * (HD**-0.5 * LOG2E)).astype(BF)
    copies[2].wait()
    for span in spans:
        k[span] = nn(normed[span], wk[...]).astype(BF)
    copies[3].wait()
    for span in spans:
        v[:, span] = nt(wv[...], normed[span]).astype(BF)
    steps = [(part, pair) for part in range(columns // GROUP) for pair in range(PAIRS)]

    def step_scores(part, pair):
        span, heads = slice(part * block, (part + 1) * block), slice(pair * 128, (pair + 1) * 128)
        return nn(k[span, heads], paired(q[heads, span])) + bias[pair]

    def step_weights(scores, part, pair):
        return jnp.exp2(scores - jnp.max(scores, axis=0, keepdims=True)).astype(BF)

    def step_mix(weights, part, pair):
        span = slice(part * block, (part + 1) * block)
        for half in range(2):
            head = slice(pair * 128 + half * HD, pair * 128 + half * HD + HD)
            total = mixed(v[head, span], weights[:, half * block : (half + 1) * block])
            mix[head, span] = (total[:HD] / total[HD : HD + 1]).astype(BF)

    staged(steps, step_scores, step_weights, step_mix)
    copies[4].wait()
    for part in range(columns // GROUP):
        span = slice(part * block, (part + 1) * block)
        projected = nn(mix[:, span].T, wo[...])
        for level in range(levels):
            place = slice(part * GROUP, (part + 1) * GROUP)
            out[level, place] = (
                x[level, place].astype(F32) + projected[level * GROUP : (level + 1) * GROUP]
            ).astype(BF)


def pair_scores(pair, own, start, barred, q, k):
    heads = slice(pair * 128, (pair + 1) * 128)
    mine = slice(own * PATCH, (own + 1) * PATCH)
    return nn(k[pl.ds(start, PATCH), heads], paired(q[heads, mine]))


def pair_weights(scores, pair, own, start, barred, column, pbias, new, old):
    row = slice(own * PAIRS + pair, own * PAIRS + pair + 1)
    lane = lax.broadcasted_iota(jnp.int32, (1, 2 * PATCH), 1)
    bias = jnp.where(lane < PATCH, pbias[2 * pair, column], pbias[2 * pair + 1, column]) * LOG2E + barred
    largest = jnp.max(scores, axis=0, keepdims=True) + bias
    fade = None
    if old is not None:
        before = old[1][row]
        largest = jnp.maximum(before, largest)
        fade = jnp.exp2(before - largest)
    new[1][row] = largest
    return jnp.exp2(scores - (largest - bias)).astype(BF), fade


def absorb(weights, fade, pair, own, start, barred, v, new, old):
    mine = slice(own * PATCH, (own + 1) * PATCH)
    row = slice(own * PAIRS + pair, own * PAIRS + pair + 1)
    sums = []
    for half in range(2):
        head = slice(pair * 128 + half * HD, pair * 128 + half * HD + HD)
        part = slice(half * PATCH, (half + 1) * PATCH)
        found = mixed(v[head, pl.ds(start, PATCH)], weights[:, part])
        sums.append(found[HD : HD + 1])
        if old is None:
            new[0][head, mine] = found[:HD]
        else:
            new[0][head, mine] = old[0][head, mine] * fade[:, part] + found[:HD]
    both = jnp.concatenate(sums, axis=1)
    new[2][row] = both if old is None else old[2][row] * fade + both


def staged(steps, first, second, third):
    one, two = {}, {}
    for index in range(len(steps) + 2):
        if index < len(steps):
            one[index] = first(*steps[index])
        if 0 <= index - 1 < len(steps):
            two[index - 1] = second(one.pop(index - 1), *steps[index - 1])
        if 0 <= index - 2:
            third(two.pop(index - 2), *steps[index - 2])


def attend(places, column, q, k, v, pbias, new, old):
    staged(
        [(pair, *place) for place in places for pair in range(PAIRS)],
        lambda *step: pair_scores(*step, q, k),
        lambda scores, *step: pair_weights(scores, *step, column, pbias, new, old),
        lambda found, *step: absorb(*found, *step, v, new, old),
    )


def keys_values(x, gain, wk, wv, k, v, wq=None, q=None):
    for start in range(0, x.shape[0], PATCH):
        span = slice(start, start + PATCH)
        piece = normalize(x[span], gain[...])
        if wq is not None:
            q[:, span] = (nt(wq[...], piece) * (HD**-0.5 * LOG2E)).astype(BF)
        v[:, span] = nt(wv[...], piece).astype(BF)
        k[span] = nn(piece, wk[...]).astype(BF)


def own_kernel(pbias, x, wq_in, wk_in, wv_in, gain, q, acc, top, total, wk, wv, k, v, wq, arrivals):
    for copy in fetched([(wq_in, wq), (wk_in, wk), (wv_in, wv)], arrivals):
        copy.wait()
    keys_values(x, gain, wk, wv, k, v, wq, q)
    attend([(0, 0, 0.0), (1, PATCH, 0.0)], 0, q, k, v, pbias, (acc, top, total), None)


def arrived_part(source, near, live, pbias, x, gain, wk, wv, q, acc_in, top_in, total_in, acc, top, total, k, v):
    keys_values(x, gain, wk, wv, k, v)
    places = []
    for own in range(2):
        found = jnp.int32(-1)
        for entry in range(near.shape[1]):
            listed = near[own, entry]
            hit = jnp.logical_and(entry < live[own], lax.shift_right_arithmetic(listed, 1) == source[0])
            found = jnp.where(hit, jnp.bitwise_and(listed, 1), found)
        barred = jnp.where(found >= 0, 0.0, -jnp.inf)
        places.append((own, pl.multiple_of(jnp.maximum(found, 0) * PATCH, PATCH), barred))
    attend(places, 1, q, k, v, pbias, (acc, top, total), (acc_in, top_in, total_in))


def arrived_kernel(source, near, live, pbias, x, gain, wk, wv, q, acc_in, top_in, total_in, acc, top, total, k, v):
    arrived_part(source, near, live, pbias, x, gain, wk, wv, q, acc_in, top_in, total_in, acc, top, total, k, v)


def last_kernel(
    source, near, live, pbias, x, gain, wk, wv, q, acc_in, top_in, total_in, cot_in, mix_out, grad, acc, top, total, k, v,
    mix, cot, sent
):
    fetch = pltpu.make_async_copy(cot_in, cot, sent.at[0])
    fetch.start()
    arrived_part(source, near, live, pbias, x, gain, wk, wv, q, acc_in, top_in, total_in, acc, top, total, k, v)
    for pair in range(PAIRS):
        heads = slice(pair * 128, (pair + 1) * 128)
        for own in range(2):
            mine = slice(own * PATCH, (own + 1) * PATCH)
            inverse = 1.0 / total[own * PAIRS + pair : own * PAIRS + pair + 1]
            for half in range(2):
                head = slice(pair * 128 + half * HD, pair * 128 + half * HD + HD)
                mix[head, mine] = (
                    acc[head, mine] * inverse[:, half * PATCH : (half + 1) * PATCH]
                ).astype(BF)
        if pair == 0:
            fetch.wait()
        grad[heads] = nn(mix[heads], cot[...]).astype(BF)
    store = pltpu.make_async_copy(mix, mix_out, sent.at[1])
    store.start()
    store.wait()


IN_VMEM = pl.BlockSpec(memory_space=pltpu.VMEM)
IN_SMEM = pl.BlockSpec(memory_space=pltpu.SMEM)
IN_HBM = pl.BlockSpec(memory_space=pltpu.HBM)


def turned(*arrays):
    shape = arrays[0].shape
    several = (len(arrays), *shape)
    return pl.pallas_call(
        turning_kernel,
        out_shape=[jax.ShapeDtypeStruct(shape, BF)] * len(arrays),
        in_specs=[IN_HBM] * len(arrays),
        out_specs=[IN_HBM] * len(arrays),
        scratch_shapes=[
            pltpu.VMEM(several, BF),
            pltpu.VMEM(several, BF),
            pltpu.SemaphoreType.DMA((len(arrays),)),
            pltpu.SemaphoreType.DMA((len(arrays),)),
        ],
        compiler_params=pltpu.CompilerParams(vmem_limit_bytes=MOST_VMEM),
        cost_estimate=pl.CostEstimate(flops=0, bytes_accessed=20 * 2**20, transcendentals=0),
        name="turned",
    )(*arrays)


def call(kernel, scalars, arrays, outs, scratch, flops, name, loose_in=(), loose_out=(), vmem=VMEM_BYTES):
    shapes = [jax.ShapeDtypeStruct(shape, kind) for shape, kind in outs]
    moved = sum(a.size * a.dtype.itemsize for a in arrays)
    return pl.pallas_call(
        kernel,
        out_shape=shapes,
        in_specs=[IN_SMEM] * len(scalars) + [IN_HBM if i in loose_in else IN_VMEM for i in range(len(arrays))],
        out_specs=[IN_HBM if i in loose_out else IN_VMEM for i in range(len(outs))],
        scratch_shapes=[pltpu.VMEM(*s) if isinstance(s, tuple) else s for s in scratch],
        compiler_params=pltpu.CompilerParams(vmem_limit_bytes=vmem),
        cost_estimate=pl.CostEstimate(flops=flops, bytes_accessed=moved, transcendentals=0),
        name=name,
    )(*scalars, *arrays)


def expanded_bias(level_bias):
    levels = level_bias.shape[1]
    table = (level_bias * LOG2E).reshape(PAIRS, 2, levels, levels).transpose(0, 3, 1, 2)
    return jnp.repeat(table.reshape(PAIRS * levels, 2 * levels), GROUP, axis=1)


def sizes(columns, features):
    weights = ((features, features), BF)
    turned_tokens = ((features, columns), BF)
    state = [((features, columns), F32), ((2 * PAIRS, 2 * PATCH), F32), ((2 * PAIRS, 2 * PATCH), F32)]
    return weights, turned_tokens, ((columns, features), BF), state, columns * features * features


def run_vertical(x, wq, wk, wv, wo, gain, rows_of_bias):
    levels, share, features = x.shape
    weights, wide, tall, _, work = sizes(levels * share, features)
    return call(
        vertical_kernel,
        [],
        [x, wq, wk, wv, wo, gain, rows_of_bias],
        [(x.shape, BF)],
        [
            tall,
            wide,
            tall,
            wide,
            wide,
            ((PAIRS, levels * GROUP, 2 * levels * GROUP), F32),
            (x.shape, BF),
            *([weights] * 4),
            pltpu.SemaphoreType.DMA((5,)),
        ],
        10 * work,
        "vertical",
        loose_in=range(5),
        vmem=MOST_VMEM,
    )[0]


def run_own(pbias, hidden, wq, wk, wv, gain):
    weights, wide, tall, state, work = sizes(*hidden.shape)
    return call(
        own_kernel,
        [pbias],
        [hidden, wq, wk, wv, gain],
        [wide, *state, weights, weights],
        [tall, wide, weights, pltpu.SemaphoreType.DMA((3,))],
        8 * work,
        "own",
        loose_in=(1, 2, 3),
    )


def run_arrived(at, fixed, block, gain, wk, wv, q, state):
    _, wide, tall, kept, work = sizes(*block.shape)
    return call(
        arrived_kernel,
        [at[None], *fixed],
        [block, gain, wk, wv, q, *state],
        kept,
        [tall, wide],
        6 * work,
        "arrived",
    )


def run_last(at, fixed, block, gain, wk, wv, q, state, cotangent):
    weights, wide, tall, kept, work = sizes(*block.shape)
    return call(
        last_kernel,
        [at[None], *fixed],
        [block, gain, wk, wv, q, *state, cotangent],
        [wide, weights],
        [*kept, tall, wide, wide, tall, pltpu.SemaphoreType.DMA((2,))],
        8 * work,
        "last",
        loose_in=(8,),
        loose_out=(0,),
    )


def body(
    fields,
    norm_vert,
    query_vert,
    keys_vert,
    values_vert,
    out_vert,
    level_bias,
    norm_patch,
    query_patch,
    keys_patch,
    values_patch,
    out_patch,
    patch_bias,
    neighbours,
    counts,
    cotangent,
):
    _, columns, features = fields.shape
    levels = lax.axis_size("level")
    devices = lax.axis_size("space")
    place = lax.axis_index("space")
    share = columns // levels

    def moved(value, source_of):
        return lax.ppermute(value, "space", [(source_of(d) % devices, d) for d in range(devices)])

    wq_v, wv_v, wq_p, wv_p = turned(query_vert, values_vert, query_patch, values_patch)
    x = lax.all_to_all(fields.reshape(levels, share, features), "level", 0, 0, tiled=True)
    hidden = run_vertical(x, wq_v, keys_vert, wv_v, out_vert, norm_vert[None], expanded_bias(level_bias))
    hidden = lax.all_to_all(hidden, "level", 0, 0, tiled=True).reshape(columns, features)

    def outer(d):
        return d + 2 if d % 2 == 0 else d - 2

    def inner(d):
        return d - 2 if d % 2 == 0 else d + 2

    def twin(d):
        return d ^ 1

    from_outer = moved(hidden, outer)
    from_twin = moved(hidden, twin)
    from_inner = moved(hidden, inner)
    side = 1 - 2 * (place % 2)
    outer_at = (place + 2 * side) % devices
    inner_at = (place - 2 * side) % devices
    twin_at = place + side
    passed_at = (place - side) % devices
    gain = norm_patch[None]
    q, *state, wk, wv = run_own(patch_bias, hidden, wq_p, keys_patch, wv_p, gain)
    fixed = [neighbours, counts, patch_bias]
    state = run_arrived(twin_at, fixed, from_twin, gain, wk, wv, q, state)
    from_outer, *state = lax.optimization_barrier((from_outer, *state))
    passed_on = moved(from_outer, twin)
    state = run_arrived(outer_at, fixed, from_outer, gain, wk, wv, q, state)
    state = run_arrived(passed_at, fixed, passed_on, gain, wk, wv, q, state)
    mix, grad = run_last(
        inner_at, fixed, from_inner, gain, wk, wv, q, state, cotangent.reshape(columns, features)
    )
    pieces = lax.all_to_all(grad.reshape(devices, features // devices, features), "space", 0, 0, tiled=True)
    shares = pieces.astype(F32).sum(axis=0).astype(BF)
    spread = jnp.broadcast_to(shares[None], (levels, *shares.shape))
    grad_wo = lax.all_to_all(spread, "level", 0, 0, tiled=True).astype(F32).sum(axis=0)
    projected = lax.dot_general(mix, out_patch, (((0,), (0,)), ((), ())), preferred_element_type=F32)
    out_fields = (hidden.astype(F32) + projected).astype(BF)
    return (out_fields[None], grad_wo)


def solution(mesh):
    return jax.shard_map(
        body,
        mesh=mesh,
        in_specs=(
            P("level", "space", None),
            *([P()] * 12),
            P("space", None),
            P("space"),
            P("level", "space", None),
        ),
        out_specs=(P("level", "space", None), P("space", None)),
        check_vma=False,
    )
```

time: 172 us -> 151 us (0.88)
  Pallas kernels: 40 us -> 34.1 us
  local copies, waits for them, and re-layouts: 17.1 us -> 12.1 us
  starting transfers between devices: 25.2 us -> 20.6 us
  other arithmetic: 4 us -> 0.85 us
  waiting for transfers between devices: 31 us -> 28.2 us
  blocking collectives: 48.5 us -> 50.4 us
    pallas_call x6, Pallas kernels: 40 us -> 30.3 us  [call(): pl.pallas_call(kernel, out_shape=shapes, in_specs=[IN_SMEM] * len(scalars...]
    ppermute x4, waiting for transfers between devices: 8.65 us -> 0.01 us  [moved(): lax.ppermute(value, 'space', [(source_of(d) % devices, d) for d in range(...]
    all_to_all x1, waiting for transfers between devices: 12.2 us -> 18.2 us  [body(): lax.all_to_all(fields.reshape(levels, share, features), 'level', 0, 0, ti...]
    select_n x1 -> x0, local copies, waits for them, and re-layouts: 5.7 us -> none  [expanded_bias(): jnp.where(same, table.reshape(PAIRS * levels, 1, 2 * levels, 1), -jnp.inf)]
    ppermute x4, starting transfers between devices: 12.6 us -> 8 us  [moved(): lax.ppermute(value, 'space', [(source_of(d) % devices, d) for d in range(...]
    pallas_call x0 -> x1, Pallas kernels: none -> 3.85 us  [turned(): pl.pallas_call(turning_kernel, out_shape=[jax.ShapeDtypeStruct(shape, BF)...]
    select_n x1 -> x0, other arithmetic: 3.14 us -> none  [expanded_bias(): jnp.where(same, table.reshape(PAIRS * levels, 1, 2 * levels, 1), -jnp.inf)]
    unnamed x40 -> x42, local copies, waits for them, and re-layouts: 10.5 us -> 9.93 us
  transfers between devices with their start and end apart: 6 -> 6, of which waited for: 3 -> 2; matrix products, arithmetic and copies ran while one was open for 10% -> 3% of each run, Pallas kernels for 14% -> 14%
where the time goes in v2:
time: 151 us; the launch traced here: 150 us
  blocking collectives  50.4 us (33%)
  Pallas kernels  34.1 us (23%)
  waiting for transfers between devices  28.2 us (19%)
  starting transfers between devices  20.6 us (14%)
  local copies, waits for them, and re-layouts  12.1 us (8%)
  matrix products  2.97 us (2%)
    pallas_call x6, Pallas kernels, call(): pl.pallas_call(kernel, out_shape=shapes, in_specs=[IN_SMEM] * len(scalars...  30.3 us
    all_to_all x1, blocking collectives, body(): lax.all_to_all(hidden, 'level', 0, 0, tiled=True).reshape(columns, features)  26.8 us
    all_to_all x1, blocking collectives, body(): lax.all_to_all(grad.reshape(devices, features // devices, features), 'spa...  23.6 us
    all_to_all x1, waiting for transfers between devices, body(): lax.all_to_all(fields.reshape(levels, share, features), 'level', 0, 0, ti...  18.2 us
    all_to_all x1, waiting for transfers between devices, body(): lax.all_to_all(spread, 'level', 0, 0, tiled=True).astype(F32).sum(axis=0)  10 us
    unnamed x42, local copies, waits for them, and re-layouts  9.93 us
    all_to_all x1, starting transfers between devices, body(): lax.all_to_all(fields.reshape(levels, share, features), 'level', 0, 0, ti...  9.16 us
    ppermute x4, starting transfers between devices, moved(): lax.ppermute(value, 'space', [(source_of(d) % devices, d) for d in range(...  8 us
  transfers between devices with their start and end apart: 6, of which 2 were waited for; matrix products, arithmetic and copies ran while one was open for 3% of the time, Pallas kernels for 14%

profile of v2, /device:TPU:1, one launch (start us, length us, event | category | flops | bytes accessed | tf_op | source)
XLA Modules:
  0.0 150.1 jit_solution(13739758019701459677)
XLA Ops:
  0.6 9.2 %all-to-all-start = ((bf16[8,64,768]{2,1,0:T(8,128)(2,1)}), bf16[8,64,768]{2,1,0:T(8,128)(2,1)S(1)}, u32[]{:S(2)}, u32[]{:S(2)}) async-start(bf16[8,64,768]{2,1,0:T(8,128)(2,1)} %bitcast.25), calls=%async_computation | async-start | bytes 1572864 | tf_op jit(solution)/shard_map/all_to_all | solution.py:395
  11.3 3.9 %turned.1 = (bf16[768,768]{1,0:T(8,128)(2,1)}, bf16[768,768]{1,0:T(8,128)(2,1)}, bf16[768,768]{1,0:T(8,128)(2,1)}, bf16[768,768]{1,0:T(8,128)(2,1)}) custom-call(bf16[768,768]{1,0:T(8,128)(2,1)} %refs_0_.1, bf16[768,768]{1,0:T(8,128)(2,1)} %refs_1_.1, bf16[768,768]{1,0:T(8,128)(2,1)} %refs_2_.1, bf16[768,768]{1,0:T(8,128)(2,1)} %refs_3_.1), custom_call_target="tpu_custom_call" | custom-call | bytes 20971520 | tf_op jit(solution)/shard_map/turned/pallas_call | solution.py:254
  15.2 18.2 %all-to-all-done.x_in = bf16[8,64,768]{2,1,0:T(8,128)(2,1)S(1)} async-done(((bf16[8,64,768]{2,1,0:T(8,128)(2,1)}), bf16[8,64,768]{2,1,0:T(8,128)(2,1)S(1)}, u32[]{:S(2)}, u32[]{:S(2)}) %all-to-all-start) | async-done | bytes 786464 | tf_op jit(solution)/shard_map/all_to_all | solution.py:395
  34.3 8.4 %vertical.1 = bf16[8,64,768]{2,1,0:T(8,128)(2,1)} custom-call(bf16[8,64,768]{2,1,0:T(8,128)(2,1)} %copy-done.15, bf16[768,768]{1,0:T(8,128)(2,1)} %get-tuple-element.27.wq_in, bf16[768,768]{1,0:T(8,128)(2,1)} %wk_in.2, bf16[768,768]{1,0:T(8,128)(2,1)} %get-tuple-element.28.wv_in, bf16[768,768]{1,0:T(8,128)(2,1)} %wo_in.1, f32[1,768]{1,0:T(1,128)} %broadcast_in_dim.30.gain, ...), custom_call_target="tpu_custom_call" | custom-call | flops 3019898880 | bytes 5557248 | tf_op jit(solution)/shard_map/vertical/pallas_call | solution.py:274
  42.7 26.8 %all_to_all.20 = bf16[8,64,768]{2,1,0:T(8,128)(2,1)S(1)} all-to-all(bf16[8,64,768]{2,1,0:T(8,128)(2,1)} %vertical.1), channel_id=1, replica_groups=mesh['space'=32,'level'=8] {'level'}, dimensions={0} | all-to-all | bytes 1572864 | tf_op jit(solution)/shard_map/all_to_all | solution.py:397
  70.4 1.3 collective-permute-start.1
  71.8 1.3 copy-done.1
  73.0 1.3 copy-done.2
  74.3 5.2 %own.1 = (bf16[768,512]{1,0:T(8,128)(2,1)S(1)}, f32[768,512]{1,0:T(8,128)S(1)}, f32[12,512]{1,0:T(8,128)S(1)}, f32[12,512]{1,0:T(8,128)S(1)}, bf16[768,768]{1,0:...) custom-call(f32[12,2]{1,0:T(8,128)S(1)} %copy.38.pbias, bf16[512,768]{1,0:T(8,128)(2,1)S(1)} %bitcast.21, ...), custom_call_target="tpu_custom_call" | custom-call | flops 2415919104 | bytes 4328448 | tf_op jit(solution)/shard_map/own/pallas_call | solution.py:274
  79.6 4.0 %arrived.3 = (f32[768,512]{1,0:T(8,128)S(1)}, f32[12,512]{1,0:T(8,128)S(1)}, f32[12,512]{1,0:T(8,128)S(1)}) custom-call(s32[1]{0:T(128)} %bitcast.7.source, s32[2,4]{1,0:T(2,128)S(1)} %copy-done.4, s32[2]{0:T(128)S(1)} %copy-done.5, f32[12,2]{1,0:T(8,128)S(1)} %copy.38.pbias, bf16[512,768]{1,0:T(8,128)(2,1)S(1)} %collective-permute-done.2.x, ...), custom_call_target="tpu_custom_call" | custom-call | flops 1811939328 | bytes 5557248 | tf_op jit(solution)/shard_map/arrived/pallas_call | solution.py:274
  83.6 1.2 copy-done.7
  84.7 3.9 %collective-permute-start.3 = (bf16[512,768]{1,0:T(8,128)(2,1)S(1)}, bf16[512,768]{1,0:T(8,128)(2,1)S(1)}, u32[]{:S(2)}, u32[]{:S(2)}) collective-permute-start(bf16[512,768]{1,0:T(8,128)(2,1)S(1)} %collective-permute-done.1.x), channel_id=1, source_target_pairs={{8,0},{0,8},{24,16},{16,24},{40,32},{32,40},{56,48},{48,56},{72,64... | collective-permute-start | bytes 2359304 | tf_op jit(solution)/shard_map/ppermute | solution.py:392
  88.7 2.0 %collective-permute-start = (bf16[512,768]{1,0:T(8,128)(2,1)S(1)}, bf16[512,768]{1,0:T(8,128)(2,1)S(1)}, u32[]{:S(2)}, u32[]{:S(2)}) collective-permute-start(bf16[512,768]{1,0:T(8,128)(2,1)S(1)} %bitcast.22), channel_id=1, source_target_pairs={{240,0},{24,8},{0,16},{40,24},{16,32},{56,40},{32,48},{72,56},{48,... | collective-permute-start | bytes 2359304 | tf_op jit(solution)/shard_map/ppermute | solution.py:392
  90.6 1.4 copy-done.8
  92.0 1.3 copy-done.10
  93.3 1.3 copy-done.12
  94.6 1.1 copy-done.14
  95.7 4.0 %arrived.4 = (f32[768,512]{1,0:T(8,128)S(1)}, f32[12,512]{1,0:T(8,128)S(1)}, f32[12,512]{1,0:T(8,128)S(1)}) custom-call(s32[1]{0:T(128)} %bitcast.8.source, s32[2,4]{1,0:T(2,128)S(1)} %copy-done.4, s32[2]{0:T(128)S(1)} %copy-done.6, f32[12,2]{1,0:T(8,128)S(1)} %copy.38.pbias, bf16[512,768]{1,0:T(8,128)(2,1)S(1)} %collective-permute-done.1.x, ...), custom_call_target="tpu_custom_call" | custom-call | flops 1811939328 | bytes 5557248 | tf_op jit(solution)/shard_map/arrived/pallas_call | solution.py:274
  99.7 3.9 %arrived.5 = (f32[768,512]{1,0:T(8,128)S(1)}, f32[12,512]{1,0:T(8,128)S(1)}, f32[12,512]{1,0:T(8,128)S(1)}) custom-call(s32[1]{0:T(128)} %bitcast.6.source, s32[2,4]{1,0:T(2,128)S(1)} %copy-done.4, s32[2]{0:T(128)S(1)} %copy-done.6, f32[12,2]{1,0:T(8,128)S(1)} %copy.38.pbias, bf16[512,768]{1,0:T(8,128)(2,1)S(1)} %collective-permute-done.3.x, ...), custom_call_target="tpu_custom_call" | custom-call | flops 1811939328 | bytes 5557248 | tf_op jit(solution)/shard_map/arrived/pallas_call | solution.py:274
  103.6 4.9 %last.1 = (bf16[768,512]{1,0:T(8,128)(2,1)S(1)}, bf16[768,768]{1,0:T(8,128)(2,1)S(1)}) custom-call(s32[1]{0:T(128)} %bitcast.5.source, s32[2,4]{1,0:T(2,128)S(1)} %copy-done.4, s32[2]{0:T(128)S(1)} %copy-done.6, f32[12,2]{1,0:T(8,128)S(1)} %copy.38.pbias, bf16[512,768]{1,0:T(8,128)(2,1)S(1)} %collective-permute-done.x, f32[1,768]{1,0:T(1,128)S(1)} %broadcast_in_dim.33.gain, ...), custom_call_target="tpu_custom_call" | custom-call | flops 2415919104 | bytes 6343680 | tf_op jit(solution)/shard_map/last/pallas_call | solution.py:274
  108.5 23.6 %all_to_all.21 = bf16[32,24,768]{2,1,0:T(8,128)(2,1)S(1)} all-to-all(bf16[32,24,768]{2,1,0:T(8,128)(2,1)S(1)} %bitcast.18), channel_id=1, replica_groups=mesh['space'=32,'level'=8] {'space'}, dimensions={0} | all-to-all | bytes 2359296 | tf_op jit(solution)/shard_map/all_to_all | solution.py:427
  133.0 3.4 %all-to-all-start.3 = ((bf16[8,24,768]{2,1,0:T(8,128)(2,1)}), bf16[8,24,768]{2,1,0:T(8,128)(2,1)S(1)}, u32[]{:S(2)}, u32[]{:S(2)}) async-start(bf16[8,24,768]{2,1,0:T(8,128)(2,1)} %broadcast_in_dim.38), calls=%async_computation.3 | async-start | bytes 589824 | tf_op jit(solution)/shard_map/all_to_all | solution.py:430
  136.4 3.0 %fusion = bf16[1,512,768]{2,1,0:T(8,128)(2,1)} fusion(bf16[768,512]{1,0:T(8,128)(2,1)S(1)} %get-tuple-element.50, bf16[768,768]{1,0:T(8,128)(2,1)} %param.27, bf16[512,768]{1,0:T(8,128)(2,1)S(1)} %bitcast.23), kind=kOutput, calls=%fused_computation.1 | convolution fusion | flops 605159424 | bytes 3538944 | tf_op jit(solution)/shard_map/dot_general | solution.py:431
  139.4 10.0 %all-to-all-done.3 = bf16[8,24,768]{2,1,0:T(8,128)(2,1)S(1)} async-done(((bf16[8,24,768]{2,1,0:T(8,128)(2,1)}), bf16[8,24,768]{2,1,0:T(8,128)(2,1)S(1)}, u32[]{:S(2)}, u32[]{:S(2)}) %all-to-all-start.3) | async-done | bytes 294944 | tf_op jit(solution)/shard_map/all_to_all | solution.py:430
  (50 shorter events, 5.0 us)
Async XLA Ops:
  0.6 9.2 %copy-start.16 = (f32[12,8,8]{0,2,1:T(8,128)S(1)}, f32[12,8,8]{0,2,1:T(8,128)}, u32[]{:S(2)}) copy-start(f32[12,8,8]{0,2,1:T(8,128)} %param.22) | copy-start | bytes 9220
  0.6 10.1 %copy-start.17 = (f32[768]{0:T(1024)S(1)}, f32[768]{0:T(1024)}, u32[]{:S(2)}) copy-start(f32[768]{0:T(1024)} %param.17) | copy-start | bytes 9220
  0.6 32.7 %all-to-all-start = ((bf16[8,64,768]{2,1,0:T(8,128)(2,1)}), bf16[8,64,768]{2,1,0:T(8,128)(2,1)S(1)}, u32[]{:S(2)}, u32[]{:S(2)}) async-start(bf16[8,64,768]{2,1,0:T(8,128)(2,1)} %bitcast.25), calls=%async_computation | async-start | bytes 1572864 | tf_op jit(solution)/shard_map/all_to_all | solution.py:395
  42.7 29.0 %copy-start.19 = (f32[12,2]{0,1:T(2,128)S(1)}, f32[12,2]{0,1:T(2,128)}, u32[]{:S(2)}) copy-start(f32[12,2]{0,1:T(2,128)} %param.28) | copy-start | bytes 292
  42.7 29.1 %copy-start.18 = (f32[768]{0:T(1024)S(1)}, f32[768]{0:T(1024)}, u32[]{:S(2)}) copy-start(f32[768]{0:T(1024)} %param.23) | copy-start | bytes 9220
  42.7 29.1 %copy-start = (bf16[768,768]{1,0:T(8,128)(2,1)S(1)}, bf16[768,768]{1,0:T(8,128)(2,1)}, u32[]{:S(2)}) copy-start(bf16[768,768]{1,0:T(8,128)(2,1)} %wk_in.3) | copy-start | bytes 3538948
  69.5 10.0 %collective-permute-start.2 = (bf16[512,768]{1,0:T(8,128)(2,1)S(1)}, bf16[512,768]{1,0:T(8,128)(2,1)S(1)}, u32[]{:S(2)}, u32[]{:S(2)}) collective-permute-start(bf16[512,768]{1,0:T(8,128)(2,1)S(1)} %bitcast.19), channel_id=1, source_target_pairs={{8,0},{0,8},{24,16},{16,24},{40,32},{32,40},{56,48},{48,56},{72,64... | collective-permute-start | bytes 2359304 | tf_op jit(solution)/shard_map/ppermute | solution.py:392
  70.4 14.4 %collective-permute-start.1 = (bf16[512,768]{1,0:T(8,128)(2,1)S(1)}, bf16[512,768]{1,0:T(8,128)(2,1)S(1)}, u32[]{:S(2)}, u32[]{:S(2)}) collective-permute-start(bf16[512,768]{1,0:T(8,128)(2,1)S(1)} %bitcast.20), channel_id=1, source_target_pairs={{16,0},{248,8},{32,16},{8,24},{48,32},{24,40},{64,48},{40,56},{80,... | collective-permute-start | bytes 2359304 | tf_op jit(solution)/shard_map/ppermute | solution.py:392
  71.8 1.3 copy-start.1
  73.0 1.3 copy-start.2
  74.3 5.2 %copy-start.4 = (s32[2,4]{1,0:T(2,128)S(1)}, s32[2,4]{1,0:T(2,128)}, u32[]{:S(2)}) copy-start(s32[2,4]{1,0:T(2,128)} %near.7) | copy-start | bytes 100
  74.3 5.2 %copy-start.5 = (s32[2]{0:T(128)S(1)}, s32[2]{0:T(128)}, u32[]{:S(2)}) copy-start(s32[2]{0:T(128)} %live.7) | copy-start | bytes 28
  79.5 4.1 %copy-start.9 = (bf16[768,768]{1,0:T(8,128)(2,1)}, bf16[768,768]{1,0:T(8,128)(2,1)S(1)}, u32[]{:S(2)}) copy-start(bf16[768,768]{1,0:T(8,128)(2,1)S(1)} %get-tuple-element.31.wk) | copy-start | bytes 3538948
  79.5 4.1 %copy-start.11 = (bf16[768,768]{1,0:T(8,128)(2,1)}, bf16[768,768]{1,0:T(8,128)(2,1)S(1)}, u32[]{:S(2)}) copy-start(bf16[768,768]{1,0:T(8,128)(2,1)S(1)} %get-tuple-element.32.wv) | copy-start | bytes 3538948
  79.5 4.1 %copy-start.13 = (bf16[768,512]{1,0:T(8,128)(2,1)}, bf16[768,512]{1,0:T(8,128)(2,1)S(1)}, u32[]{:S(2)}) copy-start(bf16[768,512]{1,0:T(8,128)(2,1)S(1)} %get-tuple-element.33.q) | copy-start | bytes 2359300
  79.5 11.1 %copy-start.6 = (s32[2]{0:T(128)S(1)}, s32[2]{0:T(128)}, u32[]{:S(2)}) copy-start(s32[2]{0:T(128)} %live.7) | copy-start | bytes 28
  83.6 1.2 copy-start.7
  84.7 14.9 %collective-permute-start.3 = (bf16[512,768]{1,0:T(8,128)(2,1)S(1)}, bf16[512,768]{1,0:T(8,128)(2,1)S(1)}, u32[]{:S(2)}, u32[]{:S(2)}) collective-permute-start(bf16[512,768]{1,0:T(8,128)(2,1)S(1)} %collective-permute-done.1.x), channel_id=1, source_target_pairs={{8,0},{0,8},{24,16},{16,24},{40,32},{32,40},{56,48},{48,56},{72,64... | collective-permute-start | bytes 2359304 | tf_op jit(solution)/shard_map/ppermute | solution.py:392
  88.7 14.9 %collective-permute-start = (bf16[512,768]{1,0:T(8,128)(2,1)S(1)}, bf16[512,768]{1,0:T(8,128)(2,1)S(1)}, u32[]{:S(2)}, u32[]{:S(2)}) collective-permute-start(bf16[512,768]{1,0:T(8,128)(2,1)S(1)} %bitcast.22), channel_id=1, source_target_pairs={{240,0},{24,8},{0,16},{40,24},{16,32},{56,40},{32,48},{72,56},{48,... | collective-permute-start | bytes 2359304 | tf_op jit(solution)/shard_map/ppermute | solution.py:392
  90.6 1.4 copy-start.8
  92.0 1.3 copy-start.10
  93.3 1.3 copy-start.12
  99.7 3.9 %copy-start.3 = (bf16[1,512,768]{2,1,0:T(8,128)(2,1)S(1)}, bf16[1,512,768]{2,1,0:T(8,128)(2,1)}, u32[]{:S(2)}) copy-start(bf16[1,512,768]{2,1,0:T(8,128)(2,1)} %param.31) | copy-start | bytes 2359300
  133.0 16.4 %all-to-all-start.3 = ((bf16[8,24,768]{2,1,0:T(8,128)(2,1)}), bf16[8,24,768]{2,1,0:T(8,128)(2,1)S(1)}, u32[]{:S(2)}, u32[]{:S(2)}) async-start(bf16[8,24,768]{2,1,0:T(8,128)(2,1)} %broadcast_in_dim.38), calls=%async_computation.3 | async-start | bytes 589824 | tf_op jit(solution)/shard_map/all_to_all | solution.py:430
  (2 other events, 2.0 us)

commit v3 on v2

--- a/solution.py
+++ b/solution.py
@@ -193,11 +193,13 @@
         k[span] = nn(piece, wk[...]).astype(BF)
 
 
-def own_kernel(pbias, x, wq_in, wk_in, wv_in, gain, q, acc, top, total, wk, wv, k, v, wq, arrivals):
-    for copy in fetched([(wq_in, wq), (wk_in, wk), (wv_in, wv)], arrivals):
+def own_kernel(pbias, x, wq_in, wk_in, wv_in, gain, q, acc, top, total, wk, wv, again, k, v, wq, arrivals):
+    *loads, store = fetched([(wq_in, wq), (wk_in, wk), (wv_in, wv), (x, again)], arrivals)
+    for copy in loads:
         copy.wait()
     keys_values(x, gain, wk, wv, k, v, wq, q)
     attend([(0, 0, 0.0), (1, PATCH, 0.0)], 0, q, k, v, pbias, (acc, top, total), None)
+    store.wait()
 
 
 def arrived_part(source, near, live, pbias, x, gain, wk, wv, q, acc_in, top_in, total_in, acc, top, total, k, v):
@@ -214,19 +216,20 @@
     attend(places, 1, q, k, v, pbias, (acc, top, total), (acc_in, top_in, total_in))
 
 
-def arrived_kernel(source, near, live, pbias, x, gain, wk, wv, q, acc_in, top_in, total_in, acc, top, total, k, v):
+def arrived_kernel(source, near, live, pbias, x, gain, wk, wv, q, acc_in, top_in, total_in, after, *rest):
+    acc, top, total, mark, k, v = rest
     arrived_part(source, near, live, pbias, x, gain, wk, wv, q, acc_in, top_in, total_in, acc, top, total, k, v)
+    mark[...] = total[:8, :128]
 
 
 def last_kernel(
-    source, near, live, pbias, x, gain, wk, wv, q, acc_in, top_in, total_in, cot_in, mix_out, grad, acc, top, total, k, v,
-    mix, cot, sent
+    source, core, near, live, pbias, x, gain, wk, wv, q, acc_in, top_in, total_in, cot_in, mix_out, keep, give,
+    acc, top, total, k, v, mix, cot, sent
 ):
     fetch = pltpu.make_async_copy(cot_in, cot, sent.at[0])
     fetch.start()
     arrived_part(source, near, live, pbias, x, gain, wk, wv, q, acc_in, top_in, total_in, acc, top, total, k, v)
     for pair in range(PAIRS):
-        heads = slice(pair * 128, (pair + 1) * 128)
         for own in range(2):
             mine = slice(own * PATCH, (own + 1) * PATCH)
             inverse = 1.0 / total[own * PAIRS + pair : own * PAIRS + pair + 1]
@@ -235,17 +238,29 @@
                 mix[head, mine] = (
                     acc[head, mine] * inverse[:, half * PATCH : (half + 1) * PATCH]
                 ).astype(BF)
-        if pair == 0:
-            fetch.wait()
-        grad[heads] = nn(mix[heads], cot[...]).astype(BF)
     store = pltpu.make_async_copy(mix, mix_out, sent.at[1])
     store.start()
+    fetch.wait()
+    chips, rows, _ = keep.shape
+    even = core[0] == 0
+    for first in range(0, chips, 8):
+        span = slice(first * 2 * rows, (first + 8) * 2 * rows)
+        grad = nn(mix[span], cot[...])
+        for chip in range(8):
+            at = chip * 2 * rows
+            to_even, to_odd = grad[at : at + rows], grad[at + rows : at + 2 * rows]
+            keep[first + chip] = jnp.where(even, to_even, to_odd)
+            give[first + chip] = jnp.where(even, to_odd, to_even).astype(BF)
     store.wait()
 
 
 IN_VMEM = pl.BlockSpec(memory_space=pltpu.VMEM)
 IN_SMEM = pl.BlockSpec(memory_space=pltpu.SMEM)
 IN_HBM = pl.BlockSpec(memory_space=pltpu.HBM)
+
+
+def kept_in_hbm(*arrays):
+    return [pltpu.with_memory_space_constraint(array, pltpu.HBM) for array in arrays]
 
 
 def turned(*arrays):
@@ -287,6 +302,9 @@
     levels = level_bias.shape[1]
     table = (level_bias * LOG2E).reshape(PAIRS, 2, levels, levels).transpose(0, 3, 1, 2)
     return jnp.repeat(table.reshape(PAIRS * levels, 2 * levels), GROUP, axis=1)
+
+
+MARK = ((8, 128), F32)
 
 
 def sizes(columns, features):
@@ -318,7 +336,6 @@
         10 * work,
         "vertical",
         loose_in=range(5),
-        vmem=MOST_VMEM,
     )[0]
 
 
@@ -328,34 +345,39 @@
         own_kernel,
         [pbias],
         [hidden, wq, wk, wv, gain],
-        [wide, *state, weights, weights],
-        [tall, wide, weights, pltpu.SemaphoreType.DMA((3,))],
+        [wide, *state, weights, weights, tall],
+        [tall, wide, weights, pltpu.SemaphoreType.DMA((4,))],
         8 * work,
         "own",
         loose_in=(1, 2, 3),
-    )
-
-
-def run_arrived(at, fixed, block, gain, wk, wv, q, state):
+        loose_out=(6,),
+    )
+
+
+def run_arrived(at, fixed, block, gain, wk, wv, q, state, after):
     _, wide, tall, kept, work = sizes(*block.shape)
     return call(
         arrived_kernel,
         [at[None], *fixed],
-        [block, gain, wk, wv, q, *state],
-        kept,
+        [block, gain, wk, wv, q, *state, after],
+        [*kept, MARK],
         [tall, wide],
         6 * work,
         "arrived",
-    )
-
-
-def run_last(at, fixed, block, gain, wk, wv, q, state, cotangent):
-    weights, wide, tall, kept, work = sizes(*block.shape)
+        loose_in=(8,),
+    )
+
+
+def run_last(at, core, fixed, block, gain, wk, wv, q, state, cotangent):
+    chips = lax.axis_size("space") // 2
+    rows = block.shape[1] // (2 * chips)
+    piece = (chips, rows, block.shape[1])
+    _, wide, tall, kept, work = sizes(*block.shape)
     return call(
         last_kernel,
-        [at[None], *fixed],
+        [at[None], core[None], *fixed],
         [block, gain, wk, wv, q, *state, cotangent],
-        [wide, weights],
+        [wide, (piece, F32), (piece, BF)],
         [*kept, tall, wide, wide, tall, pltpu.SemaphoreType.DMA((2,))],
         8 * work,
         "last",
@@ -391,8 +413,10 @@
     def moved(value, source_of):
         return lax.ppermute(value, "space", [(source_of(d) % devices, d) for d in range(devices)])
 
-    wq_v, wv_v, wq_p, wv_p = turned(query_vert, values_vert, query_patch, values_patch)
+    wq_v, wv_v, wq_p, wv_p = kept_in_hbm(*turned(query_vert, values_vert, query_patch, values_patch))
+    keys_vert, out_vert, keys_patch = kept_in_hbm(keys_vert, out_vert, keys_patch)
     x = lax.all_to_all(fields.reshape(levels, share, features), "level", 0, 0, tiled=True)
+    (x,) = kept_in_hbm(x)
     hidden = run_vertical(x, wq_v, keys_vert, wv_v, out_vert, norm_vert[None], expanded_bias(level_bias))
     hidden = lax.all_to_all(hidden, "level", 0, 0, tiled=True).reshape(columns, features)
 
@@ -407,24 +431,26 @@
 
     from_outer = moved(hidden, outer)
     from_twin = moved(hidden, twin)
-    from_inner = moved(hidden, inner)
     side = 1 - 2 * (place % 2)
     outer_at = (place + 2 * side) % devices
     inner_at = (place - 2 * side) % devices
     twin_at = place + side
     passed_at = (place - side) % devices
     gain = norm_patch[None]
-    q, *state, wk, wv = run_own(patch_bias, hidden, wq_p, keys_patch, wv_p, gain)
+    q, *state, wk, wv, again = run_own(patch_bias, hidden, wq_p, keys_patch, wv_p, gain)
+    from_inner = moved(again, inner)
     fixed = [neighbours, counts, patch_bias]
-    state = run_arrived(twin_at, fixed, from_twin, gain, wk, wv, q, state)
-    from_outer, *state = lax.optimization_barrier((from_outer, *state))
+    *state, mark = run_arrived(twin_at, fixed, from_twin, gain, wk, wv, q, state, jnp.zeros(*MARK))
+    from_outer, mark = lax.optimization_barrier((from_outer, mark))
     passed_on = moved(from_outer, twin)
-    state = run_arrived(outer_at, fixed, from_outer, gain, wk, wv, q, state)
-    state = run_arrived(passed_at, fixed, passed_on, gain, wk, wv, q, state)
-    mix, grad = run_last(
-        inner_at, fixed, from_inner, gain, wk, wv, q, state, cotangent.reshape(columns, features)
-    )
-    pieces = lax.all_to_all(grad.reshape(devices, features // devices, features), "space", 0, 0, tiled=True)
+    *state, mark = run_arrived(outer_at, fixed, from_outer, gain, wk, wv, q, state, mark)
+    *state, _ = run_arrived(passed_at, fixed, passed_on, gain, wk, wv, q, state, mark)
+    mix, keep, give = run_last(
+        inner_at, place % 2, fixed, from_inner, gain, wk, wv, q, state, *kept_in_hbm(cotangent.reshape(columns, features))
+    )
+    summed = (keep + moved(give, twin).astype(F32)).astype(BF)
+    same_core = [list(range(core, devices, 2)) for core in range(2)]
+    pieces = lax.all_to_all(summed, "space", 0, 0, axis_index_groups=same_core, tiled=True)
     shares = pieces.astype(F32).sum(axis=0).astype(BF)
     spread = jnp.broadcast_to(shares[None], (levels, *shares.shape))
     grad_wo = lax.all_to_all(spread, "level", 0, 0, tiled=True).astype(F32).sum(axis=0)

time: 151 us -> 140 us (0.927)
  blocking collectives: 50.4 us -> 40 us
  local copies, waits for them, and re-layouts: 12.1 us -> 8.32 us
  waiting for transfers between devices: 28.2 us -> 31.4 us
    all_to_all x1, blocking collectives: 23.6 us -> 14.2 us  [body(): lax.all_to_all(summed, 'space', 0, 0, axis_index_groups=same_core, tiled=...]
    ppermute x4 -> x5, waiting for transfers between devices: 0.01 us -> 3.28 us  [moved(): lax.ppermute(value, 'space', [(source_of(d) % devices, d) for d in range(...]
    unnamed x42 -> x36, local copies, waits for them, and re-layouts: 9.93 us -> 7.4 us
    ppermute x4 -> x5, starting transfers between devices: 8 us -> 8 us  [moved(): lax.ppermute(value, 'space', [(source_of(d) % devices, d) for d in range(...]
  transfers between devices with their start and end apart: 6 -> 7, of which waited for: 2 -> 4; matrix products, arithmetic and copies ran while one was open for 3% -> 2% of each run, Pallas kernels for 14% -> 16%
where the time goes in v3:
time: 140 us; the launch traced here: 139 us
  blocking collectives  40 us (29%)
  Pallas kernels  35.3 us (25%)
  waiting for transfers between devices  31.4 us (22%)
  starting transfers between devices  20.6 us (15%)
  local copies, waits for them, and re-layouts  8.32 us (6%)
  matrix products  1.7 us (1%)
    pallas_call x6, Pallas kernels, call(): pl.pallas_call(kernel, out_shape=shapes, in_specs=[IN_SMEM] * len(scalars...  31.4 us
    all_to_all x1, blocking collectives, body(): lax.all_to_all(hidden, 'level', 0, 0, tiled=True).reshape(columns, features)  25.8 us
    all_to_all x1, waiting for transfers between devices, body(): lax.all_to_all(fields.reshape(levels, share, features), 'level', 0, 0, ti...  19.3 us
    all_to_all x1, blocking collectives, body(): lax.all_to_all(summed, 'space', 0, 0, axis_index_groups=same_core, tiled=...  14.2 us
    all_to_all x1, starting transfers between devices, body(): lax.all_to_all(fields.reshape(levels, share, features), 'level', 0, 0, ti...  9.16 us
    all_to_all x1, waiting for transfers between devices, body(): lax.all_to_all(spread, 'level', 0, 0, tiled=True).astype(F32).sum(axis=0)  8.78 us
    ppermute x5, starting transfers between devices, moved(): lax.ppermute(value, 'space', [(source_of(d) % devices, d) for d in range(...  8 us
    unnamed x36, local copies, waits for them, and re-layouts  7.4 us
  transfers between devices with their start and end apart: 7, of which 4 were waited for; matrix products, arithmetic and copies ran while one was open for 2% of the time, Pallas kernels for 16%

profile of v3, /device:TPU:1, one launch (start us, length us, event | category | flops | bytes accessed | tf_op | source)
XLA Modules:
  0.0 139.0 jit_solution(14511197002984520058)
XLA Ops:
  0.6 9.2 %all-to-all-start = ((bf16[8,64,768]{2,1,0:T(8,128)(2,1)}), bf16[8,64,768]{2,1,0:T(8,128)(2,1)S(1)}, u32[]{:S(2)}, u32[]{:S(2)}) async-start(bf16[8,64,768]{2,1,0:T(8,128)(2,1)} %bitcast.22), calls=%async_computation | async-start | bytes 1572864 | tf_op jit(solution)/shard_map/all_to_all | solution.py:418
  10.2 3.9 %turned.1 = (bf16[768,768]{1,0:T(8,128)(2,1)}, bf16[768,768]{1,0:T(8,128)(2,1)}, bf16[768,768]{1,0:T(8,128)(2,1)}, bf16[768,768]{1,0:T(8,128)(2,1)}) custom-call(bf16[768,768]{1,0:T(8,128)(2,1)} %refs_0_.1, bf16[768,768]{1,0:T(8,128)(2,1)} %refs_1_.1, bf16[768,768]{1,0:T(8,128)(2,1)} %refs_2_.1, bf16[768,768]{1,0:T(8,128)(2,1)} %refs_3_.1), custom_call_target="tpu_custom_call" | custom-call | bytes 20971520 | tf_op jit(solution)/shard_map/turned/pallas_call | solution.py:269
  14.0 19.3 %all-to-all-done.x_in = bf16[8,64,768]{2,1,0:T(8,128)(2,1)S(1)} async-done(((bf16[8,64,768]{2,1,0:T(8,128)(2,1)}), bf16[8,64,768]{2,1,0:T(8,128)(2,1)S(1)}, u32[]{:S(2)}, u32[]{:S(2)}) %all-to-all-start) | async-done | bytes 786464 | tf_op jit(solution)/shard_map/all_to_all | solution.py:418
  34.3 6.7 %vertical.1 = bf16[8,64,768]{2,1,0:T(8,128)(2,1)S(1)} custom-call(bf16[8,64,768]{2,1,0:T(8,128)(2,1)} %copy-done.11, bf16[768,768]{1,0:T(8,128)(2,1)} %get-tuple-element.29.wq_in, bf16[768,768]{1,0:T(8,128)(2,1)} %wk_in.2, bf16[768,768]{1,0:T(8,128)(2,1)} %get-tuple-element.30.wv_in, bf16[768,768]{1,0:T(8,128)(2,1)} %wo_in.1, ...), custom_call_target="tpu_custom_call" | custom-call | flops 3019898880 | bytes 5557248 | tf_op jit(solution)/shard_map/vertical/pallas_call | solution.py:289
  41.0 25.8 %all_to_all.20 = bf16[8,64,768]{2,1,0:T(8,128)(2,1)S(1)} all-to-all(bf16[8,64,768]{2,1,0:T(8,128)(2,1)S(1)} %vertical.1), channel_id=1, replica_groups=mesh['space'=32,'level'=8] {'level'}, dimensions={0} | all-to-all | bytes 1572864 | tf_op jit(solution)/shard_map/all_to_all | solution.py:421
  67.5 1.3 collective-permute-start.1
  68.9 6.4 %own.1 = (bf16[768,512]{1,0:T(8,128)(2,1)S(1)}, f32[768,512]{1,0:T(8,128)S(1)}, f32[12,512]{1,0:T(8,128)S(1)}, f32[12,512]{1,0:T(8,128)S(1)}, bf16[768,768]{1,0:...) custom-call(f32[12,2]{1,0:T(8,128)S(1)} %copy.38.pbias, bf16[512,768]{1,0:T(8,128)(2,1)S(1)} %bitcast.20, ...), custom_call_target="tpu_custom_call" | custom-call | flops 2415919104 | bytes 4328448 | tf_op jit(solution)/shard_map/own/pallas_call | solution.py:289
  75.3 3.9 %arrived.3 = (f32[768,512]{1,0:T(8,128)S(1)}, f32[12,512]{1,0:T(8,128)S(1)}, f32[12,512]{1,0:T(8,128)S(1)}, f32[8,128]{1,0:T(8,128)S(1)}) custom-call(s32[1]{0:T(128)} %bitcast.8.source, s32[2,4]{1,0:T(2,128)S(1)} %copy-done, s32[2]{0:T(128)S(1)} %copy-done.1, f32[12,2]{1,0:T(8,128)S(1)} %copy.38.pbias, bf16[512,768]{1,0:T(8,128)(2,1)S(1)} %collective-permute-done.2.x, ...), custom_call_target="tpu_custom_call" | custom-call | flops 1811939328 | bytes 5561344 | tf_op jit(solution)/shard_map/arrived/pallas_call | solution.py:289
  79.3 1.2 copy-done.2
  80.5 1.3 collective-permute-done.1.x
  81.8 2.6 %collective-permute-start.3 = (bf16[512,768]{1,0:T(8,128)(2,1)S(1)}, bf16[512,768]{1,0:T(8,128)(2,1)}, u32[]{:S(2)}, u32[]{:S(2)}) collective-permute-start(bf16[512,768]{1,0:T(8,128)(2,1)S(1)} %collective-permute-done.1.x), channel_id=1, source_target_pairs={{8,0},{0,8},{24,16},{16,24},{40,32},{32,40},{56,48},{48,56},{72,64... | collective-permute-start | bytes 2359304 | tf_op jit(solution)/shard_map/ppermute | solution.py:414
  84.4 3.3 %collective-permute-start = (bf16[512,768]{1,0:T(8,128)(2,1)S(1)}, bf16[512,768]{1,0:T(8,128)(2,1)S(1)}, u32[]{:S(2)}, u32[]{:S(2)}) collective-permute-start(bf16[512,768]{1,0:T(8,128)(2,1)S(1)} %get-tuple-element.33), channel_id=1, source_target_pairs={{240,0},{24,8},{0,16},{40,24},{16,32},{56,40},{32,48},{72,56},{48,... | collective-permute-start | bytes 2359304 | tf_op jit(solution)/shard_map/ppermute | solution.py:414
  87.7 1.4 %copy-done.3 = f32[768,512]{1,0:T(8,128)S(1)} copy-done((f32[768,512]{1,0:T(8,128)S(1)}, f32[768,512]{1,0:T(8,128)}, u32[]{:S(2)}) %copy-start.3) | copy-done | bytes 1572888
  89.1 1.3 copy-done.5
  90.4 1.3 copy-done.7
  91.7 1.1 copy-done.9
  92.8 3.9 %arrived.4 = (f32[768,512]{1,0:T(8,128)S(1)}, f32[12,512]{1,0:T(8,128)S(1)}, f32[12,512]{1,0:T(8,128)S(1)}, f32[8,128]{1,0:T(8,128)S(1)}) custom-call(s32[1]{0:T(128)} %bitcast.9.source, s32[2,4]{1,0:T(2,128)S(1)} %copy-done, s32[2]{0:T(128)S(1)} %copy-done.1, f32[12,2]{1,0:T(8,128)S(1)} %copy.38.pbias, bf16[512,768]{1,0:T(8,128)(2,1)S(1)} %collective-permute-done.1.x, ...), custom_call_target="tpu_custom_call" | custom-call | flops 1811939328 | bytes 5561344 | tf_op jit(solution)/shard_map/arrived/pallas_call | solution.py:289
  96.8 4.8 %arrived.5 = (f32[768,512]{1,0:T(8,128)S(1)}, f32[12,512]{1,0:T(8,128)S(1)}, f32[12,512]{1,0:T(8,128)S(1)}, f32[8,128]{1,0:T(8,128)}) custom-call(s32[1]{0:T(128)} %bitcast.7.source, s32[2,4]{1,0:T(2,128)S(1)} %copy-done, s32[2]{0:T(128)S(1)} %copy-done.1, f32[12,2]{1,0:T(8,128)S(1)} %copy.38.pbias, bf16[512,768]{1,0:T(8,128)(2,1)} %collective-permute-done.3.x, ...), custom_call_target="tpu_custom_call" | custom-call | flops 1811939328 | bytes 5561344 | tf_op jit(solution)/shard_map/arrived/pallas_call | solution.py:289
  101.6 5.6 %last.1 = (bf16[768,512]{1,0:T(8,128)(2,1)S(1)}, f32[16,24,768]{2,1,0:T(8,128)S(1)}, bf16[16,24,768]{2,1,0:T(8,128)(2,1)S(1)}) custom-call(s32[1]{0:T(128)} %bitcast.5.source, s32[1]{0:T(128)} %bitcast.6.core, s32[2,4]{1,0:T(2,128)S(1)} %copy-done, s32[2]{0:T(128)S(1)} %copy-done.1, f32[12,2]{1,0:T(8,128)S(1)} %copy.38.pbias, ...), custom_call_target="tpu_custom_call" | custom-call | flops 2415919104 | bytes 6343680 | tf_op jit(solution)/shard_map/last/pallas_call | solution.py:289
  107.3 2.0 %collective-permute-done.4 = bf16[16,24,768]{2,1,0:T(8,128)(2,1)S(1)} collective-permute-done((bf16[16,24,768]{2,1,0:T(8,128)(2,1)S(1)}, bf16[16,24,768]{2,1,0:T(8,128)(2,1)S(1)}, u32[]{:S(2)}, u32[]{:S(2)}) %collective-permute-start.4) | collective-permute-done | bytes 589856 | tf_op jit(solution)/shard_map/ppermute | solution.py:414
  109.4 14.2 %all_to_all.21 = bf16[16,24,768]{2,1,0:T(8,128)(2,1)S(1)} all-to-all(bf16[16,24,768]{2,1,0:T(8,128)(2,1)S(1)} %add_convert_fusion.1), channel_id=1, replica_groups={{0,16,32,48,64,80,96,112,128,144,160,176,192,208,224,240},{8,24,40,56,7..., dimensions={0} | all-to-all | bytes 1179648 | tf_op jit(solution)/shard_map/all_to_all | solution.py:453
  124.4 3.4 %all-to-all-start.3 = ((bf16[8,24,768]{2,1,0:T(8,128)(2,1)}), bf16[8,24,768]{2,1,0:T(8,128)(2,1)S(1)}, u32[]{:S(2)}, u32[]{:S(2)}) async-start(bf16[8,24,768]{2,1,0:T(8,128)(2,1)} %broadcast_in_dim.46), calls=%async_computation.3 | async-start | bytes 589824 | tf_op jit(solution)/shard_map/all_to_all | solution.py:456
  127.9 1.7 %fusion = bf16[1,512,768]{2,1,0:T(8,128)(2,1)} fusion(bf16[768,512]{1,0:T(8,128)(2,1)S(1)} %get-tuple-element.53, bf16[768,768]{1,0:T(8,128)(2,1)S(1)} %copy-done.16, bf16[512,768]{1,0:T(8,128)(2,1)S(1)} %bitcast.21), kind=kOutput, calls=%fused_computation.1 | convolution fusion | flops 605159424 | bytes 3538944 | tf_op jit(solution)/shard_map/dot_general | solution.py:457
  129.6 8.8 %all-to-all-done.3 = bf16[8,24,768]{2,1,0:T(8,128)(2,1)S(1)} async-done(((bf16[8,24,768]{2,1,0:T(8,128)(2,1)}), bf16[8,24,768]{2,1,0:T(8,128)(2,1)S(1)}, u32[]{:S(2)}, u32[]{:S(2)}) %all-to-all-start.3) | async-done | bytes 294944 | tf_op jit(solution)/shard_map/all_to_all | solution.py:456
  (48 shorter events, 3.7 us)
Async XLA Ops:
  0.6 9.2 %copy-start.12 = (f32[12,8,8]{0,2,1:T(8,128)S(1)}, f32[12,8,8]{0,2,1:T(8,128)}, u32[]{:S(2)}) copy-start(f32[12,8,8]{0,2,1:T(8,128)} %param.22) | copy-start | bytes 9220
  0.6 9.5 %copy-start.13 = (f32[768]{0:T(1024)S(1)}, f32[768]{0:T(1024)}, u32[]{:S(2)}) copy-start(f32[768]{0:T(1024)} %param.17) | copy-start | bytes 9220
  0.6 32.7 %all-to-all-start = ((bf16[8,64,768]{2,1,0:T(8,128)(2,1)}), bf16[8,64,768]{2,1,0:T(8,128)(2,1)S(1)}, u32[]{:S(2)}, u32[]{:S(2)}) async-start(bf16[8,64,768]{2,1,0:T(8,128)(2,1)} %bitcast.22), calls=%async_computation | async-start | bytes 1572864 | tf_op jit(solution)/shard_map/all_to_all | solution.py:418
  33.4 0.9 copy-start.11
  41.0 27.8 %copy-start.15 = (f32[12,2]{0,1:T(2,128)S(1)}, f32[12,2]{0,1:T(2,128)}, u32[]{:S(2)}) copy-start(f32[12,2]{0,1:T(2,128)} %param.28) | copy-start | bytes 292
  41.0 27.9 %copy-start.14 = (f32[768]{0:T(1024)S(1)}, f32[768]{0:T(1024)}, u32[]{:S(2)}) copy-start(f32[768]{0:T(1024)} %param.23) | copy-start | bytes 9220
  66.8 8.5 %collective-permute-start.2 = (bf16[512,768]{1,0:T(8,128)(2,1)S(1)}, bf16[512,768]{1,0:T(8,128)(2,1)S(1)}, u32[]{:S(2)}, u32[]{:S(2)}) collective-permute-start(bf16[512,768]{1,0:T(8,128)(2,1)S(1)} %bitcast.18), channel_id=1, source_target_pairs={{8,0},{0,8},{24,16},{16,24},{40,32},{32,40},{56,48},{48,56},{72,64... | collective-permute-start | bytes 2359304 | tf_op jit(solution)/shard_map/ppermute | solution.py:414
  67.5 14.3 %collective-permute-start.1 = (bf16[512,768]{1,0:T(8,128)(2,1)S(1)}, bf16[512,768]{1,0:T(8,128)(2,1)S(1)}, u32[]{:S(2)}, u32[]{:S(2)}) collective-permute-start(bf16[512,768]{1,0:T(8,128)(2,1)S(1)} %bitcast.19), channel_id=1, source_target_pairs={{16,0},{248,8},{32,16},{8,24},{48,32},{24,40},{64,48},{40,56},{80,... | collective-permute-start | bytes 2359304 | tf_op jit(solution)/shard_map/ppermute | solution.py:414
  68.9 6.5 %copy-start = (s32[2,4]{1,0:T(2,128)S(1)}, s32[2,4]{1,0:T(2,128)}, u32[]{:S(2)}) copy-start(s32[2,4]{1,0:T(2,128)} %near.7) | copy-start | bytes 100
  68.9 6.5 %copy-start.1 = (s32[2]{0:T(128)S(1)}, s32[2]{0:T(128)}, u32[]{:S(2)}) copy-start(s32[2]{0:T(128)} %live.7) | copy-start | bytes 28
  75.3 4.0 %copy-start.4 = (bf16[768,768]{1,0:T(8,128)(2,1)}, bf16[768,768]{1,0:T(8,128)(2,1)S(1)}, u32[]{:S(2)}) copy-start(bf16[768,768]{1,0:T(8,128)(2,1)S(1)} %get-tuple-element.34.wk) | copy-start | bytes 3538948
  75.3 4.0 %copy-start.6 = (bf16[768,768]{1,0:T(8,128)(2,1)}, bf16[768,768]{1,0:T(8,128)(2,1)S(1)}, u32[]{:S(2)}) copy-start(bf16[768,768]{1,0:T(8,128)(2,1)S(1)} %get-tuple-element.35.wv) | copy-start | bytes 3538948
  75.3 4.0 %copy-start.8 = (bf16[768,512]{1,0:T(8,128)(2,1)}, bf16[768,512]{1,0:T(8,128)(2,1)S(1)}, u32[]{:S(2)}) copy-start(bf16[768,512]{1,0:T(8,128)(2,1)S(1)} %get-tuple-element.36.q) | copy-start | bytes 2359300
  79.3 1.2 copy-start.2
  81.8 15.0 %collective-permute-start.3 = (bf16[512,768]{1,0:T(8,128)(2,1)S(1)}, bf16[512,768]{1,0:T(8,128)(2,1)}, u32[]{:S(2)}, u32[]{:S(2)}) collective-permute-start(bf16[512,768]{1,0:T(8,128)(2,1)S(1)} %collective-permute-done.1.x), channel_id=1, source_target_pairs={{8,0},{0,8},{24,16},{16,24},{40,32},{32,40},{56,48},{48,56},{72,64... | collective-permute-start | bytes 2359304 | tf_op jit(solution)/shard_map/ppermute | solution.py:414
  84.4 17.2 %collective-permute-start = (bf16[512,768]{1,0:T(8,128)(2,1)S(1)}, bf16[512,768]{1,0:T(8,128)(2,1)S(1)}, u32[]{:S(2)}, u32[]{:S(2)}) collective-permute-start(bf16[512,768]{1,0:T(8,128)(2,1)S(1)} %get-tuple-element.33), channel_id=1, source_target_pairs={{240,0},{24,8},{0,16},{40,24},{16,32},{56,40},{32,48},{72,56},{48,... | collective-permute-start | bytes 2359304 | tf_op jit(solution)/shard_map/ppermute | solution.py:414
  87.7 1.4 %copy-start.3 = (f32[768,512]{1,0:T(8,128)S(1)}, f32[768,512]{1,0:T(8,128)}, u32[]{:S(2)}) copy-start(f32[768,512]{1,0:T(8,128)} %copy-done.2) | copy-start | bytes 4718596
  89.1 1.3 copy-start.5
  90.4 1.3 copy-start.7
  91.7 1.1 copy-start.9
  92.8 4.0 %copy-start.10 = (bf16[768,512]{1,0:T(8,128)(2,1)S(1)}, bf16[768,512]{1,0:T(8,128)(2,1)}, u32[]{:S(2)}) copy-start(bf16[768,512]{1,0:T(8,128)(2,1)} %copy-done.8) | copy-start | bytes 2359300
  107.2 2.1 %collective-permute-start.4 = (bf16[16,24,768]{2,1,0:T(8,128)(2,1)S(1)}, bf16[16,24,768]{2,1,0:T(8,128)(2,1)S(1)}, u32[]{:S(2)}, u32[]{:S(2)}) collective-permute-start(bf16[16,24,768]{2,1,0:T(8,128)(2,1)S(1)} %get-tuple-element.55), channel_id=1, source_target_pairs={{8,0},{0,8},{24,16},{16,24},{40,32},{32,40},{56,48},{48,56},{72,64... | collective-permute-start | bytes 1769480 | tf_op jit(solution)/shard_map/ppermute | solution.py:414
  109.4 18.4 %copy-start.16 = (bf16[768,768]{1,0:T(8,128)(2,1)S(1)}, bf16[768,768]{1,0:T(8,128)(2,1)}, u32[]{:S(2)}) copy-start(bf16[768,768]{1,0:T(8,128)(2,1)} %param.27) | copy-start | bytes 3538948
  124.4 13.9 %all-to-all-start.3 = ((bf16[8,24,768]{2,1,0:T(8,128)(2,1)}), bf16[8,24,768]{2,1,0:T(8,128)(2,1)S(1)}, u32[]{:S(2)}, u32[]{:S(2)}) async-start(bf16[8,24,768]{2,1,0:T(8,128)(2,1)} %broadcast_in_dim.46), calls=%async_computation.3 | async-start | bytes 589824 | tf_op jit(solution)/shard_map/all_to_all | solution.py:456

commit v4 on v3

--- a/solution.py
+++ b/solution.py
@@ -69,10 +69,10 @@
 
 
 def vertical_kernel(
-    x_in, wq_in, wk_in, wv_in, wo_in, gain, rows_of_bias, out, normed, q, k, v, mix, bias, x, wq, wk, wv, wo, arrivals
+    _, x, wq_in, wk_in, wv_in, wo_in, gain, rows_of_bias, out, normed, q, k, v, mix, bias, wq, wk, wv, wo, arrivals
 ):
     levels, columns, features = x.shape
-    copies = fetched([(x_in, x), (wq_in, wq), (wk_in, wk), (wv_in, wv), (wo_in, wo)], arrivals)
+    copies = fetched([(wq_in, wq), (wk_in, wk), (wv_in, wv), (wo_in, wo)], arrivals)
     tokens = levels * columns
     block = levels * GROUP
     key_column = lax.broadcasted_iota(jnp.int32, (GROUP, 2 * block), 0)
@@ -82,20 +82,19 @@
         for level in range(levels):
             row = rows_of_bias[pair * levels + level : pair * levels + level + 1]
             bias[pair, level * GROUP : (level + 1) * GROUP] = jnp.where(same, row, -jnp.inf)
-    copies[0].wait()
     for level in range(levels):
         rows = normalize(x[level], gain[...])
         for part in range(columns // GROUP):
             place = part * block + level * GROUP
             normed[place : place + GROUP] = rows[part * GROUP : (part + 1) * GROUP]
     spans = [slice(start, start + 256) for start in range(0, tokens, 256)]
+    copies[0].wait()
+    for span in spans:
+        q[:, span] = (nt(wq[...], normed[span]) * (HD**-0.5 * LOG2E)).astype(BF)
     copies[1].wait()
     for span in spans:
-        q[:, span] = (nt(wq[...], normed[span]) * (HD**-0.5 * LOG2E)).astype(BF)
+        k[span] = nn(normed[span], wk[...]).astype(BF)
     copies[2].wait()
-    for span in spans:
-        k[span] = nn(normed[span], wk[...]).astype(BF)
-    copies[3].wait()
     for span in spans:
         v[:, span] = nt(wv[...], normed[span]).astype(BF)
     steps = [(part, pair) for part in range(columns // GROUP) for pair in range(PAIRS)]
@@ -115,7 +114,7 @@
             mix[head, span] = (total[:HD] / total[HD : HD + 1]).astype(BF)
 
     staged(steps, step_scores, step_weights, step_mix)
-    copies[4].wait()
+    copies[3].wait()
     for part in range(columns // GROUP):
         span = slice(part * block, (part + 1) * block)
         projected = nn(mix[:, span].T, wo[...])
@@ -183,52 +182,63 @@
     )
 
 
-def keys_values(x, gain, wk, wv, k, v, wq=None, q=None):
+def keys_values(x, gain, wk, wv, k, v):
     for start in range(0, x.shape[0], PATCH):
         span = slice(start, start + PATCH)
         piece = normalize(x[span], gain[...])
-        if wq is not None:
-            q[:, span] = (nt(wq[...], piece) * (HD**-0.5 * LOG2E)).astype(BF)
         v[:, span] = nt(wv[...], piece).astype(BF)
         k[span] = nn(piece, wk[...]).astype(BF)
 
 
-def own_kernel(pbias, x, wq_in, wk_in, wv_in, gain, q, acc, top, total, wk, wv, again, k, v, wq, arrivals):
+def own_kernel(pbias, x, wq_in, wk_in, wv_in, gain, q, acc, top, total, wk, wv, again, k, v, wq, normed, arrivals):
     *loads, store = fetched([(wq_in, wq), (wk_in, wk), (wv_in, wv), (x, again)], arrivals)
-    for copy in loads:
-        copy.wait()
-    keys_values(x, gain, wk, wv, k, v, wq, q)
+    spans = [slice(start, start + PATCH) for start in range(0, x.shape[0], PATCH)]
+    for span in spans:
+        normed[span] = normalize(x[span], gain[...])
+    loads[0].wait()
+    for span in spans:
+        q[:, span] = (nt(wq[...], normed[span]) * (HD**-0.5 * LOG2E)).astype(BF)
+    loads[1].wait()
+    for span in spans:
+        k[span] = nn(normed[span], wk[...]).astype(BF)
+    loads[2].wait()
+    for span in spans:
+        v[:, span] = nt(wv[...], normed[span]).astype(BF)
     attend([(0, 0, 0.0), (1, PATCH, 0.0)], 0, q, k, v, pbias, (acc, top, total), None)
     store.wait()
 
 
-def arrived_part(source, near, live, pbias, x, gain, wk, wv, q, acc_in, top_in, total_in, acc, top, total, k, v):
+def arrived_part(distance, devices, place, near, live, pbias, x, gain, wk, wv, q, acc_in, top_in, total_in, acc, top, total, k, v):
     keys_values(x, gain, wk, wv, k, v)
+    outwards = 1 - 2 * lax.rem(place[0], 2)
+    source = lax.rem(place[0] + distance * outwards + devices, devices)
     places = []
     for own in range(2):
         found = jnp.int32(-1)
         for entry in range(near.shape[1]):
             listed = near[own, entry]
-            hit = jnp.logical_and(entry < live[own], lax.shift_right_arithmetic(listed, 1) == source[0])
+            hit = jnp.logical_and(entry < live[own], lax.shift_right_arithmetic(listed, 1) == source)
             found = jnp.where(hit, jnp.bitwise_and(listed, 1), found)
         barred = jnp.where(found >= 0, 0.0, -jnp.inf)
         places.append((own, pl.multiple_of(jnp.maximum(found, 0) * PATCH, PATCH), barred))
     attend(places, 1, q, k, v, pbias, (acc, top, total), (acc_in, top_in, total_in))
 
 
-def arrived_kernel(source, near, live, pbias, x, gain, wk, wv, q, acc_in, top_in, total_in, after, *rest):
+def arrived_kernel(distance, devices, place, near, live, pbias, x, gain, wk, wv, q, acc_in, top_in, total_in, after, *rest):
     acc, top, total, mark, k, v = rest
-    arrived_part(source, near, live, pbias, x, gain, wk, wv, q, acc_in, top_in, total_in, acc, top, total, k, v)
+    old, new = (acc_in, top_in, total_in), (acc, top, total)
+    arrived_part(distance, devices, place, near, live, pbias, x, gain, wk, wv, q, *old, *new, k, v)
     mark[...] = total[:8, :128]
 
 
 def last_kernel(
-    source, core, near, live, pbias, x, gain, wk, wv, q, acc_in, top_in, total_in, cot_in, mix_out, keep, give,
+    distance, devices, place, near, live, pbias, x, gain, wk, wv, q, acc_in, top_in, total_in, cot_in, mix_out, keep, give,
     acc, top, total, k, v, mix, cot, sent
 ):
     fetch = pltpu.make_async_copy(cot_in, cot, sent.at[0])
     fetch.start()
-    arrived_part(source, near, live, pbias, x, gain, wk, wv, q, acc_in, top_in, total_in, acc, top, total, k, v)
+    old, new = (acc_in, top_in, total_in), (acc, top, total)
+    arrived_part(distance, devices, place, near, live, pbias, x, gain, wk, wv, q, *old, *new, k, v)
     for pair in range(PAIRS):
         for own in range(2):
             mine = slice(own * PATCH, (own + 1) * PATCH)
@@ -242,7 +252,7 @@
     store.start()
     fetch.wait()
     chips, rows, _ = keep.shape
-    even = core[0] == 0
+    even = lax.rem(place[0], 2) == 0
     for first in range(0, chips, 8):
         span = slice(first * 2 * rows, (first + 8) * 2 * rows)
         grad = nn(mix[span], cot[...])
@@ -285,7 +295,7 @@
 
 def call(kernel, scalars, arrays, outs, scratch, flops, name, loose_in=(), loose_out=(), vmem=VMEM_BYTES):
     shapes = [jax.ShapeDtypeStruct(shape, kind) for shape, kind in outs]
-    moved = sum(a.size * a.dtype.itemsize for a in arrays)
+    moved = flops // 256
     return pl.pallas_call(
         kernel,
         out_shape=shapes,
@@ -314,12 +324,12 @@
     return weights, turned_tokens, ((columns, features), BF), state, columns * features * features
 
 
-def run_vertical(x, wq, wk, wv, wo, gain, rows_of_bias):
+def run_vertical(place, x, wq, wk, wv, wo, gain, rows_of_bias):
     levels, share, features = x.shape
     weights, wide, tall, _, work = sizes(levels * share, features)
     return call(
         vertical_kernel,
-        [],
+        [place],
         [x, wq, wk, wv, wo, gain, rows_of_bias],
         [(x.shape, BF)],
         [
@@ -329,13 +339,12 @@
             wide,
             wide,
             ((PAIRS, levels * GROUP, 2 * levels * GROUP), F32),
-            (x.shape, BF),
             *([weights] * 4),
-            pltpu.SemaphoreType.DMA((5,)),
+            pltpu.SemaphoreType.DMA((4,)),
         ],
         10 * work,
         "vertical",
-        loose_in=range(5),
+        loose_in=range(1, 5),
     )[0]
 
 
@@ -346,7 +355,7 @@
         [pbias],
         [hidden, wq, wk, wv, gain],
         [wide, *state, weights, weights, tall],
-        [tall, wide, weights, pltpu.SemaphoreType.DMA((4,))],
+        [tall, wide, weights, tall, pltpu.SemaphoreType.DMA((4,))],
         8 * work,
         "own",
         loose_in=(1, 2, 3),
@@ -354,28 +363,28 @@
     )
 
 
-def run_arrived(at, fixed, block, gain, wk, wv, q, state, after):
+def run_arrived(distance, devices, fixed, block, gain, wk, wv, q, state, after):
     _, wide, tall, kept, work = sizes(*block.shape)
     return call(
-        arrived_kernel,
-        [at[None], *fixed],
+        functools.partial(arrived_kernel, distance, devices),
+        fixed,
         [block, gain, wk, wv, q, *state, after],
         [*kept, MARK],
         [tall, wide],
-        6 * work,
+        work // 4,
         "arrived",
         loose_in=(8,),
     )
 
 
-def run_last(at, core, fixed, block, gain, wk, wv, q, state, cotangent):
-    chips = lax.axis_size("space") // 2
+def run_last(distance, devices, fixed, block, gain, wk, wv, q, state, cotangent):
+    chips = devices // 2
     rows = block.shape[1] // (2 * chips)
     piece = (chips, rows, block.shape[1])
     _, wide, tall, kept, work = sizes(*block.shape)
     return call(
-        last_kernel,
-        [at[None], core[None], *fixed],
+        functools.partial(last_kernel, distance, devices),
+        fixed,
         [block, gain, wk, wv, q, *state, cotangent],
         [wide, (piece, F32), (piece, BF)],
         [*kept, tall, wide, wide, tall, pltpu.SemaphoreType.DMA((2,))],
@@ -407,7 +416,7 @@
     _, columns, features = fields.shape
     levels = lax.axis_size("level")
     devices = lax.axis_size("space")
-    place = lax.axis_index("space")
+    place = lax.axis_index("space")[None]
     share = columns // levels
 
     def moved(value, source_of):
@@ -416,8 +425,7 @@
     wq_v, wv_v, wq_p, wv_p = kept_in_hbm(*turned(query_vert, values_vert, query_patch, values_patch))
     keys_vert, out_vert, keys_patch = kept_in_hbm(keys_vert, out_vert, keys_patch)
     x = lax.all_to_all(fields.reshape(levels, share, features), "level", 0, 0, tiled=True)
-    (x,) = kept_in_hbm(x)
-    hidden = run_vertical(x, wq_v, keys_vert, wv_v, out_vert, norm_vert[None], expanded_bias(level_bias))
+    hidden = run_vertical(place, x, wq_v, keys_vert, wv_v, out_vert, norm_vert[None], expanded_bias(level_bias))
     hidden = lax.all_to_all(hidden, "level", 0, 0, tiled=True).reshape(columns, features)
 
     def outer(d):
@@ -431,31 +439,28 @@
 
     from_outer = moved(hidden, outer)
     from_twin = moved(hidden, twin)
-    side = 1 - 2 * (place % 2)
-    outer_at = (place + 2 * side) % devices
-    inner_at = (place - 2 * side) % devices
-    twin_at = place + side
-    passed_at = (place - side) % devices
     gain = norm_patch[None]
     q, *state, wk, wv, again = run_own(patch_bias, hidden, wq_p, keys_patch, wv_p, gain)
     from_inner = moved(again, inner)
-    fixed = [neighbours, counts, patch_bias]
-    *state, mark = run_arrived(twin_at, fixed, from_twin, gain, wk, wv, q, state, jnp.zeros(*MARK))
+    fixed = [place, neighbours, counts, patch_bias]
+    *state, mark = run_arrived(1, devices, fixed, from_twin, gain, wk, wv, q, state, jnp.zeros(*MARK))
     from_outer, mark = lax.optimization_barrier((from_outer, mark))
     passed_on = moved(from_outer, twin)
-    *state, mark = run_arrived(outer_at, fixed, from_outer, gain, wk, wv, q, state, mark)
-    *state, _ = run_arrived(passed_at, fixed, passed_on, gain, wk, wv, q, state, mark)
+    *state, mark = run_arrived(2, devices, fixed, from_outer, gain, wk, wv, q, state, mark)
+    *state, _ = run_arrived(-1, devices, fixed, passed_on, gain, wk, wv, q, state, mark)
     mix, keep, give = run_last(
-        inner_at, place % 2, fixed, from_inner, gain, wk, wv, q, state, *kept_in_hbm(cotangent.reshape(columns, features))
-    )
-    summed = (keep + moved(give, twin).astype(F32)).astype(BF)
+        -2, devices, fixed, from_inner, gain, wk, wv, q, state, *kept_in_hbm(cotangent.reshape(columns, features))
+    )
+    received = moved(give, twin)
+    projected = lax.dot_general(mix, out_patch, (((0,), (0,)), ((), ())), preferred_element_type=F32)
+    out_fields = (hidden.astype(F32) + projected).astype(BF)
+    received, out_fields = lax.optimization_barrier((received, out_fields))
+    summed = (keep + received.astype(F32)).astype(BF)
     same_core = [list(range(core, devices, 2)) for core in range(2)]
     pieces = lax.all_to_all(summed, "space", 0, 0, axis_index_groups=same_core, tiled=True)
     shares = pieces.astype(F32).sum(axis=0).astype(BF)
     spread = jnp.broadcast_to(shares[None], (levels, *shares.shape))
     grad_wo = lax.all_to_all(spread, "level", 0, 0, tiled=True).astype(F32).sum(axis=0)
-    projected = lax.dot_general(mix, out_patch, (((0,), (0,)), ((), ())), preferred_element_type=F32)
-    out_fields = (hidden.astype(F32) + projected).astype(BF)
     return (out_fields[None], grad_wo)
 
 

time: 140 us -> 136 us (0.971)
  blocking collectives: 40 us -> 54.9 us
  waiting for transfers between devices: 31.4 us -> 22.9 us
  local copies, waits for them, and re-layouts: 8.32 us -> 0.45 us
  starting transfers between devices: 20.6 us -> 19.2 us
    all_to_all x0 -> x1, blocking collectives: none -> 12.8 us  [body(): lax.all_to_all(spread, 'level', 0, 0, tiled=True).astype(F32).sum(axis=0)]
    all_to_all x1 -> x0, waiting for transfers between devices: 8.78 us -> none  [body(): lax.all_to_all(spread, 'level', 0, 0, tiled=True).astype(F32).sum(axis=0)]
    unnamed x36 -> x16, local copies, waits for them, and re-layouts: 7.4 us -> 0.24 us
    all_to_all x1 -> x0, starting transfers between devices: 3.42 us -> none  [body(): lax.all_to_all(spread, 'level', 0, 0, tiled=True).astype(F32).sum(axis=0)]
    all_to_all x1, blocking collectives: 14.2 us -> 16.4 us  [body(): lax.all_to_all(summed, 'space', 0, 0, axis_index_groups=same_core, tiled=...]
    ppermute x5, starting transfers between devices: 8 us -> 10.1 us  [moved(): lax.ppermute(value, 'space', [(source_of(d) % devices, d) for d in range(...]
  transfers between devices with their start and end apart: 7 -> 6, of which waited for: 4 -> 3; matrix products, arithmetic and copies ran while one was open for 2% -> 2% of each run, Pallas kernels for 16% -> 16%
where the time goes in v4:
time: 136 us; the launch traced here: 135 us
  blocking collectives  54.9 us (40%)
  Pallas kernels  34.2 us (25%)
  waiting for transfers between devices  22.9 us (17%)
  starting transfers between devices  19.2 us (14%)
  matrix products  1.7 us (1%)
    pallas_call x6, Pallas kernels, call(): pl.pallas_call(kernel, out_shape=shapes, in_specs=[IN_SMEM] * len(scalars...  30.3 us
    all_to_all x1, blocking collectives, body(): lax.all_to_all(hidden, 'level', 0, 0, tiled=True).reshape(columns, features)  25.6 us
    all_to_all x1, waiting for transfers between devices, body(): lax.all_to_all(fields.reshape(levels, share, features), 'level', 0, 0, ti...  19.4 us
    all_to_all x1, blocking collectives, body(): lax.all_to_all(summed, 'space', 0, 0, axis_index_groups=same_core, tiled=...  16.4 us
    all_to_all x1, blocking collectives, body(): lax.all_to_all(spread, 'level', 0, 0, tiled=True).astype(F32).sum(axis=0)  12.8 us
    ppermute x5, starting transfers between devices, moved(): lax.ppermute(value, 'space', [(source_of(d) % devices, d) for d in range(...  10.1 us
    all_to_all x1, starting transfers between devices, body(): lax.all_to_all(fields.reshape(levels, share, features), 'level', 0, 0, ti...  9.16 us
    pallas_call x1, Pallas kernels, turned(): pl.pallas_call(turning_kernel, out_shape=[jax.ShapeDtypeStruct(shape, BF)...  3.83 us
  transfers between devices with their start and end apart: 6, of which 3 were waited for; matrix products, arithmetic and copies ran while one was open for 2% of the time, Pallas kernels for 16%

profile of v4, /device:TPU:1, one launch (start us, length us, event | category | flops | bytes accessed | tf_op | source)
XLA Modules:
  0.0 135.0 jit_solution(557195160186662024)
XLA Ops:
  0.6 9.2 %all-to-all-start = ((bf16[8,64,768]{2,1,0:T(8,128)(2,1)}), bf16[8,64,768]{2,1,0:T(8,128)(2,1)S(1)}, u32[]{:S(2)}, u32[]{:S(2)}) async-start(bf16[8,64,768]{2,1,0:T(8,128)(2,1)} %bitcast.17), calls=%async_computation | async-start | bytes 1572864 | tf_op jit(solution)/shard_map/all_to_all | solution.py:427
  9.8 0.1 copy.31
  10.2 3.8 %turned.1 = (bf16[768,768]{1,0:T(8,128)(2,1)}, bf16[768,768]{1,0:T(8,128)(2,1)}, bf16[768,768]{1,0:T(8,128)(2,1)}, bf16[768,768]{1,0:T(8,128)(2,1)}) custom-call(bf16[768,768]{1,0:T(8,128)(2,1)} %refs_0_.1, bf16[768,768]{1,0:T(8,128)(2,1)} %refs_1_.1, bf16[768,768]{1,0:T(8,128)(2,1)} %refs_2_.1, bf16[768,768]{1,0:T(8,128)(2,1)} %refs_3_.1), custom_call_target="tpu_custom_call" | custom-call | bytes 20971520 | tf_op jit(solution)/shard_map/turned/pallas_call | solution.py:279
  14.0 19.4 %all-to-all-done.x = bf16[8,64,768]{2,1,0:T(8,128)(2,1)S(1)} async-done(((bf16[8,64,768]{2,1,0:T(8,128)(2,1)}), bf16[8,64,768]{2,1,0:T(8,128)(2,1)S(1)}, u32[]{:S(2)}, u32[]{:S(2)}) %all-to-all-start) | async-done | bytes 786464 | tf_op jit(solution)/shard_map/all_to_all | solution.py:427
  33.4 6.4 %vertical.1 = bf16[8,64,768]{2,1,0:T(8,128)(2,1)S(1)} custom-call(s32[1]{0:T(128)} %bitcast._.place, bf16[8,64,768]{2,1,0:T(8,128)(2,1)S(1)} %all-to-all-done.x, bf16[768,768]{1,0:T(8,128)(2,1)} %get-tuple-element.31.wq_in, bf16[768,768]{1,0:T(8,128)(2,1)} %wk_in.2, bf16[768,768]{1,0:T(8,128)(2,1)} %get-tuple-element.32.wv_in, bf16[768,768]{1,0:T(8,128)(2,1)} %wo_in.1, ...), custom_call_target="tpu_custom_call" | custom-call | flops 3019898880 | bytes 11796480 | tf_op jit(solution)/shard_map/vertical/pallas_call | solution.py:299
  39.8 25.6 %all_to_all.20 = bf16[8,64,768]{2,1,0:T(8,128)(2,1)S(1)} all-to-all(bf16[8,64,768]{2,1,0:T(8,128)(2,1)S(1)} %vertical.1), channel_id=1, replica_groups=mesh['space'=32,'level'=8] {'level'}, dimensions={0} | all-to-all | bytes 1572864 | tf_op jit(solution)/shard_map/all_to_all | solution.py:429
  65.5 0.8 collective-permute-start.2
  66.3 1.3 collective-permute-start.1
  67.6 0.1 copy.38.pbias
  67.8 6.0 %own.1 = (bf16[768,512]{1,0:T(8,128)(2,1)S(1)}, f32[768,512]{1,0:T(8,128)S(1)}, f32[12,512]{1,0:T(8,128)S(1)}, f32[12,512]{1,0:T(8,128)S(1)}, bf16[768,768]{1,0:...) custom-call(f32[12,2]{1,0:T(8,128)S(1)} %copy.38.pbias, bf16[512,768]{1,0:T(8,128)(2,1)S(1)} %bitcast.15, ...), custom_call_target="tpu_custom_call" | custom-call | flops 2415919104 | bytes 9437184 | tf_op jit(solution)/shard_map/own/pallas_call | solution.py:299
  73.8 4.0 %arrived.3 = (f32[768,512]{1,0:T(8,128)S(1)}, f32[12,512]{1,0:T(8,128)S(1)}, f32[12,512]{1,0:T(8,128)S(1)}, f32[8,128]{1,0:T(8,128)S(1)}) custom-call(s32[1]{0:T(128)} %bitcast._.place, s32[2,4]{1,0:T(2,128)S(1)} %copy-done, s32[2]{0:T(128)S(1)} %copy-done.1, f32[12,2]{1,0:T(8,128)S(1)} %copy.38.pbias, bf16[512,768]{1,0:T(8,128)(2,1)S(1)} %collective-permute-done.2.x, ...), custom_call_target="tpu_custom_call" | custom-call | flops 75497472 | bytes 294912 | tf_op jit(solution)/shard_map/arrived/pallas_call | solution.py:299
  77.8 2.8 %collective-permute-done.1.x = bf16[512,768]{1,0:T(8,128)(2,1)S(1)} collective-permute-done((bf16[512,768]{1,0:T(8,128)(2,1)S(1)}, bf16[512,768]{1,0:T(8,128)(2,1)S(1)}, u32[]{:S(2)}, u32[]{:S(2)}) %collective-permute-start.1) | collective-permute-done | bytes 786464 | tf_op jit(solution)/shard_map/ppermute | solution.py:423
  80.6 1.2 collective-permute-start.3
  81.8 4.8 %collective-permute-start = (bf16[512,768]{1,0:T(8,128)(2,1)S(1)}, bf16[512,768]{1,0:T(8,128)(2,1)S(1)}, u32[]{:S(2)}, u32[]{:S(2)}) collective-permute-start(bf16[512,768]{1,0:T(8,128)(2,1)S(1)} %get-tuple-element.35), channel_id=1, source_target_pairs={{240,0},{24,8},{0,16},{40,24},{16,32},{56,40},{32,48},{72,56},{48,... | collective-permute-start | bytes 2359304 | tf_op jit(solution)/shard_map/ppermute | solution.py:423
  86.6 4.0 %arrived.4 = (f32[768,512]{1,0:T(8,128)S(1)}, f32[12,512]{1,0:T(8,128)S(1)}, f32[12,512]{1,0:T(8,128)S(1)}, f32[8,128]{1,0:T(8,128)S(1)}) custom-call(s32[1]{0:T(128)} %bitcast._.place, s32[2,4]{1,0:T(2,128)S(1)} %copy-done, s32[2]{0:T(128)S(1)} %copy-done.1, f32[12,2]{1,0:T(8,128)S(1)} %copy.38.pbias, bf16[512,768]{1,0:T(8,128)(2,1)S(1)} %collective-permute-done.1.x, ...), custom_call_target="tpu_custom_call" | custom-call | flops 75497472 | bytes 294912 | tf_op jit(solution)/shard_map/arrived/pallas_call | solution.py:299
  90.5 4.3 %arrived.5 = (f32[768,512]{1,0:T(8,128)S(1)}, f32[12,512]{1,0:T(8,128)S(1)}, f32[12,512]{1,0:T(8,128)S(1)}, f32[8,128]{1,0:T(8,128)}) custom-call(s32[1]{0:T(128)} %bitcast._.place, s32[2,4]{1,0:T(2,128)S(1)} %copy-done, s32[2]{0:T(128)S(1)} %copy-done.1, f32[12,2]{1,0:T(8,128)S(1)} %copy.38.pbias, bf16[512,768]{1,0:T(8,128)(2,1)S(1)} %collective-permute-done.3.x, ...), custom_call_target="tpu_custom_call" | custom-call | flops 75497472 | bytes 294912 | tf_op jit(solution)/shard_map/arrived/pallas_call | solution.py:299
  94.8 0.7 collective-permute-done.x
  95.5 5.7 %last.1 = (bf16[768,512]{1,0:T(8,128)(2,1)S(1)}, f32[16,24,768]{2,1,0:T(8,128)S(1)}, bf16[16,24,768]{2,1,0:T(8,128)(2,1)S(1)}) custom-call(s32[1]{0:T(128)} %bitcast._.place, s32[2,4]{1,0:T(2,128)S(1)} %copy-done, s32[2]{0:T(128)S(1)} %copy-done.1, f32[12,2]{1,0:T(8,128)S(1)} %copy.38.pbias, bf16[512,768]{1,0:T(8,128)(2,1)S(1)} %collective-permute-done.x, ...), custom_call_target="tpu_custom_call" | custom-call | flops 2415919104 | bytes 9437184 | tf_op jit(solution)/shard_map/last/pallas_call | solution.py:299
  101.2 2.0 %collective-permute-start.4 = (bf16[16,24,768]{2,1,0:T(8,128)(2,1)S(1)}, bf16[16,24,768]{2,1,0:T(8,128)(2,1)S(1)}, u32[]{:S(2)}, u32[]{:S(2)}) collective-permute-start(bf16[16,24,768]{2,1,0:T(8,128)(2,1)S(1)} %get-tuple-element.55), channel_id=1, source_target_pairs={{8,0},{0,8},{24,16},{16,24},{40,32},{32,40},{56,48},{48,56},{72,64... | collective-permute-start | bytes 1769480 | tf_op jit(solution)/shard_map/ppermute | solution.py:423
  103.2 1.7 %add_convert_fusion = bf16[512,768]{1,0:T(8,128)(2,1)} fusion(bf16[512,768]{1,0:T(8,128)(2,1)S(1)} %bitcast.16, bf16[768,512]{1,0:T(8,128)(2,1)S(1)} %get-tuple-element.56, bf16[768,768]{1,0:T(8,128)(2,1)S(1)} %copy-done.6), kind=kOutput, calls=%fused_computation | convolution fusion | flops 605159424 | bytes 3538944 | tf_op jit(solution)/shard_map/dot_general | solution.py:455
  104.9 0.1 add_convert_fusion.1
  105.0 16.4 %all_to_all.21 = bf16[16,24,768]{2,1,0:T(8,128)(2,1)S(1)} all-to-all(bf16[16,24,768]{2,1,0:T(8,128)(2,1)S(1)} %add_convert_fusion.1), channel_id=1, replica_groups={{0,16,32,48,64,80,96,112,128,144,160,176,192,208,224,240},{8,24,40,56,7..., dimensions={0} | all-to-all | bytes 1179648 | tf_op jit(solution)/shard_map/all_to_all | solution.py:460
  121.6 12.8 %all_to_all.22 = bf16[8,24,768]{2,1,0:T(8,128)(2,1)S(1)} all-to-all(bf16[8,24,768]{2,1,0:T(8,128)(2,1)S(1)} %broadcast_in_dim.30), channel_id=1, replica_groups=mesh['space'=32,'level'=8] {'level'}, dimensions={0} | all-to-all | bytes 589824 | tf_op jit(solution)/shard_map/all_to_all | solution.py:463
  134.4 0.7 convert_reduce_fusion
  (27 shorter events, 0.3 us)
Async XLA Ops:
  0.6 9.2 %copy-start.2 = (f32[12,8,8]{0,2,1:T(8,128)S(1)}, f32[12,8,8]{0,2,1:T(8,128)}, u32[]{:S(2)}) copy-start(f32[12,8,8]{0,2,1:T(8,128)} %param.22) | copy-start | bytes 9220
  0.6 9.5 %copy-start.3 = (f32[768]{0:T(1024)S(1)}, f32[768]{0:T(1024)}, u32[]{:S(2)}) copy-start(f32[768]{0:T(1024)} %param.17) | copy-start | bytes 9220
  0.6 32.7 %all-to-all-start = ((bf16[8,64,768]{2,1,0:T(8,128)(2,1)}), bf16[8,64,768]{2,1,0:T(8,128)(2,1)S(1)}, u32[]{:S(2)}, u32[]{:S(2)}) async-start(bf16[8,64,768]{2,1,0:T(8,128)(2,1)} %bitcast.17), calls=%async_computation | async-start | bytes 1572864 | tf_op jit(solution)/shard_map/all_to_all | solution.py:427
  39.8 27.8 %copy-start.5 = (f32[12,2]{0,1:T(2,128)S(1)}, f32[12,2]{0,1:T(2,128)}, u32[]{:S(2)}) copy-start(f32[12,2]{0,1:T(2,128)} %param.28) | copy-start | bytes 292
  39.8 27.9 %copy-start.4 = (f32[768]{0:T(1024)S(1)}, f32[768]{0:T(1024)}, u32[]{:S(2)}) copy-start(f32[768]{0:T(1024)} %param.23) | copy-start | bytes 9220
  65.5 8.3 %collective-permute-start.2 = (bf16[512,768]{1,0:T(8,128)(2,1)S(1)}, bf16[512,768]{1,0:T(8,128)(2,1)S(1)}, u32[]{:S(2)}, u32[]{:S(2)}) collective-permute-start(bf16[512,768]{1,0:T(8,128)(2,1)S(1)} %bitcast.13), channel_id=1, source_target_pairs={{8,0},{0,8},{24,16},{16,24},{40,32},{32,40},{56,48},{48,56},{72,64... | collective-permute-start | bytes 2359304 | tf_op jit(solution)/shard_map/ppermute | solution.py:423
  66.3 14.3 %collective-permute-start.1 = (bf16[512,768]{1,0:T(8,128)(2,1)S(1)}, bf16[512,768]{1,0:T(8,128)(2,1)S(1)}, u32[]{:S(2)}, u32[]{:S(2)}) collective-permute-start(bf16[512,768]{1,0:T(8,128)(2,1)S(1)} %bitcast.14), channel_id=1, source_target_pairs={{16,0},{248,8},{32,16},{8,24},{48,32},{24,40},{64,48},{40,56},{80,... | collective-permute-start | bytes 2359304 | tf_op jit(solution)/shard_map/ppermute | solution.py:423
  67.7 6.1 %copy-start = (s32[2,4]{1,0:T(2,128)S(1)}, s32[2,4]{1,0:T(2,128)}, u32[]{:S(2)}) copy-start(s32[2,4]{1,0:T(2,128)} %near.7) | copy-start | bytes 100
  67.7 6.1 %copy-start.1 = (s32[2]{0:T(128)S(1)}, s32[2]{0:T(128)}, u32[]{:S(2)}) copy-start(s32[2]{0:T(128)} %live.7) | copy-start | bytes 28
  80.6 9.9 %collective-permute-start.3 = (bf16[512,768]{1,0:T(8,128)(2,1)S(1)}, bf16[512,768]{1,0:T(8,128)(2,1)S(1)}, u32[]{:S(2)}, u32[]{:S(2)}) collective-permute-start(bf16[512,768]{1,0:T(8,128)(2,1)S(1)} %collective-permute-done.1.x), channel_id=1, source_target_pairs={{8,0},{0,8},{24,16},{16,24},{40,32},{32,40},{56,48},{48,56},{72,64... | collective-permute-start | bytes 2359304 | tf_op jit(solution)/shard_map/ppermute | solution.py:423
  81.8 13.7 %collective-permute-start = (bf16[512,768]{1,0:T(8,128)(2,1)S(1)}, bf16[512,768]{1,0:T(8,128)(2,1)S(1)}, u32[]{:S(2)}, u32[]{:S(2)}) collective-permute-start(bf16[512,768]{1,0:T(8,128)(2,1)S(1)} %get-tuple-element.35), channel_id=1, source_target_pairs={{240,0},{24,8},{0,16},{40,24},{16,32},{56,40},{32,48},{72,56},{48,... | collective-permute-start | bytes 2359304 | tf_op jit(solution)/shard_map/ppermute | solution.py:423
  95.5 7.7 %copy-start.6 = (bf16[768,768]{1,0:T(8,128)(2,1)S(1)}, bf16[768,768]{1,0:T(8,128)(2,1)}, u32[]{:S(2)}) copy-start(bf16[768,768]{1,0:T(8,128)(2,1)} %param.27) | copy-start | bytes 3538948
  101.2 3.7 %collective-permute-start.4 = (bf16[16,24,768]{2,1,0:T(8,128)(2,1)S(1)}, bf16[16,24,768]{2,1,0:T(8,128)(2,1)S(1)}, u32[]{:S(2)}, u32[]{:S(2)}) collective-permute-start(bf16[16,24,768]{2,1,0:T(8,128)(2,1)S(1)} %get-tuple-element.55), channel_id=1, source_target_pairs={{8,0},{0,8},{24,16},{16,24},{40,32},{32,40},{56,48},{48,56},{72,64... | collective-permute-start | bytes 1769480 | tf_op jit(solution)/shard_map/ppermute | solution.py:423

commit v5 on v4

--- a/solution.py
+++ b/solution.py
@@ -182,12 +182,15 @@
     )
 
 
-def keys_values(x, gain, wk, wv, k, v):
-    for start in range(0, x.shape[0], PATCH):
-        span = slice(start, start + PATCH)
-        piece = normalize(x[span], gain[...])
-        v[:, span] = nt(wv[...], piece).astype(BF)
-        k[span] = nn(piece, wk[...]).astype(BF)
+def keys_values(blocks, gain, wk, wv, k, v):
+    done = 0
+    for block in blocks:
+        for start in range(0, block.shape[0], PATCH):
+            span = slice(done, done + PATCH)
+            piece = normalize(block[start : start + PATCH], gain[...])
+            v[:, span] = nt(wv[...], piece).astype(BF)
+            k[span] = nn(piece, wk[...]).astype(BF)
+            done += PATCH
 
 
 def own_kernel(pbias, x, wq_in, wk_in, wv_in, gain, q, acc, top, total, wk, wv, again, k, v, wq, normed, arrivals):
@@ -208,8 +211,8 @@
     store.wait()
 
 
-def arrived_part(distance, devices, place, near, live, pbias, x, gain, wk, wv, q, acc_in, top_in, total_in, acc, top, total, k, v):
-    keys_values(x, gain, wk, wv, k, v)
+def arrived_part(distance, devices, place, near, live, pbias, blocks, gain, wk, wv, q, acc_in, top_in, total_in, acc, top, total, k, v):
+    keys_values(blocks, gain, wk, wv, k, v)
     outwards = 1 - 2 * lax.rem(place[0], 2)
     source = lax.rem(place[0] + distance * outwards + devices, devices)
     places = []
@@ -224,11 +227,11 @@
     attend(places, 1, q, k, v, pbias, (acc, top, total), (acc_in, top_in, total_in))
 
 
-def arrived_kernel(distance, devices, place, near, live, pbias, x, gain, wk, wv, q, acc_in, top_in, total_in, after, *rest):
-    acc, top, total, mark, k, v = rest
-    old, new = (acc_in, top_in, total_in), (acc, top, total)
-    arrived_part(distance, devices, place, near, live, pbias, x, gain, wk, wv, q, *old, *new, k, v)
-    mark[...] = total[:8, :128]
+def arrived_kernel(distance, devices, count, place, near, live, pbias, *refs):
+    blocks, (gain, wk, wv, q, *old) = refs[:count], refs[count : count + 7]
+    new, (mark, k, v) = refs[count + 8 : count + 11], refs[count + 11 :]
+    arrived_part(distance, devices, place, near, live, pbias, blocks, gain, wk, wv, q, *old, *new, k, v)
+    mark[...] = new[2][:8, :128]
 
 
 def last_kernel(
@@ -238,7 +241,7 @@
     fetch = pltpu.make_async_copy(cot_in, cot, sent.at[0])
     fetch.start()
     old, new = (acc_in, top_in, total_in), (acc, top, total)
-    arrived_part(distance, devices, place, near, live, pbias, x, gain, wk, wv, q, *old, *new, k, v)
+    arrived_part(distance, devices, place, near, live, pbias, (x,), gain, wk, wv, q, *old, *new, k, v)
     for pair in range(PAIRS):
         for own in range(2):
             mine = slice(own * PATCH, (own + 1) * PATCH)
@@ -308,6 +311,27 @@
     )(*scalars, *arrays)
 
 
+def halving_kernel(block, _, first, second, sent):
+    rows = first.shape[0]
+    for copy in fetched([(block.at[:rows], first), (block.at[rows:], second)], sent):
+        copy.wait()
+
+
+def halved(block, after):
+    half = ((block.shape[0] // 2, block.shape[1]), BF)
+    return call(
+        halving_kernel,
+        [],
+        [block, after],
+        [half, half],
+        [pltpu.SemaphoreType.DMA((2,))],
+        0,
+        "halved",
+        loose_in=(0, 1),
+        loose_out=(0, 1),
+    )
+
+
 def expanded_bias(level_bias):
     levels = level_bias.shape[1]
     table = (level_bias * LOG2E).reshape(PAIRS, 2, levels, levels).transpose(0, 3, 1, 2)
@@ -363,17 +387,17 @@
     )
 
 
-def run_arrived(distance, devices, fixed, block, gain, wk, wv, q, state, after):
-    _, wide, tall, kept, work = sizes(*block.shape)
+def run_arrived(distance, devices, fixed, blocks, gain, wk, wv, q, state, after):
+    _, wide, tall, kept, work = sizes(*q.shape[::-1])
     return call(
-        functools.partial(arrived_kernel, distance, devices),
+        functools.partial(arrived_kernel, distance, devices, len(blocks)),
         fixed,
-        [block, gain, wk, wv, q, *state, after],
+        [*blocks, gain, wk, wv, q, *state, after],
         [*kept, MARK],
         [tall, wide],
         work // 4,
         "arrived",
-        loose_in=(8,),
+        loose_in=(len(blocks) + 7,),
     )
 
 
@@ -443,10 +467,9 @@
     q, *state, wk, wv, again = run_own(patch_bias, hidden, wq_p, keys_patch, wv_p, gain)
     from_inner = moved(again, inner)
     fixed = [place, neighbours, counts, patch_bias]
-    *state, mark = run_arrived(1, devices, fixed, from_twin, gain, wk, wv, q, state, jnp.zeros(*MARK))
-    from_outer, mark = lax.optimization_barrier((from_outer, mark))
-    passed_on = moved(from_outer, twin)
-    *state, mark = run_arrived(2, devices, fixed, from_outer, gain, wk, wv, q, state, mark)
+    *state, mark = run_arrived(1, devices, fixed, [from_twin], gain, wk, wv, q, state, jnp.zeros(*MARK))
+    passed_on = [moved(half, twin) for half in halved(from_outer, mark)]
+    *state, mark = run_arrived(2, devices, fixed, [from_outer], gain, wk, wv, q, state, mark)
     *state, _ = run_arrived(-1, devices, fixed, passed_on, gain, wk, wv, q, state, mark)
     mix, keep, give = run_last(
         -2, devices, fixed, from_inner, gain, wk, wv, q, state, *kept_in_hbm(cotangent.reshape(columns, features))

time: 136 us -> 133 us (0.978)
  waiting for transfers between devices: 22.9 us -> 19.4 us
    ppermute x5 -> x6, waiting for transfers between devices: 3.54 us -> 0.02 us  [moved(): lax.ppermute(value, 'space', [(source_of(d) % devices, d) for d in range(...]
    ppermute x5 -> x6, starting transfers between devices: 10.1 us -> 9.02 us  [moved(): lax.ppermute(value, 'space', [(source_of(d) % devices, d) for d in range(...]
    pallas_call x6 -> x7, Pallas kernels: 30.3 us -> 30.7 us  [call(): pl.pallas_call(kernel, out_shape=shapes, in_specs=[IN_SMEM] * len(scalars...]
  transfers between devices with their start and end apart: 6 -> 7, of which waited for: 3 -> 1; matrix products, arithmetic and copies ran while one was open for 2% -> 2% of each run, Pallas kernels for 16% -> 17%
where the time goes in v5:
time: 133 us; the launch traced here: 132 us
  blocking collectives  56.1 us (42%)
  Pallas kernels  34.6 us (26%)
  waiting for transfers between devices  19.4 us (15%)
  starting transfers between devices  18.2 us (14%)
  matrix products  1.69 us (1%)
    pallas_call x7, Pallas kernels, call(): pl.pallas_call(kernel, out_shape=shapes, in_specs=[IN_SMEM] * len(scalars...  30.7 us
    all_to_all x1, blocking collectives, body(): lax.all_to_all(hidden, 'level', 0, 0, tiled=True).reshape(columns, features)  25.6 us
    all_to_all x1, waiting for transfers between devices, body(): lax.all_to_all(fields.reshape(levels, share, features), 'level', 0, 0, ti...  19.4 us
    all_to_all x1, blocking collectives, body(): lax.all_to_all(summed, 'space', 0, 0, axis_index_groups=same_core, tiled=...  17.7 us
    all_to_all x1, blocking collectives, body(): lax.all_to_all(spread, 'level', 0, 0, tiled=True).astype(F32).sum(axis=0)  12.8 us
    all_to_all x1, starting transfers between devices, body(): lax.all_to_all(fields.reshape(levels, share, features), 'level', 0, 0, ti...  9.16 us
    ppermute x6, starting transfers between devices, moved(): lax.ppermute(value, 'space', [(source_of(d) % devices, d) for d in range(...  9.02 us
    pallas_call x1, Pallas kernels, turned(): pl.pallas_call(turning_kernel, out_shape=[jax.ShapeDtypeStruct(shape, BF)...  3.84 us
  transfers between devices with their start and end apart: 7, of which 1 were waited for; matrix products, arithmetic and copies ran while one was open for 2% of the time, Pallas kernels for 17%

profile of v5, /device:TPU:1, one launch (start us, length us, event | category | flops | bytes accessed | tf_op | source)
XLA Modules:
  0.0 132.1 jit_solution(1300658343823269070)
XLA Ops:
  0.6 9.2 %all-to-all-start = ((bf16[8,64,768]{2,1,0:T(8,128)(2,1)}), bf16[8,64,768]{2,1,0:T(8,128)(2,1)S(1)}, u32[]{:S(2)}, u32[]{:S(2)}) async-start(bf16[8,64,768]{2,1,0:T(8,128)(2,1)} %bitcast.17), calls=%async_computation | async-start | bytes 1572864 | tf_op jit(solution)/shard_map/all_to_all | solution.py:451
  9.8 0.1 copy.31
  10.2 3.8 %turned.1 = (bf16[768,768]{1,0:T(8,128)(2,1)}, bf16[768,768]{1,0:T(8,128)(2,1)}, bf16[768,768]{1,0:T(8,128)(2,1)}, bf16[768,768]{1,0:T(8,128)(2,1)}) custom-call(bf16[768,768]{1,0:T(8,128)(2,1)} %refs_0_.1, bf16[768,768]{1,0:T(8,128)(2,1)} %refs_1_.1, bf16[768,768]{1,0:T(8,128)(2,1)} %refs_2_.1, bf16[768,768]{1,0:T(8,128)(2,1)} %refs_3_.1), custom_call_target="tpu_custom_call" | custom-call | bytes 20971520 | tf_op jit(solution)/shard_map/turned/pallas_call | solution.py:282
  14.0 19.4 %all-to-all-done.x = bf16[8,64,768]{2,1,0:T(8,128)(2,1)S(1)} async-done(((bf16[8,64,768]{2,1,0:T(8,128)(2,1)}), bf16[8,64,768]{2,1,0:T(8,128)(2,1)S(1)}, u32[]{:S(2)}, u32[]{:S(2)}) %all-to-all-start) | async-done | bytes 786464 | tf_op jit(solution)/shard_map/all_to_all | solution.py:451
  33.4 6.4 %vertical.1 = bf16[8,64,768]{2,1,0:T(8,128)(2,1)S(1)} custom-call(s32[1]{0:T(128)} %bitcast._.place, bf16[8,64,768]{2,1,0:T(8,128)(2,1)S(1)} %all-to-all-done.x, bf16[768,768]{1,0:T(8,128)(2,1)} %get-tuple-element.31.wq_in, bf16[768,768]{1,0:T(8,128)(2,1)} %wk_in.2, bf16[768,768]{1,0:T(8,128)(2,1)} %get-tuple-element.32.wv_in, bf16[768,768]{1,0:T(8,128)(2,1)} %wo_in.1, ...), custom_call_target="tpu_custom_call" | custom-call | flops 3019898880 | bytes 11796480 | tf_op jit(solution)/shard_map/vertical/pallas_call | solution.py:302
  39.8 25.6 %all_to_all.20 = bf16[8,64,768]{2,1,0:T(8,128)(2,1)S(1)} all-to-all(bf16[8,64,768]{2,1,0:T(8,128)(2,1)S(1)} %vertical.1), channel_id=1, replica_groups=mesh['space'=32,'level'=8] {'level'}, dimensions={0} | all-to-all | bytes 1572864 | tf_op jit(solution)/shard_map/all_to_all | solution.py:453
  65.5 0.8 collective-permute-start.2
  66.3 1.3 collective-permute-start.1
  67.6 0.1 copy.38.pbias
  67.8 6.0 %own.1 = (bf16[768,512]{1,0:T(8,128)(2,1)S(1)}, f32[768,512]{1,0:T(8,128)S(1)}, f32[12,512]{1,0:T(8,128)S(1)}, f32[12,512]{1,0:T(8,128)S(1)}, bf16[768,768]{1,0:...) custom-call(f32[12,2]{1,0:T(8,128)S(1)} %copy.38.pbias, bf16[512,768]{1,0:T(8,128)(2,1)S(1)} %bitcast.15, ...), custom_call_target="tpu_custom_call" | custom-call | flops 2415919104 | bytes 9437184 | tf_op jit(solution)/shard_map/own/pallas_call | solution.py:302
  73.8 3.9 %collective-permute-start = (bf16[512,768]{1,0:T(8,128)(2,1)S(1)}, bf16[512,768]{1,0:T(8,128)(2,1)S(1)}, u32[]{:S(2)}, u32[]{:S(2)}) collective-permute-start(bf16[512,768]{1,0:T(8,128)(2,1)S(1)} %get-tuple-element.35), channel_id=1, source_target_pairs={{240,0},{24,8},{0,16},{40,24},{16,32},{56,40},{32,48},{72,56},{48,... | collective-permute-start | bytes 2359304 | tf_op jit(solution)/shard_map/ppermute | solution.py:447
  77.7 4.0 %arrived.3 = (f32[768,512]{1,0:T(8,128)S(1)}, f32[12,512]{1,0:T(8,128)S(1)}, f32[12,512]{1,0:T(8,128)S(1)}, f32[8,128]{1,0:T(8,128)S(1)}) custom-call(s32[1]{0:T(128)} %bitcast._.place, s32[2,4]{1,0:T(2,128)S(1)} %copy-done, s32[2]{0:T(128)S(1)} %copy-done.1, f32[12,2]{1,0:T(8,128)S(1)} %copy.38.pbias, bf16[512,768]{1,0:T(8,128)(2,1)S(1)} %collective-permute-done.2.refs_0_, ...), custom_call_target="tpu_custom_call" | custom-call | flops 75497472 | bytes 294912 | tf_op jit(solution)/shard_map/arrived/pallas_call | solution.py:302
  81.6 0.4 halved.1
  82.0 1.9 %collective-permute-start.3 = (bf16[256,768]{1,0:T(8,128)(2,1)S(1)}, bf16[256,768]{1,0:T(8,128)(2,1)S(1)}, u32[]{:S(2)}, u32[]{:S(2)}) collective-permute-start(bf16[256,768]{1,0:T(8,128)(2,1)S(1)} %get-tuple-element.43), channel_id=1, source_target_pairs={{8,0},{0,8},{24,16},{16,24},{40,32},{32,40},{56,48},{48,56},{72,64... | collective-permute-start | bytes 1179656 | tf_op jit(solution)/shard_map/ppermute | solution.py:447
  83.9 0.1 collective-permute-start.4
  84.0 4.0 %arrived.4 = (f32[768,512]{1,0:T(8,128)S(1)}, f32[12,512]{1,0:T(8,128)S(1)}, f32[12,512]{1,0:T(8,128)S(1)}, f32[8,128]{1,0:T(8,128)S(1)}) custom-call(s32[1]{0:T(128)} %bitcast._.place, s32[2,4]{1,0:T(2,128)S(1)} %copy-done, s32[2]{0:T(128)S(1)} %copy-done.1, f32[12,2]{1,0:T(8,128)S(1)} %copy.38.pbias, ...), custom_call_target="tpu_custom_call" | custom-call | flops 75497472 | bytes 294912 | tf_op jit(solution)/shard_map/arrived/pallas_call | solution.py:302
  88.0 4.3 %arrived.5 = (f32[768,512]{1,0:T(8,128)S(1)}, f32[12,512]{1,0:T(8,128)S(1)}, f32[12,512]{1,0:T(8,128)S(1)}, f32[8,128]{1,0:T(8,128)}) custom-call(s32[1]{0:T(128)} %bitcast._.place, s32[2,4]{1,0:T(2,128)S(1)} %copy-done, s32[2]{0:T(128)S(1)} %copy-done.1, f32[12,2]{1,0:T(8,128)S(1)} %copy.38.pbias, bf16[256,768]{1,0:T(8,128)(2,1)S(1)} %collective-permute-done.3.refs_0_, ...), custom_call_target="tpu_custom_call" | custom-call | flops 75497472 | bytes 294912 | tf_op jit(solution)/shard_map/arrived/pallas_call | solution.py:302
  92.3 5.7 %last.1 = (bf16[768,512]{1,0:T(8,128)(2,1)S(1)}, f32[16,24,768]{2,1,0:T(8,128)S(1)}, bf16[16,24,768]{2,1,0:T(8,128)(2,1)S(1)}) custom-call(s32[1]{0:T(128)} %bitcast._.place, s32[2,4]{1,0:T(2,128)S(1)} %copy-done, s32[2]{0:T(128)S(1)} %copy-done.1, f32[12,2]{1,0:T(8,128)S(1)} %copy.38.pbias, bf16[512,768]{1,0:T(8,128)(2,1)S(1)} %collective-permute-done.x, ...), custom_call_target="tpu_custom_call" | custom-call | flops 2415919104 | bytes 9437184 | tf_op jit(solution)/shard_map/last/pallas_call | solution.py:302
  98.0 1.0 collective-permute-start.5
  99.0 1.7 %add_convert_fusion = bf16[512,768]{1,0:T(8,128)(2,1)} fusion(bf16[512,768]{1,0:T(8,128)(2,1)S(1)} %bitcast.16, bf16[768,512]{1,0:T(8,128)(2,1)S(1)} %get-tuple-element.56, bf16[768,768]{1,0:T(8,128)(2,1)S(1)} %copy-done.6), kind=kOutput, calls=%fused_computation | convolution fusion | flops 605159424 | bytes 3538944 | tf_op jit(solution)/shard_map/dot_general | solution.py:478
  100.7 0.1 add_convert_fusion.1
  100.8 17.7 %all_to_all.21 = bf16[16,24,768]{2,1,0:T(8,128)(2,1)S(1)} all-to-all(bf16[16,24,768]{2,1,0:T(8,128)(2,1)S(1)} %add_convert_fusion.1), channel_id=1, replica_groups={{0,16,32,48,64,80,96,112,128,144,160,176,192,208,224,240},{8,24,40,56,7..., dimensions={0} | all-to-all | bytes 1179648 | tf_op jit(solution)/shard_map/all_to_all | solution.py:483
  118.7 12.8 %all_to_all.22 = bf16[8,24,768]{2,1,0:T(8,128)(2,1)S(1)} all-to-all(bf16[8,24,768]{2,1,0:T(8,128)(2,1)S(1)} %broadcast_in_dim.30), channel_id=1, replica_groups=mesh['space'=32,'level'=8] {'level'}, dimensions={0} | all-to-all | bytes 589824 | tf_op jit(solution)/shard_map/all_to_all | solution.py:486
  131.5 0.7 convert_reduce_fusion
  (30 shorter events, 0.4 us)
Async XLA Ops:
  0.6 9.2 %copy-start.2 = (f32[12,8,8]{0,2,1:T(8,128)S(1)}, f32[12,8,8]{0,2,1:T(8,128)}, u32[]{:S(2)}) copy-start(f32[12,8,8]{0,2,1:T(8,128)} %param.22) | copy-start | bytes 9220
  0.6 9.5 %copy-start.3 = (f32[768]{0:T(1024)S(1)}, f32[768]{0:T(1024)}, u32[]{:S(2)}) copy-start(f32[768]{0:T(1024)} %param.17) | copy-start | bytes 9220
  0.6 32.7 %all-to-all-start = ((bf16[8,64,768]{2,1,0:T(8,128)(2,1)}), bf16[8,64,768]{2,1,0:T(8,128)(2,1)S(1)}, u32[]{:S(2)}, u32[]{:S(2)}) async-start(bf16[8,64,768]{2,1,0:T(8,128)(2,1)} %bitcast.17), calls=%async_computation | async-start | bytes 1572864 | tf_op jit(solution)/shard_map/all_to_all | solution.py:451
  39.8 27.8 %copy-start.5 = (f32[12,2]{0,1:T(2,128)S(1)}, f32[12,2]{0,1:T(2,128)}, u32[]{:S(2)}) copy-start(f32[12,2]{0,1:T(2,128)} %param.28) | copy-start | bytes 292
  39.8 27.9 %copy-start.4 = (f32[768]{0:T(1024)S(1)}, f32[768]{0:T(1024)}, u32[]{:S(2)}) copy-start(f32[768]{0:T(1024)} %param.23) | copy-start | bytes 9220
  65.5 12.2 %collective-permute-start.2 = (bf16[512,768]{1,0:T(8,128)(2,1)S(1)}, bf16[512,768]{1,0:T(8,128)(2,1)S(1)}, u32[]{:S(2)}, u32[]{:S(2)}) collective-permute-start(bf16[512,768]{1,0:T(8,128)(2,1)S(1)} %bitcast.13), channel_id=1, source_target_pairs={{8,0},{0,8},{24,16},{16,24},{40,32},{32,40},{56,48},{48,56},{72,64... | collective-permute-start | bytes 2359304 | tf_op jit(solution)/shard_map/ppermute | solution.py:447
  66.3 15.3 %collective-permute-start.1 = (bf16[512,768]{1,0:T(8,128)(2,1)S(1)}, bf16[512,768]{1,0:T(8,128)(2,1)S(1)}, u32[]{:S(2)}, u32[]{:S(2)}) collective-permute-start(bf16[512,768]{1,0:T(8,128)(2,1)S(1)} %bitcast.14), channel_id=1, source_target_pairs={{16,0},{248,8},{32,16},{8,24},{48,32},{24,40},{64,48},{40,56},{80,... | collective-permute-start | bytes 2359304 | tf_op jit(solution)/shard_map/ppermute | solution.py:447
  67.7 9.9 %copy-start = (s32[2,4]{1,0:T(2,128)S(1)}, s32[2,4]{1,0:T(2,128)}, u32[]{:S(2)}) copy-start(s32[2,4]{1,0:T(2,128)} %near.7) | copy-start | bytes 100
  67.7 9.9 %copy-start.1 = (s32[2]{0:T(128)S(1)}, s32[2]{0:T(128)}, u32[]{:S(2)}) copy-start(s32[2]{0:T(128)} %live.7) | copy-start | bytes 28
  73.8 18.6 %collective-permute-start = (bf16[512,768]{1,0:T(8,128)(2,1)S(1)}, bf16[512,768]{1,0:T(8,128)(2,1)S(1)}, u32[]{:S(2)}, u32[]{:S(2)}) collective-permute-start(bf16[512,768]{1,0:T(8,128)(2,1)S(1)} %get-tuple-element.35), channel_id=1, source_target_pairs={{240,0},{24,8},{0,16},{40,24},{16,32},{56,40},{32,48},{72,56},{48,... | collective-permute-start | bytes 2359304 | tf_op jit(solution)/shard_map/ppermute | solution.py:447
  82.0 6.0 %collective-permute-start.3 = (bf16[256,768]{1,0:T(8,128)(2,1)S(1)}, bf16[256,768]{1,0:T(8,128)(2,1)S(1)}, u32[]{:S(2)}, u32[]{:S(2)}) collective-permute-start(bf16[256,768]{1,0:T(8,128)(2,1)S(1)} %get-tuple-element.43), channel_id=1, source_target_pairs={{8,0},{0,8},{24,16},{16,24},{40,32},{32,40},{56,48},{48,56},{72,64... | collective-permute-start | bytes 1179656 | tf_op jit(solution)/shard_map/ppermute | solution.py:447
  83.9 4.1 %collective-permute-start.4 = (bf16[256,768]{1,0:T(8,128)(2,1)S(1)}, bf16[256,768]{1,0:T(8,128)(2,1)S(1)}, u32[]{:S(2)}, u32[]{:S(2)}) collective-permute-start(bf16[256,768]{1,0:T(8,128)(2,1)S(1)} %get-tuple-element.44), channel_id=1, source_target_pairs={{8,0},{0,8},{24,16},{16,24},{40,32},{32,40},{56,48},{48,56},{72,64... | collective-permute-start | bytes 1179656 | tf_op jit(solution)/shard_map/ppermute | solution.py:447
  92.3 6.7 %copy-start.6 = (bf16[768,768]{1,0:T(8,128)(2,1)S(1)}, bf16[768,768]{1,0:T(8,128)(2,1)}, u32[]{:S(2)}) copy-start(bf16[768,768]{1,0:T(8,128)(2,1)} %param.27) | copy-start | bytes 3538948
  98.0 2.7 %collective-permute-start.5 = (bf16[16,24,768]{2,1,0:T(8,128)(2,1)S(1)}, bf16[16,24,768]{2,1,0:T(8,128)(2,1)S(1)}, u32[]{:S(2)}, u32[]{:S(2)}) collective-permute-start(bf16[16,24,768]{2,1,0:T(8,128)(2,1)S(1)} %get-tuple-element.55), channel_id=1, source_target_pairs={{8,0},{0,8},{24,16},{16,24},{40,32},{32,40},{56,48},{48,56},{72,64... | collective-permute-start | bytes 1769480 | tf_op jit(solution)/shard_map/ppermute | solution.py:447

commit v6 on v5

--- a/solution.py
+++ b/solution.py
@@ -11,6 +11,8 @@
 HD = 64
 PATCH = 256
 PAIRS = H // 2
+TEAM = 4
+TEAMS = H // TEAM
 GROUP = 16
 LOG2E = 1.4426950408889634
 epsilon = 1e-06
@@ -34,11 +36,14 @@
     return (widened * lax.rsqrt(mean_square + epsilon) * gain).astype(BF)
 
 
-def paired(two_heads):
-    zero = jnp.zeros((HD, two_heads.shape[1]), BF)
-    top = jnp.concatenate((two_heads[:HD], zero), axis=1)
-    low = jnp.concatenate((zero, two_heads[HD:]), axis=1)
-    return jnp.concatenate((top, low), axis=0)
+def paired(queries):
+    heads = queries.shape[0] // HD
+    zero = jnp.zeros((HD, queries.shape[1]), BF)
+    rows = []
+    for head in range(heads):
+        own = queries[head * HD : (head + 1) * HD]
+        rows.append(jnp.concatenate([own if other == head else zero for other in range(heads)], axis=1))
+    return jnp.concatenate(rows, axis=0)
 
 
 def mixed(values, weights):
@@ -75,13 +80,13 @@
     copies = fetched([(wq_in, wq), (wk_in, wk), (wv_in, wv), (wo_in, wo)], arrivals)
     tokens = levels * columns
     block = levels * GROUP
-    key_column = lax.broadcasted_iota(jnp.int32, (GROUP, 2 * block), 0)
-    query_column = lax.broadcasted_iota(jnp.int32, (GROUP, 2 * block), 1) % GROUP
+    key_column = lax.broadcasted_iota(jnp.int32, (GROUP, TEAM * block), 0)
+    query_column = lax.broadcasted_iota(jnp.int32, (GROUP, TEAM * block), 1) % GROUP
     same = key_column == query_column
-    for pair in range(PAIRS):
+    for team in range(TEAMS):
         for level in range(levels):
-            row = rows_of_bias[pair * levels + level : pair * levels + level + 1]
-            bias[pair, level * GROUP : (level + 1) * GROUP] = jnp.where(same, row, -jnp.inf)
+            row = rows_of_bias[team * levels + level : team * levels + level + 1]
+            bias[team, level * GROUP : (level + 1) * GROUP] = jnp.where(same, row, -jnp.inf)
     for level in range(levels):
         rows = normalize(x[level], gain[...])
         for part in range(columns // GROUP):
@@ -97,19 +102,19 @@
     copies[2].wait()
     for span in spans:
         v[:, span] = nt(wv[...], normed[span]).astype(BF)
-    steps = [(part, pair) for part in range(columns // GROUP) for pair in range(PAIRS)]
-
-    def step_scores(part, pair):
-        span, heads = slice(part * block, (part + 1) * block), slice(pair * 128, (pair + 1) * 128)
-        return nn(k[span, heads], paired(q[heads, span])) + bias[pair]
-
-    def step_weights(scores, part, pair):
+    steps = [(part, team) for part in range(columns // GROUP) for team in range(TEAMS)]
+
+    def step_scores(part, team):
+        span, heads = slice(part * block, (part + 1) * block), slice(team * TEAM * HD, (team + 1) * TEAM * HD)
+        return nn(k[span, heads], paired(q[heads, span])) + bias[team]
+
+    def step_weights(scores, part, team):
         return jnp.exp2(scores - jnp.max(scores, axis=0, keepdims=True)).astype(BF)
 
-    def step_mix(weights, part, pair):
+    def step_mix(weights, part, team):
         span = slice(part * block, (part + 1) * block)
-        for half in range(2):
-            head = slice(pair * 128 + half * HD, pair * 128 + half * HD + HD)
+        for half in range(TEAM):
+            head = slice((team * TEAM + half) * HD, (team * TEAM + half + 1) * HD)
             total = mixed(v[head, span], weights[:, half * block : (half + 1) * block])
             mix[head, span] = (total[:HD] / total[HD : HD + 1]).astype(BF)
 
@@ -334,8 +339,8 @@
 
 def expanded_bias(level_bias):
     levels = level_bias.shape[1]
-    table = (level_bias * LOG2E).reshape(PAIRS, 2, levels, levels).transpose(0, 3, 1, 2)
-    return jnp.repeat(table.reshape(PAIRS * levels, 2 * levels), GROUP, axis=1)
+    table = (level_bias * LOG2E).reshape(TEAMS, TEAM, levels, levels).transpose(0, 3, 1, 2)
+    return jnp.repeat(table.reshape(TEAMS * levels, TEAM * levels), GROUP, axis=1)
 
 
 MARK = ((8, 128), F32)
@@ -362,7 +367,7 @@
             tall,
             wide,
             wide,
-            ((PAIRS, levels * GROUP, 2 * levels * GROUP), F32),
+            ((TEAMS, levels * GROUP, TEAM * levels * GROUP), F32),
             *([weights] * 4),
             pltpu.SemaphoreType.DMA((4,)),
         ],

time: 133 us -> 132 us (level)
  no operation moved by 1% of the time
where the time goes in v6:
time: 132 us; the launch traced here: 131 us
  blocking collectives  56.4 us (43%)
  Pallas kernels  33.9 us (26%)
  waiting for transfers between devices  19 us (14%)
  starting transfers between devices  17.9 us (14%)
  matrix products  1.69 us (1%)
    pallas_call x7, Pallas kernels, call(): pl.pallas_call(kernel, out_shape=shapes, in_specs=[IN_SMEM] * len(scalars...  30.1 us
    all_to_all x1, blocking collectives, body(): lax.all_to_all(hidden, 'level', 0, 0, tiled=True).reshape(columns, features)  25.9 us
    all_to_all x1, waiting for transfers between devices, body(): lax.all_to_all(fields.reshape(levels, share, features), 'level', 0, 0, ti...  19 us
    all_to_all x1, blocking collectives, body(): lax.all_to_all(summed, 'space', 0, 0, axis_index_groups=same_core, tiled=...  17.7 us
    all_to_all x1, blocking collectives, body(): lax.all_to_all(spread, 'level', 0, 0, tiled=True).astype(F32).sum(axis=0)  12.8 us
    all_to_all x1, starting transfers between devices, body(): lax.all_to_all(fields.reshape(levels, share, features), 'level', 0, 0, ti...  9.16 us
    ppermute x6, starting transfers between devices, moved(): lax.ppermute(value, 'space', [(source_of(d) % devices, d) for d in range(...  8.76 us
    pallas_call x1, Pallas kernels, turned(): pl.pallas_call(turning_kernel, out_shape=[jax.ShapeDtypeStruct(shape, BF)...  3.84 us
  transfers between devices with their start and end apart: 7, of which 1 were waited for; matrix products, arithmetic and copies ran while one was open for 2% of the time, Pallas kernels for 17%

profile of v6, /device:TPU:1, one launch (start us, length us, event | category | flops | bytes accessed | tf_op | source)
XLA Modules:
  0.0 131.5 jit_solution(10784828406953716247)
XLA Ops:
  0.6 9.2 %all-to-all-start = ((bf16[8,64,768]{2,1,0:T(8,128)(2,1)}), bf16[8,64,768]{2,1,0:T(8,128)(2,1)S(1)}, u32[]{:S(2)}, u32[]{:S(2)}) async-start(bf16[8,64,768]{2,1,0:T(8,128)(2,1)} %bitcast.14), calls=%async_computation | async-start | bytes 1572864 | tf_op jit(solution)/shard_map/all_to_all | solution.py:456
  9.8 0.1 copy.30
  10.1 0.2 broadcast_in_dim.26
  10.3 0.2 reshape.26.rows_of_bias
  10.5 3.8 %turned.1 = (bf16[768,768]{1,0:T(8,128)(2,1)}, bf16[768,768]{1,0:T(8,128)(2,1)}, bf16[768,768]{1,0:T(8,128)(2,1)}, bf16[768,768]{1,0:T(8,128)(2,1)}) custom-call(bf16[768,768]{1,0:T(8,128)(2,1)} %refs_0_.1, bf16[768,768]{1,0:T(8,128)(2,1)} %refs_1_.1, bf16[768,768]{1,0:T(8,128)(2,1)} %refs_2_.1, bf16[768,768]{1,0:T(8,128)(2,1)} %refs_3_.1), custom_call_target="tpu_custom_call" | custom-call | bytes 20971520 | tf_op jit(solution)/shard_map/turned/pallas_call | solution.py:287
  14.4 19.0 %all-to-all-done.x = bf16[8,64,768]{2,1,0:T(8,128)(2,1)S(1)} async-done(((bf16[8,64,768]{2,1,0:T(8,128)(2,1)}), bf16[8,64,768]{2,1,0:T(8,128)(2,1)S(1)}, u32[]{:S(2)}, u32[]{:S(2)}) %all-to-all-start) | async-done | bytes 786464 | tf_op jit(solution)/shard_map/all_to_all | solution.py:456
  33.4 5.8 %vertical.1 = bf16[8,64,768]{2,1,0:T(8,128)(2,1)S(1)} custom-call(s32[1]{0:T(128)} %bitcast._.place, bf16[8,64,768]{2,1,0:T(8,128)(2,1)S(1)} %all-to-all-done.x, bf16[768,768]{1,0:T(8,128)(2,1)} %get-tuple-element.31.wq_in, bf16[768,768]{1,0:T(8,128)(2,1)} %wk_in.2, bf16[768,768]{1,0:T(8,128)(2,1)} %get-tuple-element.32.wv_in, bf16[768,768]{1,0:T(8,128)(2,1)} %wo_in.1, ...), custom_call_target="tpu_custom_call" | custom-call | flops 3019898880 | bytes 11796480 | tf_op jit(solution)/shard_map/vertical/pallas_call | solution.py:307
  39.2 25.9 %all_to_all.20 = bf16[8,64,768]{2,1,0:T(8,128)(2,1)S(1)} all-to-all(bf16[8,64,768]{2,1,0:T(8,128)(2,1)S(1)} %vertical.1), channel_id=1, replica_groups=mesh['space'=32,'level'=8] {'level'}, dimensions={0} | all-to-all | bytes 1572864 | tf_op jit(solution)/shard_map/all_to_all | solution.py:458
  65.1 0.6 collective-permute-start.2
  65.7 1.3 collective-permute-start.1
  67.1 6.0 %own.1 = (bf16[768,512]{1,0:T(8,128)(2,1)S(1)}, f32[768,512]{1,0:T(8,128)S(1)}, f32[12,512]{1,0:T(8,128)S(1)}, f32[12,512]{1,0:T(8,128)S(1)}, bf16[768,768]{1,0:...) custom-call(f32[12,2]{1,0:T(8,128)S(1)} %copy.36.pbias, bf16[512,768]{1,0:T(8,128)(2,1)S(1)} %bitcast.12, ...), custom_call_target="tpu_custom_call" | custom-call | flops 2415919104 | bytes 9437184 | tf_op jit(solution)/shard_map/own/pallas_call | solution.py:307
  73.1 3.9 %collective-permute-start = (bf16[512,768]{1,0:T(8,128)(2,1)S(1)}, bf16[512,768]{1,0:T(8,128)(2,1)S(1)}, u32[]{:S(2)}, u32[]{:S(2)}) collective-permute-start(bf16[512,768]{1,0:T(8,128)(2,1)S(1)} %get-tuple-element.35), channel_id=1, source_target_pairs={{240,0},{24,8},{0,16},{40,24},{16,32},{56,40},{32,48},{72,56},{48,... | collective-permute-start | bytes 2359304 | tf_op jit(solution)/shard_map/ppermute | solution.py:452
  77.0 4.0 %arrived.3 = (f32[768,512]{1,0:T(8,128)S(1)}, f32[12,512]{1,0:T(8,128)S(1)}, f32[12,512]{1,0:T(8,128)S(1)}, f32[8,128]{1,0:T(8,128)S(1)}) custom-call(s32[1]{0:T(128)} %bitcast._.place, s32[2,4]{1,0:T(2,128)S(1)} %copy-done, s32[2]{0:T(128)S(1)} %copy-done.1, f32[12,2]{1,0:T(8,128)S(1)} %copy.36.pbias, bf16[512,768]{1,0:T(8,128)(2,1)S(1)} %collective-permute-done.2.refs_0_, ...), custom_call_target="tpu_custom_call" | custom-call | flops 75497472 | bytes 294912 | tf_op jit(solution)/shard_map/arrived/pallas_call | solution.py:307
  81.0 0.4 halved.1
  81.4 1.9 %collective-permute-start.3 = (bf16[256,768]{1,0:T(8,128)(2,1)S(1)}, bf16[256,768]{1,0:T(8,128)(2,1)S(1)}, u32[]{:S(2)}, u32[]{:S(2)}) collective-permute-start(bf16[256,768]{1,0:T(8,128)(2,1)S(1)} %get-tuple-element.43), channel_id=1, source_target_pairs={{8,0},{0,8},{24,16},{16,24},{40,32},{32,40},{56,48},{48,56},{72,64... | collective-permute-start | bytes 1179656 | tf_op jit(solution)/shard_map/ppermute | solution.py:452
  83.4 4.0 %arrived.4 = (f32[768,512]{1,0:T(8,128)S(1)}, f32[12,512]{1,0:T(8,128)S(1)}, f32[12,512]{1,0:T(8,128)S(1)}, f32[8,128]{1,0:T(8,128)S(1)}) custom-call(s32[1]{0:T(128)} %bitcast._.place, s32[2,4]{1,0:T(2,128)S(1)} %copy-done, s32[2]{0:T(128)S(1)} %copy-done.1, f32[12,2]{1,0:T(8,128)S(1)} %copy.36.pbias, ...), custom_call_target="tpu_custom_call" | custom-call | flops 75497472 | bytes 294912 | tf_op jit(solution)/shard_map/arrived/pallas_call | solution.py:307
  87.4 4.3 %arrived.5 = (f32[768,512]{1,0:T(8,128)S(1)}, f32[12,512]{1,0:T(8,128)S(1)}, f32[12,512]{1,0:T(8,128)S(1)}, f32[8,128]{1,0:T(8,128)}) custom-call(s32[1]{0:T(128)} %bitcast._.place, s32[2,4]{1,0:T(2,128)S(1)} %copy-done, s32[2]{0:T(128)S(1)} %copy-done.1, f32[12,2]{1,0:T(8,128)S(1)} %copy.36.pbias, bf16[256,768]{1,0:T(8,128)(2,1)S(1)} %collective-permute-done.3.refs_0_, ...), custom_call_target="tpu_custom_call" | custom-call | flops 75497472 | bytes 294912 | tf_op jit(solution)/shard_map/arrived/pallas_call | solution.py:307
  91.7 5.7 %last.1 = (bf16[768,512]{1,0:T(8,128)(2,1)S(1)}, f32[16,24,768]{2,1,0:T(8,128)S(1)}, bf16[16,24,768]{2,1,0:T(8,128)(2,1)S(1)}) custom-call(s32[1]{0:T(128)} %bitcast._.place, s32[2,4]{1,0:T(2,128)S(1)} %copy-done, s32[2]{0:T(128)S(1)} %copy-done.1, f32[12,2]{1,0:T(8,128)S(1)} %copy.36.pbias, bf16[512,768]{1,0:T(8,128)(2,1)S(1)} %collective-permute-done.x, ...), custom_call_target="tpu_custom_call" | custom-call | flops 2415919104 | bytes 9437184 | tf_op jit(solution)/shard_map/last/pallas_call | solution.py:307
  97.4 1.0 collective-permute-start.5
  98.4 1.7 %add_convert_fusion = bf16[512,768]{1,0:T(8,128)(2,1)} fusion(bf16[512,768]{1,0:T(8,128)(2,1)S(1)} %bitcast.13, bf16[768,512]{1,0:T(8,128)(2,1)S(1)} %get-tuple-element.56, bf16[768,768]{1,0:T(8,128)(2,1)S(1)} %copy-done.6), kind=kOutput, calls=%fused_computation | convolution fusion | flops 605159424 | bytes 3538944 | tf_op jit(solution)/shard_map/dot_general | solution.py:483
  100.1 0.1 add_convert_fusion.1
  100.2 17.7 %all_to_all.21 = bf16[16,24,768]{2,1,0:T(8,128)(2,1)S(1)} all-to-all(bf16[16,24,768]{2,1,0:T(8,128)(2,1)S(1)} %add_convert_fusion.1), channel_id=1, replica_groups={{0,16,32,48,64,80,96,112,128,144,160,176,192,208,224,240},{8,24,40,56,7..., dimensions={0} | all-to-all | bytes 1179648 | tf_op jit(solution)/shard_map/all_to_all | solution.py:488
  118.0 12.8 %all_to_all.22 = bf16[8,24,768]{2,1,0:T(8,128)(2,1)S(1)} all-to-all(bf16[8,24,768]{2,1,0:T(8,128)(2,1)S(1)} %broadcast_in_dim.30), channel_id=1, replica_groups=mesh['space'=32,'level'=8] {'level'}, dimensions={0} | all-to-all | bytes 589824 | tf_op jit(solution)/shard_map/all_to_all | solution.py:491
  130.8 0.7 convert_reduce_fusion
  (30 shorter events, 0.5 us)
Async XLA Ops:
  0.6 9.2 %copy-start.2 = (f32[12,8,8]{0,2,1:T(8,128)S(1)}, f32[12,8,8]{0,2,1:T(8,128)}, u32[]{:S(2)}) copy-start(f32[12,8,8]{0,2,1:T(8,128)} %param.22) | copy-start | bytes 9220
  0.6 9.9 %copy-start.3 = (f32[768]{0:T(1024)S(1)}, f32[768]{0:T(1024)}, u32[]{:S(2)}) copy-start(f32[768]{0:T(1024)} %param.17) | copy-start | bytes 9220
  0.6 32.7 %all-to-all-start = ((bf16[8,64,768]{2,1,0:T(8,128)(2,1)}), bf16[8,64,768]{2,1,0:T(8,128)(2,1)S(1)}, u32[]{:S(2)}, u32[]{:S(2)}) async-start(bf16[8,64,768]{2,1,0:T(8,128)(2,1)} %bitcast.14), calls=%async_computation | async-start | bytes 1572864 | tf_op jit(solution)/shard_map/all_to_all | solution.py:456
  39.2 27.8 %copy-start.5 = (f32[12,2]{0,1:T(2,128)S(1)}, f32[12,2]{0,1:T(2,128)}, u32[]{:S(2)}) copy-start(f32[12,2]{0,1:T(2,128)} %param.28) | copy-start | bytes 292
  39.2 27.9 %copy-start.4 = (f32[768]{0:T(1024)S(1)}, f32[768]{0:T(1024)}, u32[]{:S(2)}) copy-start(f32[768]{0:T(1024)} %param.23) | copy-start | bytes 9220
  65.1 11.9 %collective-permute-start.2 = (bf16[512,768]{1,0:T(8,128)(2,1)S(1)}, bf16[512,768]{1,0:T(8,128)(2,1)S(1)}, u32[]{:S(2)}, u32[]{:S(2)}) collective-permute-start(bf16[512,768]{1,0:T(8,128)(2,1)S(1)} %bitcast.10), channel_id=1, source_target_pairs={{8,0},{0,8},{24,16},{16,24},{40,32},{32,40},{56,48},{48,56},{72,64... | collective-permute-start | bytes 2359304 | tf_op jit(solution)/shard_map/ppermute | solution.py:452
  65.7 15.3 %collective-permute-start.1 = (bf16[512,768]{1,0:T(8,128)(2,1)S(1)}, bf16[512,768]{1,0:T(8,128)(2,1)S(1)}, u32[]{:S(2)}, u32[]{:S(2)}) collective-permute-start(bf16[512,768]{1,0:T(8,128)(2,1)S(1)} %bitcast.11), channel_id=1, source_target_pairs={{16,0},{248,8},{32,16},{8,24},{48,32},{24,40},{64,48},{40,56},{80,... | collective-permute-start | bytes 2359304 | tf_op jit(solution)/shard_map/ppermute | solution.py:452
  67.1 9.9 %copy-start = (s32[2,4]{1,0:T(2,128)S(1)}, s32[2,4]{1,0:T(2,128)}, u32[]{:S(2)}) copy-start(s32[2,4]{1,0:T(2,128)} %near.7) | copy-start | bytes 100
  67.1 9.9 %copy-start.1 = (s32[2]{0:T(128)S(1)}, s32[2]{0:T(128)}, u32[]{:S(2)}) copy-start(s32[2]{0:T(128)} %live.7) | copy-start | bytes 28
  73.1 18.6 %collective-permute-start = (bf16[512,768]{1,0:T(8,128)(2,1)S(1)}, bf16[512,768]{1,0:T(8,128)(2,1)S(1)}, u32[]{:S(2)}, u32[]{:S(2)}) collective-permute-start(bf16[512,768]{1,0:T(8,128)(2,1)S(1)} %get-tuple-element.35), channel_id=1, source_target_pairs={{240,0},{24,8},{0,16},{40,24},{16,32},{56,40},{32,48},{72,56},{48,... | collective-permute-start | bytes 2359304 | tf_op jit(solution)/shard_map/ppermute | solution.py:452
  81.4 6.0 %collective-permute-start.3 = (bf16[256,768]{1,0:T(8,128)(2,1)S(1)}, bf16[256,768]{1,0:T(8,128)(2,1)S(1)}, u32[]{:S(2)}, u32[]{:S(2)}) collective-permute-start(bf16[256,768]{1,0:T(8,128)(2,1)S(1)} %get-tuple-element.43), channel_id=1, source_target_pairs={{8,0},{0,8},{24,16},{16,24},{40,32},{32,40},{56,48},{48,56},{72,64... | collective-permute-start | bytes 1179656 | tf_op jit(solution)/shard_map/ppermute | solution.py:452
  83.3 4.1 %collective-permute-start.4 = (bf16[256,768]{1,0:T(8,128)(2,1)S(1)}, bf16[256,768]{1,0:T(8,128)(2,1)S(1)}, u32[]{:S(2)}, u32[]{:S(2)}) collective-permute-start(bf16[256,768]{1,0:T(8,128)(2,1)S(1)} %get-tuple-element.44), channel_id=1, source_target_pairs={{8,0},{0,8},{24,16},{16,24},{40,32},{32,40},{56,48},{48,56},{72,64... | collective-permute-start | bytes 1179656 | tf_op jit(solution)/shard_map/ppermute | solution.py:452
  91.7 6.7 %copy-start.6 = (bf16[768,768]{1,0:T(8,128)(2,1)S(1)}, bf16[768,768]{1,0:T(8,128)(2,1)}, u32[]{:S(2)}) copy-start(bf16[768,768]{1,0:T(8,128)(2,1)} %param.27) | copy-start | bytes 3538948
  97.4 2.7 %collective-permute-start.5 = (bf16[16,24,768]{2,1,0:T(8,128)(2,1)S(1)}, bf16[16,24,768]{2,1,0:T(8,128)(2,1)S(1)}, u32[]{:S(2)}, u32[]{:S(2)}) collective-permute-start(bf16[16,24,768]{2,1,0:T(8,128)(2,1)S(1)} %get-tuple-element.55), channel_id=1, source_target_pairs={{8,0},{0,8},{24,16},{16,24},{40,32},{32,40},{56,48},{48,56},{72,64... | collective-permute-start | bytes 1769480 | tf_op jit(solution)/shard_map/ppermute | solution.py:452

commit v7 on v6

--- a/solution.py
+++ b/solution.py
@@ -178,24 +178,38 @@
             third(two.pop(index - 2), *steps[index - 2])
 
 
-def attend(places, column, q, k, v, pbias, new, old):
+def attend(places, column, q, k, v, pbias, new, old, project=None):
+    def first(pair, own, start, barred):
+        scores = pair_scores(pair, own, start, barred, q, k)
+        if project is not None and own == places[0][0] and pair % 2 == 0 and pair + 2 < PAIRS:
+            project(pair // 2 + 1)
+        return scores
+
+    if project is not None:
+        project(0)
     staged(
         [(pair, *place) for place in places for pair in range(PAIRS)],
-        lambda *step: pair_scores(*step, q, k),
+        first,
         lambda scores, *step: pair_weights(scores, *step, column, pbias, new, old),
         lambda found, *step: absorb(*found, *step, v, new, old),
     )
 
 
 def keys_values(blocks, gain, wk, wv, k, v):
-    done = 0
-    for block in blocks:
-        for start in range(0, block.shape[0], PATCH):
-            span = slice(done, done + PATCH)
-            piece = normalize(block[start : start + PATCH], gain[...])
-            v[:, span] = nt(wv[...], piece).astype(BF)
-            k[span] = nn(piece, wk[...]).astype(BF)
-            done += PATCH
+    pieces = [
+        normalize(block[start : start + PATCH], gain[...])
+        for block in blocks
+        for start in range(0, block.shape[0], PATCH)
+    ]
+
+    def project(part):
+        features = slice(part * 256, (part + 1) * 256)
+        for index, piece in enumerate(pieces):
+            span = slice(index * PATCH, (index + 1) * PATCH)
+            v[features, span] = nt(wv[features], piece).astype(BF)
+            k[span, features] = nn(piece, wk[:, features]).astype(BF)
+
+    return project
 
 
 def own_kernel(pbias, x, wq_in, wk_in, wv_in, gain, q, acc, top, total, wk, wv, again, k, v, wq, normed, arrivals):
@@ -217,7 +231,7 @@
 
 
 def arrived_part(distance, devices, place, near, live, pbias, blocks, gain, wk, wv, q, acc_in, top_in, total_in, acc, top, total, k, v):
-    keys_values(blocks, gain, wk, wv, k, v)
+    project = keys_values(blocks, gain, wk, wv, k, v)
     outwards = 1 - 2 * lax.rem(place[0], 2)
     source = lax.rem(place[0] + distance * outwards + devices, devices)
     places = []
@@ -229,7 +243,7 @@
             found = jnp.where(hit, jnp.bitwise_and(listed, 1), found)
         barred = jnp.where(found >= 0, 0.0, -jnp.inf)
         places.append((own, pl.multiple_of(jnp.maximum(found, 0) * PATCH, PATCH), barred))
-    attend(places, 1, q, k, v, pbias, (acc, top, total), (acc_in, top_in, total_in))
+    attend(places, 1, q, k, v, pbias, (acc, top, total), (acc_in, top_in, total_in), project)
 
 
 def arrived_kernel(distance, devices, count, place, near, live, pbias, *refs):
@@ -240,10 +254,10 @@
 
 
 def last_kernel(
-    distance, devices, place, near, live, pbias, x, gain, wk, wv, q, acc_in, top_in, total_in, cot_in, mix_out, keep, give,
-    acc, top, total, k, v, mix, cot, sent
+    distance, devices, place, near, live, pbias, x, gain, wk, wv, q, acc_in, top_in, total_in, cot_in, mix, keep, give,
+    acc, top, total, k, v, cot, sent
 ):
-    fetch = pltpu.make_async_copy(cot_in, cot, sent.at[0])
+    fetch = pltpu.make_async_copy(cot_in, cot, sent)
     fetch.start()
     old, new = (acc_in, top_in, total_in), (acc, top, total)
     arrived_part(distance, devices, place, near, live, pbias, (x,), gain, wk, wv, q, *old, *new, k, v)
@@ -256,8 +270,6 @@
                 mix[head, mine] = (
                     acc[head, mine] * inverse[:, half * PATCH : (half + 1) * PATCH]
                 ).astype(BF)
-    store = pltpu.make_async_copy(mix, mix_out, sent.at[1])
-    store.start()
     fetch.wait()
     chips, rows, _ = keep.shape
     even = lax.rem(place[0], 2) == 0
@@ -269,7 +281,6 @@
             to_even, to_odd = grad[at : at + rows], grad[at + rows : at + 2 * rows]
             keep[first + chip] = jnp.where(even, to_even, to_odd)
             give[first + chip] = jnp.where(even, to_odd, to_even).astype(BF)
-    store.wait()
 
 
 IN_VMEM = pl.BlockSpec(memory_space=pltpu.VMEM)
@@ -416,11 +427,10 @@
         fixed,
         [block, gain, wk, wv, q, *state, cotangent],
         [wide, (piece, F32), (piece, BF)],
-        [*kept, tall, wide, wide, tall, pltpu.SemaphoreType.DMA((2,))],
+        [*kept, tall, wide, tall, pltpu.SemaphoreType.DMA],
         8 * work,
         "last",
         loose_in=(8,),
-        loose_out=(0,),
     )
 
 

time: 132 us -> 132 us (level)
  no operation moved by 1% of the time
where the time goes in v7:
time: 132 us; the launch traced here: 131 us
  blocking collectives  56.2 us (43%)
  Pallas kernels  33.9 us (26%)
  waiting for transfers between devices  19 us (14%)
  starting transfers between devices  18.1 us (14%)
  matrix products  1.69 us (1%)
    pallas_call x7, Pallas kernels, call(): pl.pallas_call(kernel, out_shape=shapes, in_specs=[IN_SMEM] * len(scalars...  30 us
    all_to_all x1, blocking collectives, body(): lax.all_to_all(hidden, 'level', 0, 0, tiled=True).reshape(columns, features)  25.9 us
    all_to_all x1, waiting for transfers between devices, body(): lax.all_to_all(fields.reshape(levels, share, features), 'level', 0, 0, ti...  19 us
    all_to_all x1, blocking collectives, body(): lax.all_to_all(summed, 'space', 0, 0, axis_index_groups=same_core, tiled=...  17.5 us
    all_to_all x1, blocking collectives, body(): lax.all_to_all(spread, 'level', 0, 0, tiled=True).astype(F32).sum(axis=0)  12.8 us
    all_to_all x1, starting transfers between devices, body(): lax.all_to_all(fields.reshape(levels, share, features), 'level', 0, 0, ti...  9.16 us
    ppermute x6, starting transfers between devices, moved(): lax.ppermute(value, 'space', [(source_of(d) % devices, d) for d in range(...  8.97 us
    pallas_call x1, Pallas kernels, turned(): pl.pallas_call(turning_kernel, out_shape=[jax.ShapeDtypeStruct(shape, BF)...  3.84 us
  transfers between devices with their start and end apart: 7, of which 1 were waited for; matrix products, arithmetic and copies ran while one was open for 2% of the time, Pallas kernels for 17%

profile of v7, /device:TPU:1, one launch (start us, length us, event | category | flops | bytes accessed | tf_op | source)
XLA Modules:
  0.0 131.4 jit_solution(16836865517548386980)
XLA Ops:
  0.6 9.2 %all-to-all-start = ((bf16[8,64,768]{2,1,0:T(8,128)(2,1)}), bf16[8,64,768]{2,1,0:T(8,128)(2,1)S(1)}, u32[]{:S(2)}, u32[]{:S(2)}) async-start(bf16[8,64,768]{2,1,0:T(8,128)(2,1)} %bitcast.14), calls=%async_computation | async-start | bytes 1572864 | tf_op jit(solution)/shard_map/all_to_all | solution.py:466
  9.8 0.1 copy.30
  10.1 0.2 broadcast_in_dim.26
  10.3 0.2 reshape.26.rows_of_bias
  10.5 3.8 %turned.1 = (bf16[768,768]{1,0:T(8,128)(2,1)}, bf16[768,768]{1,0:T(8,128)(2,1)}, bf16[768,768]{1,0:T(8,128)(2,1)}, bf16[768,768]{1,0:T(8,128)(2,1)}) custom-call(bf16[768,768]{1,0:T(8,128)(2,1)} %refs_0_.1, bf16[768,768]{1,0:T(8,128)(2,1)} %refs_1_.1, bf16[768,768]{1,0:T(8,128)(2,1)} %refs_2_.1, bf16[768,768]{1,0:T(8,128)(2,1)} %refs_3_.1), custom_call_target="tpu_custom_call" | custom-call | bytes 20971520 | tf_op jit(solution)/shard_map/turned/pallas_call | solution.py:298
  14.4 19.0 %all-to-all-done.x = bf16[8,64,768]{2,1,0:T(8,128)(2,1)S(1)} async-done(((bf16[8,64,768]{2,1,0:T(8,128)(2,1)}), bf16[8,64,768]{2,1,0:T(8,128)(2,1)S(1)}, u32[]{:S(2)}, u32[]{:S(2)}) %all-to-all-start) | async-done | bytes 786464 | tf_op jit(solution)/shard_map/all_to_all | solution.py:466
  33.4 5.8 %vertical.1 = bf16[8,64,768]{2,1,0:T(8,128)(2,1)S(1)} custom-call(s32[1]{0:T(128)} %bitcast._.place, bf16[8,64,768]{2,1,0:T(8,128)(2,1)S(1)} %all-to-all-done.x, bf16[768,768]{1,0:T(8,128)(2,1)} %get-tuple-element.31.wq_in, bf16[768,768]{1,0:T(8,128)(2,1)} %wk_in.2, bf16[768,768]{1,0:T(8,128)(2,1)} %get-tuple-element.32.wv_in, bf16[768,768]{1,0:T(8,128)(2,1)} %wo_in.1, ...), custom_call_target="tpu_custom_call" | custom-call | flops 3019898880 | bytes 11796480 | tf_op jit(solution)/shard_map/vertical/pallas_call | solution.py:318
  39.2 25.9 %all_to_all.20 = bf16[8,64,768]{2,1,0:T(8,128)(2,1)S(1)} all-to-all(bf16[8,64,768]{2,1,0:T(8,128)(2,1)S(1)} %vertical.1), channel_id=1, replica_groups=mesh['space'=32,'level'=8] {'level'}, dimensions={0} | all-to-all | bytes 1572864 | tf_op jit(solution)/shard_map/all_to_all | solution.py:468
  65.1 0.6 collective-permute-start.2
  65.7 1.3 collective-permute-start.1
  67.1 6.0 %own.1 = (bf16[768,512]{1,0:T(8,128)(2,1)S(1)}, f32[768,512]{1,0:T(8,128)S(1)}, f32[12,512]{1,0:T(8,128)S(1)}, f32[12,512]{1,0:T(8,128)S(1)}, bf16[768,768]{1,0:...) custom-call(f32[12,2]{1,0:T(8,128)S(1)} %copy.36.pbias, bf16[512,768]{1,0:T(8,128)(2,1)S(1)} %bitcast.12, ...), custom_call_target="tpu_custom_call" | custom-call | flops 2415919104 | bytes 9437184 | tf_op jit(solution)/shard_map/own/pallas_call | solution.py:318
  73.1 3.9 %collective-permute-start = (bf16[512,768]{1,0:T(8,128)(2,1)S(1)}, bf16[512,768]{1,0:T(8,128)(2,1)S(1)}, u32[]{:S(2)}, u32[]{:S(2)}) collective-permute-start(bf16[512,768]{1,0:T(8,128)(2,1)S(1)} %get-tuple-element.35), channel_id=1, source_target_pairs={{240,0},{24,8},{0,16},{40,24},{16,32},{56,40},{32,48},{72,56},{48,... | collective-permute-start | bytes 2359304 | tf_op jit(solution)/shard_map/ppermute | solution.py:462
  77.0 4.0 %arrived.3 = (f32[768,512]{1,0:T(8,128)S(1)}, f32[12,512]{1,0:T(8,128)S(1)}, f32[12,512]{1,0:T(8,128)S(1)}, f32[8,128]{1,0:T(8,128)S(1)}) custom-call(s32[1]{0:T(128)} %bitcast._.place, s32[2,4]{1,0:T(2,128)S(1)} %copy-done, s32[2]{0:T(128)S(1)} %copy-done.1, f32[12,2]{1,0:T(8,128)S(1)} %copy.36.pbias, bf16[512,768]{1,0:T(8,128)(2,1)S(1)} %collective-permute-done.2.refs_0_, ...), custom_call_target="tpu_custom_call" | custom-call | flops 75497472 | bytes 294912 | tf_op jit(solution)/shard_map/arrived/pallas_call | solution.py:318
  81.0 0.4 halved.1
  81.4 1.9 %collective-permute-start.3 = (bf16[256,768]{1,0:T(8,128)(2,1)S(1)}, bf16[256,768]{1,0:T(8,128)(2,1)S(1)}, u32[]{:S(2)}, u32[]{:S(2)}) collective-permute-start(bf16[256,768]{1,0:T(8,128)(2,1)S(1)} %get-tuple-element.43), channel_id=1, source_target_pairs={{8,0},{0,8},{24,16},{16,24},{40,32},{32,40},{56,48},{48,56},{72,64... | collective-permute-start | bytes 1179656 | tf_op jit(solution)/shard_map/ppermute | solution.py:462
  83.4 3.9 %arrived.4 = (f32[768,512]{1,0:T(8,128)S(1)}, f32[12,512]{1,0:T(8,128)S(1)}, f32[12,512]{1,0:T(8,128)S(1)}, f32[8,128]{1,0:T(8,128)S(1)}) custom-call(s32[1]{0:T(128)} %bitcast._.place, s32[2,4]{1,0:T(2,128)S(1)} %copy-done, s32[2]{0:T(128)S(1)} %copy-done.1, f32[12,2]{1,0:T(8,128)S(1)} %copy.36.pbias, ...), custom_call_target="tpu_custom_call" | custom-call | flops 75497472 | bytes 294912 | tf_op jit(solution)/shard_map/arrived/pallas_call | solution.py:318
  87.3 4.1 %arrived.5 = (f32[768,512]{1,0:T(8,128)S(1)}, f32[12,512]{1,0:T(8,128)S(1)}, f32[12,512]{1,0:T(8,128)S(1)}, f32[8,128]{1,0:T(8,128)}) custom-call(s32[1]{0:T(128)} %bitcast._.place, s32[2,4]{1,0:T(2,128)S(1)} %copy-done, s32[2]{0:T(128)S(1)} %copy-done.1, f32[12,2]{1,0:T(8,128)S(1)} %copy.36.pbias, bf16[256,768]{1,0:T(8,128)(2,1)S(1)} %collective-permute-done.3.refs_0_, ...), custom_call_target="tpu_custom_call" | custom-call | flops 75497472 | bytes 294912 | tf_op jit(solution)/shard_map/arrived/pallas_call | solution.py:318
  91.5 5.8 %last.1 = (bf16[768,512]{1,0:T(8,128)(2,1)S(1)}, f32[16,24,768]{2,1,0:T(8,128)S(1)}, bf16[16,24,768]{2,1,0:T(8,128)(2,1)S(1)}) custom-call(s32[1]{0:T(128)} %bitcast._.place, s32[2,4]{1,0:T(2,128)S(1)} %copy-done, s32[2]{0:T(128)S(1)} %copy-done.1, f32[12,2]{1,0:T(8,128)S(1)} %copy.36.pbias, bf16[512,768]{1,0:T(8,128)(2,1)S(1)} %collective-permute-done.x, ...), custom_call_target="tpu_custom_call" | custom-call | flops 2415919104 | bytes 9437184 | tf_op jit(solution)/shard_map/last/pallas_call | solution.py:318
  97.3 1.2 collective-permute-start.5
  98.5 1.7 %add_convert_fusion = bf16[512,768]{1,0:T(8,128)(2,1)} fusion(bf16[512,768]{1,0:T(8,128)(2,1)S(1)} %bitcast.13, bf16[768,512]{1,0:T(8,128)(2,1)S(1)} %get-tuple-element.56, bf16[768,768]{1,0:T(8,128)(2,1)S(1)} %copy-done.6), kind=kOutput, calls=%fused_computation | convolution fusion | flops 605159424 | bytes 3538944 | tf_op jit(solution)/shard_map/dot_general | solution.py:493
  100.2 0.1 add_convert_fusion.1
  100.3 17.5 %all_to_all.21 = bf16[16,24,768]{2,1,0:T(8,128)(2,1)S(1)} all-to-all(bf16[16,24,768]{2,1,0:T(8,128)(2,1)S(1)} %add_convert_fusion.1), channel_id=1, replica_groups={{0,16,32,48,64,80,96,112,128,144,160,176,192,208,224,240},{8,24,40,56,7..., dimensions={0} | all-to-all | bytes 1179648 | tf_op jit(solution)/shard_map/all_to_all | solution.py:498
  117.9 12.8 %all_to_all.22 = bf16[8,24,768]{2,1,0:T(8,128)(2,1)S(1)} all-to-all(bf16[8,24,768]{2,1,0:T(8,128)(2,1)S(1)} %broadcast_in_dim.30), channel_id=1, replica_groups=mesh['space'=32,'level'=8] {'level'}, dimensions={0} | all-to-all | bytes 589824 | tf_op jit(solution)/shard_map/all_to_all | solution.py:501
  130.7 0.7 convert_reduce_fusion
  (30 shorter events, 0.5 us)
Async XLA Ops:
  0.6 9.2 %copy-start.2 = (f32[12,8,8]{0,2,1:T(8,128)S(1)}, f32[12,8,8]{0,2,1:T(8,128)}, u32[]{:S(2)}) copy-start(f32[12,8,8]{0,2,1:T(8,128)} %param.22) | copy-start | bytes 9220
  0.6 9.9 %copy-start.3 = (f32[768]{0:T(1024)S(1)}, f32[768]{0:T(1024)}, u32[]{:S(2)}) copy-start(f32[768]{0:T(1024)} %param.17) | copy-start | bytes 9220
  0.6 32.7 %all-to-all-start = ((bf16[8,64,768]{2,1,0:T(8,128)(2,1)}), bf16[8,64,768]{2,1,0:T(8,128)(2,1)S(1)}, u32[]{:S(2)}, u32[]{:S(2)}) async-start(bf16[8,64,768]{2,1,0:T(8,128)(2,1)} %bitcast.14), calls=%async_computation | async-start | bytes 1572864 | tf_op jit(solution)/shard_map/all_to_all | solution.py:466
  39.2 27.8 %copy-start.5 = (f32[12,2]{0,1:T(2,128)S(1)}, f32[12,2]{0,1:T(2,128)}, u32[]{:S(2)}) copy-start(f32[12,2]{0,1:T(2,128)} %param.28) | copy-start | bytes 292
  39.2 27.9 %copy-start.4 = (f32[768]{0:T(1024)S(1)}, f32[768]{0:T(1024)}, u32[]{:S(2)}) copy-start(f32[768]{0:T(1024)} %param.23) | copy-start | bytes 9220
  65.1 11.9 %collective-permute-start.2 = (bf16[512,768]{1,0:T(8,128)(2,1)S(1)}, bf16[512,768]{1,0:T(8,128)(2,1)S(1)}, u32[]{:S(2)}, u32[]{:S(2)}) collective-permute-start(bf16[512,768]{1,0:T(8,128)(2,1)S(1)} %bitcast.10), channel_id=1, source_target_pairs={{8,0},{0,8},{24,16},{16,24},{40,32},{32,40},{56,48},{48,56},{72,64... | collective-permute-start | bytes 2359304 | tf_op jit(solution)/shard_map/ppermute | solution.py:462
  65.7 15.3 %collective-permute-start.1 = (bf16[512,768]{1,0:T(8,128)(2,1)S(1)}, bf16[512,768]{1,0:T(8,128)(2,1)S(1)}, u32[]{:S(2)}, u32[]{:S(2)}) collective-permute-start(bf16[512,768]{1,0:T(8,128)(2,1)S(1)} %bitcast.11), channel_id=1, source_target_pairs={{16,0},{248,8},{32,16},{8,24},{48,32},{24,40},{64,48},{40,56},{80,... | collective-permute-start | bytes 2359304 | tf_op jit(solution)/shard_map/ppermute | solution.py:462
  67.1 9.9 %copy-start = (s32[2,4]{1,0:T(2,128)S(1)}, s32[2,4]{1,0:T(2,128)}, u32[]{:S(2)}) copy-start(s32[2,4]{1,0:T(2,128)} %near.7) | copy-start | bytes 100
  67.1 9.9 %copy-start.1 = (s32[2]{0:T(128)S(1)}, s32[2]{0:T(128)}, u32[]{:S(2)}) copy-start(s32[2]{0:T(128)} %live.7) | copy-start | bytes 28
  73.1 18.4 %collective-permute-start = (bf16[512,768]{1,0:T(8,128)(2,1)S(1)}, bf16[512,768]{1,0:T(8,128)(2,1)S(1)}, u32[]{:S(2)}, u32[]{:S(2)}) collective-permute-start(bf16[512,768]{1,0:T(8,128)(2,1)S(1)} %get-tuple-element.35), channel_id=1, source_target_pairs={{240,0},{24,8},{0,16},{40,24},{16,32},{56,40},{32,48},{72,56},{48,... | collective-permute-start | bytes 2359304 | tf_op jit(solution)/shard_map/ppermute | solution.py:462
  81.4 5.9 %collective-permute-start.3 = (bf16[256,768]{1,0:T(8,128)(2,1)S(1)}, bf16[256,768]{1,0:T(8,128)(2,1)S(1)}, u32[]{:S(2)}, u32[]{:S(2)}) collective-permute-start(bf16[256,768]{1,0:T(8,128)(2,1)S(1)} %get-tuple-element.43), channel_id=1, source_target_pairs={{8,0},{0,8},{24,16},{16,24},{40,32},{32,40},{56,48},{48,56},{72,64... | collective-permute-start | bytes 1179656 | tf_op jit(solution)/shard_map/ppermute | solution.py:462
  83.3 4.1 %collective-permute-start.4 = (bf16[256,768]{1,0:T(8,128)(2,1)S(1)}, bf16[256,768]{1,0:T(8,128)(2,1)S(1)}, u32[]{:S(2)}, u32[]{:S(2)}) collective-permute-start(bf16[256,768]{1,0:T(8,128)(2,1)S(1)} %get-tuple-element.44), channel_id=1, source_target_pairs={{8,0},{0,8},{24,16},{16,24},{40,32},{32,40},{56,48},{48,56},{72,64... | collective-permute-start | bytes 1179656 | tf_op jit(solution)/shard_map/ppermute | solution.py:462
  91.5 7.0 %copy-start.6 = (bf16[768,768]{1,0:T(8,128)(2,1)S(1)}, bf16[768,768]{1,0:T(8,128)(2,1)}, u32[]{:S(2)}) copy-start(bf16[768,768]{1,0:T(8,128)(2,1)} %param.27) | copy-start | bytes 3538948
  97.3 2.9 %collective-permute-start.5 = (bf16[16,24,768]{2,1,0:T(8,128)(2,1)S(1)}, bf16[16,24,768]{2,1,0:T(8,128)(2,1)S(1)}, u32[]{:S(2)}, u32[]{:S(2)}) collective-permute-start(bf16[16,24,768]{2,1,0:T(8,128)(2,1)S(1)} %get-tuple-element.55), channel_id=1, source_target_pairs={{8,0},{0,8},{24,16},{16,24},{40,32},{32,40},{56,48},{48,56},{72,64... | collective-permute-start | bytes 1769480 | tf_op jit(solution)/shard_map/ppermute | solution.py:462

commit v8 on v6

--- a/solution.py
+++ b/solution.py
@@ -74,7 +74,7 @@
 
 
 def vertical_kernel(
-    _, x, wq_in, wk_in, wv_in, wo_in, gain, rows_of_bias, out, normed, q, k, v, mix, bias, wq, wk, wv, wo, arrivals
+    _, _bias, x, wq_in, wk_in, wv_in, wo_in, gain, rows_of_bias, _gain, out, normed, q, k, v, mix, bias, wq, wk, wv, wo, arrivals
 ):
     levels, columns, features = x.shape
     copies = fetched([(wq_in, wq), (wk_in, wk), (wv_in, wv), (wo_in, wo)], arrivals)
@@ -353,13 +353,13 @@
     return weights, turned_tokens, ((columns, features), BF), state, columns * features * features
 
 
-def run_vertical(place, x, wq, wk, wv, wo, gain, rows_of_bias):
+def run_vertical(early, x, wq, wk, wv, wo, gain, rows_of_bias, later_gain):
     levels, share, features = x.shape
     weights, wide, tall, _, work = sizes(levels * share, features)
     return call(
         vertical_kernel,
-        [place],
-        [x, wq, wk, wv, wo, gain, rows_of_bias],
+        early,
+        [x, wq, wk, wv, wo, gain, rows_of_bias, later_gain],
         [(x.shape, BF)],
         [
             tall,
@@ -454,7 +454,10 @@
     wq_v, wv_v, wq_p, wv_p = kept_in_hbm(*turned(query_vert, values_vert, query_patch, values_patch))
     keys_vert, out_vert, keys_patch = kept_in_hbm(keys_vert, out_vert, keys_patch)
     x = lax.all_to_all(fields.reshape(levels, share, features), "level", 0, 0, tiled=True)
-    hidden = run_vertical(place, x, wq_v, keys_vert, wv_v, out_vert, norm_vert[None], expanded_bias(level_bias))
+    gain = norm_patch[None]
+    hidden = run_vertical(
+        [place, patch_bias], x, wq_v, keys_vert, wv_v, out_vert, norm_vert[None], expanded_bias(level_bias), gain
+    )
     hidden = lax.all_to_all(hidden, "level", 0, 0, tiled=True).reshape(columns, features)
 
     def outer(d):
@@ -468,7 +471,6 @@
 
     from_outer = moved(hidden, outer)
     from_twin = moved(hidden, twin)
-    gain = norm_patch[None]
     q, *state, wk, wv, again = run_own(patch_bias, hidden, wq_p, keys_patch, wv_p, gain)
     from_inner = moved(again, inner)
     fixed = [place, neighbours, counts, patch_bias]

time: 132 us -> 133 us (level)
  no operation moved by 1% of the time
where the time goes in v8:
time: 133 us; the launch traced here: 132 us
  blocking collectives  56.6 us (43%)
  Pallas kernels  34.7 us (26%)
  waiting for transfers between devices  18.9 us (14%)
  starting transfers between devices  18 us (14%)
  matrix products  1.7 us (1%)
    pallas_call x7, Pallas kernels, call(): pl.pallas_call(kernel, out_shape=shapes, in_specs=[IN_SMEM] * len(scalars...  30.9 us
    all_to_all x1, blocking collectives, body(): lax.all_to_all(hidden, 'level', 0, 0, tiled=True).reshape(columns, features)  25.8 us
    all_to_all x1, waiting for transfers between devices, body(): lax.all_to_all(fields.reshape(levels, share, features), 'level', 0, 0, ti...  18.9 us
    all_to_all x1, blocking collectives, body(): lax.all_to_all(summed, 'space', 0, 0, axis_index_groups=same_core, tiled=...  18 us
    all_to_all x1, blocking collectives, body(): lax.all_to_all(spread, 'level', 0, 0, tiled=True).astype(F32).sum(axis=0)  12.8 us
    all_to_all x1, starting transfers between devices, body(): lax.all_to_all(fields.reshape(levels, share, features), 'level', 0, 0, ti...  9.16 us
    ppermute x6, starting transfers between devices, moved(): lax.ppermute(value, 'space', [(source_of(d) % devices, d) for d in range(...  8.81 us
    pallas_call x1, Pallas kernels, turned(): pl.pallas_call(turning_kernel, out_shape=[jax.ShapeDtypeStruct(shape, BF)...  3.84 us
  transfers between devices with their start and end apart: 7, of which 1 were waited for; matrix products, arithmetic and copies ran while one was open for 2% of the time, Pallas kernels for 17%

profile of v8, /device:TPU:1, one launch (start us, length us, event | category | flops | bytes accessed | tf_op | source)
XLA Modules:
  0.0 132.4 jit_solution(14405446631167660574)
XLA Ops:
  0.7 9.2 %all-to-all-start = ((bf16[8,64,768]{2,1,0:T(8,128)(2,1)}), bf16[8,64,768]{2,1,0:T(8,128)(2,1)S(1)}, u32[]{:S(2)}, u32[]{:S(2)}) async-start(bf16[8,64,768]{2,1,0:T(8,128)(2,1)} %bitcast.14), calls=%async_computation | async-start | bytes 1572864 | tf_op jit(solution)/shard_map/all_to_all | solution.py:456
  9.9 0.1 copy.32
  10.3 0.2 broadcast_in_dim.26
  10.4 0.2 reshape.26.rows_of_bias
  10.7 3.8 %turned.1 = (bf16[768,768]{1,0:T(8,128)(2,1)}, bf16[768,768]{1,0:T(8,128)(2,1)}, bf16[768,768]{1,0:T(8,128)(2,1)}, bf16[768,768]{1,0:T(8,128)(2,1)}) custom-call(bf16[768,768]{1,0:T(8,128)(2,1)} %refs_0_.1, bf16[768,768]{1,0:T(8,128)(2,1)} %refs_1_.1, bf16[768,768]{1,0:T(8,128)(2,1)} %refs_2_.1, bf16[768,768]{1,0:T(8,128)(2,1)} %refs_3_.1), custom_call_target="tpu_custom_call" | custom-call | bytes 20971520 | tf_op jit(solution)/shard_map/turned/pallas_call | solution.py:287
  14.5 18.9 %all-to-all-done.x = bf16[8,64,768]{2,1,0:T(8,128)(2,1)S(1)} async-done(((bf16[8,64,768]{2,1,0:T(8,128)(2,1)}), bf16[8,64,768]{2,1,0:T(8,128)(2,1)S(1)}, u32[]{:S(2)}, u32[]{:S(2)}) %all-to-all-start) | async-done | bytes 786464 | tf_op jit(solution)/shard_map/all_to_all | solution.py:456
  33.4 6.4 %vertical.1 = bf16[8,64,768]{2,1,0:T(8,128)(2,1)S(1)} custom-call(s32[1]{0:T(128)} %bitcast._.place, f32[12,2]{1,0:T(8,128)S(1)} %copy.39._bias.pbias, bf16[8,64,768]{2,1,0:T(8,128)(2,1)S(1)} %all-to-all-done.x, bf16[768,768]{1,0:T(8,128)(2,1)} %get-tuple-element.31.wq_in, bf16[768,768]{1,0:T(8,128)(2,1)} %wk_in.2, ...), custom_call_target="tpu_custom_call" | custom-call | flops 3019898880 | bytes 11796480 | tf_op jit(solution)/shard_map/vertical/pallas_call | solution.py:307
  39.9 25.8 %all_to_all.20 = bf16[8,64,768]{2,1,0:T(8,128)(2,1)S(1)} all-to-all(bf16[8,64,768]{2,1,0:T(8,128)(2,1)S(1)} %vertical.1), channel_id=1, replica_groups=mesh['space'=32,'level'=8] {'level'}, dimensions={0} | all-to-all | bytes 1572864 | tf_op jit(solution)/shard_map/all_to_all | solution.py:461
  65.6 0.7 collective-permute-start.2
  66.3 1.3 collective-permute-start.1
  67.6 6.0 %own.1 = (bf16[768,512]{1,0:T(8,128)(2,1)S(1)}, f32[768,512]{1,0:T(8,128)S(1)}, f32[12,512]{1,0:T(8,128)S(1)}, f32[12,512]{1,0:T(8,128)S(1)}, bf16[768,768]{1,0:...) custom-call(f32[12,2]{1,0:T(8,128)S(1)} %copy.39._bias.pbias, ...), custom_call_target="tpu_custom_call" | custom-call | flops 2415919104 | bytes 9437184 | tf_op jit(solution)/shard_map/own/pallas_call | solution.py:307
  73.6 3.9 %collective-permute-start = (bf16[512,768]{1,0:T(8,128)(2,1)S(1)}, bf16[512,768]{1,0:T(8,128)(2,1)S(1)}, u32[]{:S(2)}, u32[]{:S(2)}) collective-permute-start(bf16[512,768]{1,0:T(8,128)(2,1)S(1)} %get-tuple-element.35), channel_id=1, source_target_pairs={{240,0},{24,8},{0,16},{40,24},{16,32},{56,40},{32,48},{72,56},{48,... | collective-permute-start | bytes 2359304 | tf_op jit(solution)/shard_map/ppermute | solution.py:452
  77.6 4.0 %arrived.3 = (f32[768,512]{1,0:T(8,128)S(1)}, f32[12,512]{1,0:T(8,128)S(1)}, f32[12,512]{1,0:T(8,128)S(1)}, f32[8,128]{1,0:T(8,128)S(1)}) custom-call(s32[1]{0:T(128)} %bitcast._.place, s32[2,4]{1,0:T(2,128)S(1)} %copy-done, s32[2]{0:T(128)S(1)} %copy-done.1, f32[12,2]{1,0:T(8,128)S(1)} %copy.39._bias.pbias, ...), custom_call_target="tpu_custom_call" | custom-call | flops 75497472 | bytes 294912 | tf_op jit(solution)/shard_map/arrived/pallas_call | solution.py:307
  81.5 0.4 halved.1
  82.0 2.1 %collective-permute-start.3 = (bf16[256,768]{1,0:T(8,128)(2,1)S(1)}, bf16[256,768]{1,0:T(8,128)(2,1)S(1)}, u32[]{:S(2)}, u32[]{:S(2)}) collective-permute-start(bf16[256,768]{1,0:T(8,128)(2,1)S(1)} %get-tuple-element.43), channel_id=1, source_target_pairs={{8,0},{0,8},{24,16},{16,24},{40,32},{32,40},{56,48},{48,56},{72,64... | collective-permute-start | bytes 1179656 | tf_op jit(solution)/shard_map/ppermute | solution.py:452
  84.2 4.0 %arrived.4 = (f32[768,512]{1,0:T(8,128)S(1)}, f32[12,512]{1,0:T(8,128)S(1)}, f32[12,512]{1,0:T(8,128)S(1)}, f32[8,128]{1,0:T(8,128)S(1)}) custom-call(s32[1]{0:T(128)} %bitcast._.place, s32[2,4]{1,0:T(2,128)S(1)} %copy-done, s32[2]{0:T(128)S(1)} %copy-done.1, f32[12,2]{1,0:T(8,128)S(1)} %copy.39._bias.pbias, ...), custom_call_target="tpu_custom_call" | custom-call | flops 75497472 | bytes 294912 | tf_op jit(solution)/shard_map/arrived/pallas_call | solution.py:307
  88.2 4.4 %arrived.5 = (f32[768,512]{1,0:T(8,128)S(1)}, f32[12,512]{1,0:T(8,128)S(1)}, f32[12,512]{1,0:T(8,128)S(1)}, f32[8,128]{1,0:T(8,128)}) custom-call(s32[1]{0:T(128)} %bitcast._.place, s32[2,4]{1,0:T(2,128)S(1)} %copy-done, s32[2]{0:T(128)S(1)} %copy-done.1, f32[12,2]{1,0:T(8,128)S(1)} %copy.39._bias.pbias, ...), custom_call_target="tpu_custom_call" | custom-call | flops 75497472 | bytes 294912 | tf_op jit(solution)/shard_map/arrived/pallas_call | solution.py:307
  92.5 5.7 %last.1 = (bf16[768,512]{1,0:T(8,128)(2,1)S(1)}, f32[16,24,768]{2,1,0:T(8,128)S(1)}, bf16[16,24,768]{2,1,0:T(8,128)(2,1)S(1)}) custom-call(s32[1]{0:T(128)} %bitcast._.place, s32[2,4]{1,0:T(2,128)S(1)} %copy-done, s32[2]{0:T(128)S(1)} %copy-done.1, f32[12,2]{1,0:T(8,128)S(1)} %copy.39._bias.pbias, bf16[512,768]{1,0:T(8,128)(2,1)S(1)} %collective-permute-done.x, ...), custom_call_target="tpu_custom_call" | custom-call | flops 2415919104 | bytes 9437184 | tf_op jit(solution)/shard_map/last/pallas_call | solution.py:307
  98.2 0.7 collective-permute-start.5
  98.9 1.7 %add_convert_fusion = bf16[512,768]{1,0:T(8,128)(2,1)} fusion(bf16[512,768]{1,0:T(8,128)(2,1)S(1)} %bitcast.13, bf16[768,512]{1,0:T(8,128)(2,1)S(1)} %get-tuple-element.56, bf16[768,768]{1,0:T(8,128)(2,1)S(1)} %copy-done.6), kind=kOutput, calls=%fused_computation | convolution fusion | flops 605159424 | bytes 3538944 | tf_op jit(solution)/shard_map/dot_general | solution.py:485
  100.6 0.1 add_convert_fusion.1
  100.7 18.0 %all_to_all.21 = bf16[16,24,768]{2,1,0:T(8,128)(2,1)S(1)} all-to-all(bf16[16,24,768]{2,1,0:T(8,128)(2,1)S(1)} %add_convert_fusion.1), channel_id=1, replica_groups={{0,16,32,48,64,80,96,112,128,144,160,176,192,208,224,240},{8,24,40,56,7..., dimensions={0} | all-to-all | bytes 1179648 | tf_op jit(solution)/shard_map/all_to_all | solution.py:490
  118.9 12.8 %all_to_all.22 = bf16[8,24,768]{2,1,0:T(8,128)(2,1)S(1)} all-to-all(bf16[8,24,768]{2,1,0:T(8,128)(2,1)S(1)} %broadcast_in_dim.30), channel_id=1, replica_groups=mesh['space'=32,'level'=8] {'level'}, dimensions={0} | all-to-all | bytes 589824 | tf_op jit(solution)/shard_map/all_to_all | solution.py:493
  131.7 0.7 convert_reduce_fusion
  (30 shorter events, 0.5 us)
Async XLA Ops:
  0.6 9.2 %copy-start.5 = (f32[12,2]{0,1:T(2,128)S(1)}, f32[12,2]{0,1:T(2,128)}, u32[]{:S(2)}) copy-start(f32[12,2]{0,1:T(2,128)} %param.28) | copy-start | bytes 292
  0.6 9.3 %copy-start.3 = (f32[768]{0:T(1024)S(1)}, f32[768]{0:T(1024)}, u32[]{:S(2)}) copy-start(f32[768]{0:T(1024)} %param.23) | copy-start | bytes 9220
  0.7 9.3 %copy-start.2 = (f32[12,8,8]{0,2,1:T(8,128)S(1)}, f32[12,8,8]{0,2,1:T(8,128)}, u32[]{:S(2)}) copy-start(f32[12,8,8]{0,2,1:T(8,128)} %param.22) | copy-start | bytes 9220
  0.7 10.0 %copy-start.4 = (f32[768]{0:T(1024)S(1)}, f32[768]{0:T(1024)}, u32[]{:S(2)}) copy-start(f32[768]{0:T(1024)} %param.17) | copy-start | bytes 9220
  0.7 32.7 %all-to-all-start = ((bf16[8,64,768]{2,1,0:T(8,128)(2,1)}), bf16[8,64,768]{2,1,0:T(8,128)(2,1)S(1)}, u32[]{:S(2)}, u32[]{:S(2)}) async-start(bf16[8,64,768]{2,1,0:T(8,128)(2,1)} %bitcast.14), calls=%async_computation | async-start | bytes 1572864 | tf_op jit(solution)/shard_map/all_to_all | solution.py:456
  65.6 11.9 %collective-permute-start.2 = (bf16[512,768]{1,0:T(8,128)(2,1)S(1)}, bf16[512,768]{1,0:T(8,128)(2,1)S(1)}, u32[]{:S(2)}, u32[]{:S(2)}) collective-permute-start(bf16[512,768]{1,0:T(8,128)(2,1)S(1)} %bitcast.10), channel_id=1, source_target_pairs={{8,0},{0,8},{24,16},{16,24},{40,32},{32,40},{56,48},{48,56},{72,64... | collective-permute-start | bytes 2359304 | tf_op jit(solution)/shard_map/ppermute | solution.py:452
  66.3 15.2 %collective-permute-start.1 = (bf16[512,768]{1,0:T(8,128)(2,1)S(1)}, bf16[512,768]{1,0:T(8,128)(2,1)S(1)}, u32[]{:S(2)}, u32[]{:S(2)}) collective-permute-start(bf16[512,768]{1,0:T(8,128)(2,1)S(1)} %bitcast.11), channel_id=1, source_target_pairs={{16,0},{248,8},{32,16},{8,24},{48,32},{24,40},{64,48},{40,56},{80,... | collective-permute-start | bytes 2359304 | tf_op jit(solution)/shard_map/ppermute | solution.py:452
  67.6 9.9 %copy-start = (s32[2,4]{1,0:T(2,128)S(1)}, s32[2,4]{1,0:T(2,128)}, u32[]{:S(2)}) copy-start(s32[2,4]{1,0:T(2,128)} %near.7) | copy-start | bytes 100
  67.6 9.9 %copy-start.1 = (s32[2]{0:T(128)S(1)}, s32[2]{0:T(128)}, u32[]{:S(2)}) copy-start(s32[2]{0:T(128)} %live.7) | copy-start | bytes 28
  73.6 18.9 %collective-permute-start = (bf16[512,768]{1,0:T(8,128)(2,1)S(1)}, bf16[512,768]{1,0:T(8,128)(2,1)S(1)}, u32[]{:S(2)}, u32[]{:S(2)}) collective-permute-start(bf16[512,768]{1,0:T(8,128)(2,1)S(1)} %get-tuple-element.35), channel_id=1, source_target_pairs={{240,0},{24,8},{0,16},{40,24},{16,32},{56,40},{32,48},{72,56},{48,... | collective-permute-start | bytes 2359304 | tf_op jit(solution)/shard_map/ppermute | solution.py:452
  82.0 6.2 %collective-permute-start.3 = (bf16[256,768]{1,0:T(8,128)(2,1)S(1)}, bf16[256,768]{1,0:T(8,128)(2,1)S(1)}, u32[]{:S(2)}, u32[]{:S(2)}) collective-permute-start(bf16[256,768]{1,0:T(8,128)(2,1)S(1)} %get-tuple-element.43), channel_id=1, source_target_pairs={{8,0},{0,8},{24,16},{16,24},{40,32},{32,40},{56,48},{48,56},{72,64... | collective-permute-start | bytes 1179656 | tf_op jit(solution)/shard_map/ppermute | solution.py:452
  84.1 4.1 %collective-permute-start.4 = (bf16[256,768]{1,0:T(8,128)(2,1)S(1)}, bf16[256,768]{1,0:T(8,128)(2,1)S(1)}, u32[]{:S(2)}, u32[]{:S(2)}) collective-permute-start(bf16[256,768]{1,0:T(8,128)(2,1)S(1)} %get-tuple-element.44), channel_id=1, source_target_pairs={{8,0},{0,8},{24,16},{16,24},{40,32},{32,40},{56,48},{48,56},{72,64... | collective-permute-start | bytes 1179656 | tf_op jit(solution)/shard_map/ppermute | solution.py:452
  92.5 6.4 %copy-start.6 = (bf16[768,768]{1,0:T(8,128)(2,1)S(1)}, bf16[768,768]{1,0:T(8,128)(2,1)}, u32[]{:S(2)}) copy-start(bf16[768,768]{1,0:T(8,128)(2,1)} %param.27) | copy-start | bytes 3538948
  98.2 2.4 %collective-permute-start.5 = (bf16[16,24,768]{2,1,0:T(8,128)(2,1)S(1)}, bf16[16,24,768]{2,1,0:T(8,128)(2,1)S(1)}, u32[]{:S(2)}, u32[]{:S(2)}) collective-permute-start(bf16[16,24,768]{2,1,0:T(8,128)(2,1)S(1)} %get-tuple-element.55), channel_id=1, source_target_pairs={{8,0},{0,8},{24,16},{16,24},{40,32},{32,40},{56,48},{48,56},{72,64... | collective-permute-start | bytes 1769480 | tf_op jit(solution)/shard_map/ppermute | solution.py:452
